TPU v7x, 32 devices: a whole 2x2x4 slice. The times are simulated.
32 devices in a mesh: groups: 2 (over y), hosts: 8 (over z, x), tensor: 2 (over core).
Axes of the slice: x: 2, y: 2, z: 4, core: 2. Of those that a mesh axis runs over, the one named last changes fastest.
Arguments:
- context_queries: bfloat16 [2048, 8192], P(('groups', 'hosts'), 'tensor'), parts along dimension 0, may hold values from -6 to 6
- context_keys: bfloat16 [2048, 1024], P(('groups', 'hosts'), 'tensor'), parts along dimension 0, may hold values from -6 to 6
- context_values: bfloat16 [2048, 1024], P(('groups', 'hosts'), 'tensor'), parts along dimension 0, may hold values from -6 to 6
- doc_ids: int32 [2048], P(('groups', 'hosts')), parts along dimension 0, may hold values from 0 to 31, never falling along the last dimension, each value on 1 to 128 neighbouring positions
- query_token_rows: bfloat16 [16, 8192], P(('groups', 'hosts'), 'tensor'), parts along dimension 0, may hold values from -6 to 6
- span_start: int32 [16], P(('groups', 'hosts')), parts along dimension 0, may hold values from 0 to 511
Outputs:
- block_out: bfloat16 [2048, 8192], P(('groups', 'hosts'), 'tensor'), parts along dimension 0
- answer: bfloat16 [16, 8192], P(('groups', 'hosts'), 'tensor'), parts along dimension 0
There are 2 independent parts, one for each index of `groups`. A program takes and returns all parts, laid end to end along the dimension named above; each array names one. Nothing has to cross between parts.
All inputs are finite; a program needn't handle non-finite values.
Results may differ from a plain program's by a relative error of at most 0.0043.
Values may be sent and summed in bfloat16 or wider, within the bound.
No kernel may reach another device: no remote copies, remote signals or barrier semaphores. Data moves between devices by JAX's collectives and lax.ppermute only.
A program may use at most 64 MiB of HBM per device.

v0:
```python
import jax
import jax.numpy as jnp
from jax import lax
from jax.sharding import PartitionSpec as P

HEAD_SIZE = 128


MASKED_SCORE = -1e30


def from_root(value, axis, source):
    kept = jnp.where(lax.axis_index(axis) == source, value, 0).astype(value.dtype)
    return lax.psum(kept, axis)


def head_groups(matrix, kv_count):
    count_rows = matrix.shape[0]
    return matrix.reshape(
        count_rows, kv_count, matrix.shape[1] // (kv_count * HEAD_SIZE), HEAD_SIZE
    ).transpose(1, 0, 2, 3)


def kv_groups(matrix, kv_count):
    return matrix.reshape(matrix.shape[0], kv_count, HEAD_SIZE).transpose(1, 0, 2)


def block_attention(queries, key_rows, value_rows, visible, factor):
    kv_count = key_rows.shape[1] // HEAD_SIZE

    def block_per_head(operands):
        query_part, key_part, value_part = operands
        scores = (
            jnp.einsum("rgd,sd->rgs", query_part, key_part, preferred_element_type=jnp.float32)
            * factor
        )
        shown = visible[:, None, :]
        peak_score = jnp.max(jnp.where(shown, scores, MASKED_SCORE), -1, keepdims=True)
        weights = jnp.where(shown, jnp.exp(scores - peak_score), 0.0)
        totals = jnp.sum(weights, -1)
        output = jnp.einsum(
            "rgs,sd->rgd",
            weights.astype(jnp.bfloat16),
            value_part,
            preferred_element_type=jnp.float32,
        )
        return (output / totals[..., None]).astype(jnp.bfloat16)

    outputs = lax.map(
        block_per_head,
        (
            head_groups(queries, kv_count),
            kv_groups(key_rows, kv_count),
            kv_groups(value_rows, kv_count),
        ),
    )
    return outputs.transpose(1, 0, 2, 3).reshape(queries.shape[0], queries.shape[1])


def query_partials(queries, key_rows, value_rows, visible, factor):
    kv_count = key_rows.shape[1] // HEAD_SIZE

    def query_per_head(operands):
        query_part, key_part, value_part = operands
        scores = (
            jnp.einsum("qgd,sd->qgs", query_part, key_part, preferred_element_type=jnp.float32)
            * factor
        )
        shown = visible[:, None, :]
        peak_score = jnp.max(jnp.where(shown, scores, MASKED_SCORE), -1)
        weights = jnp.where(shown, jnp.exp(scores - peak_score[..., None]), 0.0)
        totals = jnp.sum(weights, -1)
        partial_acc = jnp.einsum(
            "qgs,sd->qgd",
            weights.astype(jnp.bfloat16),
            value_part,
            preferred_element_type=jnp.float32,
        )
        return (peak_score, totals, partial_acc)

    peaks, totals, accums = lax.map(
        query_per_head,
        (
            head_groups(queries, kv_count),
            kv_groups(key_rows, kv_count),
            kv_groups(value_rows, kv_count),
        ),
    )
    query_count = queries.shape[0]
    peaks = peaks.transpose(1, 0, 2).reshape(query_count, -1)
    totals = totals.transpose(1, 0, 2).reshape(query_count, -1)
    accums = accums.transpose(1, 0, 2, 3).reshape(query_count, -1)
    return (peaks, totals, accums)


def on_device(context_queries, context_keys, context_values, doc_ids, query_token_rows, span_start):
    factor = float(HEAD_SIZE) ** (-0.5)
    host_index = lax.axis_index("hosts")
    host_count = lax.axis_size("hosts")
    block_len = context_queries.shape[0]
    per_host = query_token_rows.shape[0]
    stacked = jnp.stack([context_keys, context_values])
    anchor = from_root(stacked, "hosts", 0)
    key_rows = jnp.concatenate([anchor[0], context_keys], 0)
    value_rows = jnp.concatenate([anchor[1], context_values], 0)
    positions = jnp.arange(block_len, dtype=jnp.int32)
    causal = positions[None, :] <= positions[:, None]
    own_visible = causal & (doc_ids[:, None] == doc_ids[None, :])
    front_visible = jnp.broadcast_to(host_index > 0, (block_len, block_len))
    visible = jnp.concatenate([front_visible, own_visible], 1)
    block_out = block_attention(context_queries, key_rows, value_rows, visible, factor)
    all_queries, all_spans = (
        lax.all_gather(query_token_rows, "hosts", axis=0, tiled=True),
        lax.all_gather(span_start, "hosts", axis=0, tiled=True),
    )
    key_positions = host_index * block_len + positions
    query_visible = key_positions[None, :] >= all_spans[:, None]
    peaks, totals, accums = query_partials(
        all_queries, context_keys, context_values, query_visible, factor
    )
    received = (
        lax.all_to_all(peaks, "hosts", split_axis=0, concat_axis=0, tiled=True),
        lax.all_to_all(totals, "hosts", split_axis=0, concat_axis=0, tiled=True),
        lax.all_to_all(accums, "hosts", split_axis=0, concat_axis=0, tiled=True),
    )
    source_peaks = received[0].reshape(host_count, per_host, -1)
    source_totals = received[1].reshape(host_count, per_host, -1)
    source_accums = received[2].reshape(host_count, per_host, -1)
    overall = jnp.max(source_peaks, 0)
    scales = jnp.exp(source_peaks - overall[None])
    own_totals = jnp.sum(scales * source_totals, 0)
    own_accums = jnp.sum(jnp.repeat(scales, HEAD_SIZE, axis=2) * source_accums, 0)
    answer = (own_accums / jnp.repeat(own_totals, HEAD_SIZE, axis=1)).astype(jnp.bfloat16)
    return (block_out, answer)


def solution(mesh):
    in_specs = (
        P(("groups", "hosts"), "tensor"),
        P(("groups", "hosts"), "tensor"),
        P(("groups", "hosts"), "tensor"),
        P(("groups", "hosts")),
        P(("groups", "hosts"), "tensor"),
        P(("groups", "hosts")),
    )
    out_specs = (P(("groups", "hosts"), "tensor"), P(("groups", "hosts"), "tensor"))
    return jax.shard_map(
        on_device, mesh=mesh, in_specs=in_specs, out_specs=out_specs, check_vma=False
    )
```

profile of v0, /device:TPU:0, one launch (start us, length us, event | category | flops | bytes accessed | tf_op | source)
XLA Modules:
  0.0 166.9 jit_solution(4238791645243524496)
XLA Ops:
  7.2 1.1 copy.26
  10.2 0.8 dynamic-update-slice
  11.1 13.1 %all-reduce.1 = s32[8]{0:T(128)S(1)} all-reduce(s32[8]{0:T(128)S(1)} %dynamic-update-slice), channel_id=1, replica_groups=mesh['groups'=2,'hosts'=8,'tensor'=2] {'hosts'}, use_global_device_ids=true, to_apply=%add.1 | all-reduce | flops 8 | bytes 64
  24.2 30.5 %all-gather = bf16[8,1,4096]{2,1,0:T(2,128)(2,1)S(1)} all-gather(bf16[1,1,4096]{2,1,0:T(2,128)(2,1)S(1)} %bitcast.124), channel_id=1, replica_groups=mesh['groups'=2,'hosts'=8,'tensor'=2] {'hosts'}, dimensions={0}, use_global_device_ids=true | all-gather | bytes 73728 | tf_op jit(solution)/shard_map/all_gather | solution.py:113
  55.1 2.7 %while.26 = (s32[]{:T(128)}, f32[4,8,8]{2,1,0:T(8,128)S(1)}, f32[4,8,8]{2,1,0:T(8,128)S(1)}, f32[4,8,8,128]{3,2,1,0:T(8,128)S(1)}, bf16[4,8,8,128]{3,2,0,1:T(8,1...) while((s32[]{:T(128)}, f32[4,8,8]{2,1,0:T(8,128)S(1)}, ...), condition=%wide.region_8.9_spmd.clone, body=%wide.region_5.8_spmd.clone.sunk | while | flops 4268930 | bytes 241033 | solution.py:81
  57.8 0.7 all_to_all.18
  58.5 3.3 %all-to-all-start = ((f32[8,1,32]{2,1,0:T(1,128)}), f32[8,1,32]{2,1,0:T(1,128)S(1)}, u32[]{:S(2)}, u32[]{:S(2)}) async-start(f32[8,1,32]{2,1,0:T(1,128)} %bitcast.23), calls=%async_computation | async-start | bytes 8192 | tf_op jit(solution)/shard_map/all_to_all | solution.py:122
  61.8 0.7 all_to_all.22
  62.5 5.6 %all-to-all-done = f32[8,1,32]{2,1,0:T(1,128)S(1)} async-done(((f32[8,1,32]{2,1,0:T(1,128)}), f32[8,1,32]{2,1,0:T(1,128)S(1)}, u32[]{:S(2)}, u32[]{:S(2)}) %all-to-all-start) | async-done | bytes 1056 | tf_op jit(solution)/shard_map/all_to_all | solution.py:122
  68.1 3.3 %all-to-all-start.2 = ((f32[8,1,32]{2,1,0:T(1,128)}), f32[8,1,32]{2,1,0:T(1,128)S(1)}, u32[]{:S(2)}, u32[]{:S(2)}) async-start(f32[8,1,32]{2,1,0:T(1,128)} %bitcast.30), calls=%async_computation.2 | async-start | bytes 8192 | tf_op jit(solution)/shard_map/all_to_all | solution.py:123
  71.5 0.7 maximum_select_fusion
  72.9 4.9 %all-to-all-done.2 = f32[8,1,32]{2,1,0:T(1,128)S(1)} async-done(((f32[8,1,32]{2,1,0:T(1,128)}), f32[8,1,32]{2,1,0:T(1,128)S(1)}, u32[]{:S(2)}, u32[]{:S(2)}) %all-to-all-start.2) | async-done | bytes 1056 | tf_op jit(solution)/shard_map/all_to_all | solution.py:123
  77.8 3.5 %all-to-all-start.1 = ((f32[8,1,4096]{2,1,0:T(1,128)}), f32[8,1,4096]{2,1,0:T(1,128)S(1)}, u32[]{:S(2)}, u32[]{:S(2)}) async-start(f32[8,1,4096]{2,1,0:T(1,128)} %bitcast.27), calls=%async_computation.1 | async-start | bytes 262144 | tf_op jit(solution)/shard_map/all_to_all | solution.py:124
  82.2 6.7 %all-to-all-done.1 = f32[8,1,4096]{2,1,0:T(1,128)S(1)} async-done(((f32[8,1,4096]{2,1,0:T(1,128)}), f32[8,1,4096]{2,1,0:T(1,128)S(1)}, u32[]{:S(2)}, u32[]{:S(2)}) %all-to-all-start.1) | async-done | bytes 131104 | tf_op jit(solution)/shard_map/all_to_all | solution.py:124
  89.9 58.0 %all-reduce.4.cloned.1.call-done = bf16[2,128,512]{1,2,0:T(8,128)(2,1)} async-done(((bf16[2,128,512]{1,2,0:T(8,128)(2,1)}), bf16[2,128,512]{1,2,0:T(8,128)(2,1)}) %all-reduce.4.cloned.1.call-update) | async-done | bytes 262160 | tf_op jit(solution)/shard_map/psum | solution.py:14
  147.9 1.0 fusion.52
  148.9 0.8 maximum_bitcast_fusion
  149.6 8.3 %while.25 = (s32[]{:T(128)}, bf16[4,128,8,128]{3,1,2,0:T(8,128)(2,1)S(1)}, pred[128,256]{1,0:T(8,128)(4,1)S(1)}, bf16[4,128,8,128]{1,3,2,0:T(8,128)(2,1)S(1)}, b...) while((s32[]{:T(128)}, bf16[4,128,8,128]{3,1,2,0:T(8,128)(2,1)S(1)}, ...), condition=%wide.region_4.5_spmd, body=%wide.region_1.4_spmd.sunk | while | flops 136840704 | bytes 4958285 | solution.py:49
  150.4 1.3 fusion.70
  152.5 1.3 fusion.70
  154.6 1.3 fusion.70
  156.7 1.3 fusion.70
  158.0 0.7 copy.33
  158.7 1.4 copy.53
  (64 shorter events, 9.9 us)
Async XLA Ops:
  7.2 3.7 %copy-start.2 = (bf16[128,512]{1,0:T(8,128)(2,1)S(1)}, bf16[128,512]{1,0:T(8,128)(2,1)}, u32[]{:S(2)}) copy-start(bf16[128,512]{1,0:T(8,128)(2,1)} %param.12) | copy-start | bytes 393220
  8.9 0.7 copy-start.5
  10.9 13.2 %copy-start.3 = (bf16[1,4096]{1,0:T(2,128)(2,1)S(1)}, bf16[1,4096]{1,0:T(2,128)(2,1)}, u32[]{:S(2)}) copy-start(bf16[1,4096]{1,0:T(2,128)(2,1)} %param.14) | copy-start | bytes 24580
  57.8 23.6 %copy-start = (bf16[128,4096]{1,0:T(8,128)(2,1)S(1)}, bf16[128,4096]{1,0:T(8,128)(2,1)}, u32[]{:S(2)}) copy-start(bf16[128,4096]{1,0:T(8,128)(2,1)} %param.10) | copy-start | bytes 3145732
  58.5 9.6 %all-to-all-start = ((f32[8,1,32]{2,1,0:T(1,128)}), f32[8,1,32]{2,1,0:T(1,128)S(1)}, u32[]{:S(2)}, u32[]{:S(2)}) async-start(f32[8,1,32]{2,1,0:T(1,128)} %bitcast.23), calls=%async_computation | async-start | bytes 8192 | tf_op jit(solution)/shard_map/all_to_all | solution.py:122
  68.1 9.6 %all-to-all-start.2 = ((f32[8,1,32]{2,1,0:T(1,128)}), f32[8,1,32]{2,1,0:T(1,128)S(1)}, u32[]{:S(2)}, u32[]{:S(2)}) async-start(f32[8,1,32]{2,1,0:T(1,128)} %bitcast.30), calls=%async_computation.2 | async-start | bytes 8192 | tf_op jit(solution)/shard_map/all_to_all | solution.py:123
  71.5 76.4 %all-reduce.4.cloned.1.call-start = ((), (), s32[]{:S(2)}) async-start(), calls=%async_computation.3 | async-start | bytes 524288 | tf_op jit(solution)/shard_map/psum | solution.py:14
  77.8 3.5 %copy-start.4 = (s32[128]{0:T(128)S(1)}, s32[128]{0:T(128)}, u32[]{:S(2)}) copy-start(s32[128]{0:T(128)} %param.13) | copy-start | bytes 1540
  77.8 11.1 %all-to-all-start.1 = ((f32[8,1,4096]{2,1,0:T(1,128)}), f32[8,1,4096]{2,1,0:T(1,128)S(1)}, u32[]{:S(2)}, u32[]{:S(2)}) async-start(f32[8,1,4096]{2,1,0:T(1,128)} %bitcast.27), calls=%async_computation.1 | async-start | bytes 262144 | tf_op jit(solution)/shard_map/all_to_all | solution.py:124
  82.1 67.5 %copy-start.1 = (bf16[4,128,8,128]{3,1,2,0:T(8,128)(2,1)S(1)}, bf16[4,128,8,128]{3,1,2,0:T(8,128)(2,1)}, u32[]{:S(2)}) copy-start(bf16[4,128,8,128]{3,1,2,0:T(8,128)(2,1)} %custom-call) | copy-start | bytes 3145732
Sparse Core Ops, SparseCore 0:
  75.7 72.1 all-reduce.3
where the time goes:
time: 168 us; the launch traced here: 167 us
  waiting for transfers between devices  75.3 us (45%)
  blocking collectives  43.6 us (26%)
  between operations  14.9 us (9%)
  starting transfers between devices  10.2 us (6%)
  local copies, waits for them, and re-layouts  9.16 us (5%)
  matrix products  8.18 us (5%)
  other arithmetic  5.46 us (3%)
    psum x1, waiting for transfers between devices, from_root(): return lax.psum(kept, axis)  58 us
    all_gather x1, blocking collectives, on_device(): lax.all_gather(query_token_rows, 'hosts', axis=0, tiled=True)  30.5 us
    unnamed x1, blocking collectives  13.1 us
    all_to_all x1, waiting for transfers between devices, on_device(): lax.all_to_all(accums, 'hosts', split_axis=0, concat_axis=0, tiled=True)  6.74 us
    all_to_all x1, waiting for transfers between devices, on_device(): lax.all_to_all(peaks, 'hosts', split_axis=0, concat_axis=0, tiled=True)  5.63 us
    unnamed x20, local copies, waits for them, and re-layouts  5.27 us
    dot_general x4, matrix products, block_per_head(): jnp.einsum('rgs,sd->rgd', weights.astype(jnp.bfloat16), value_part, prefe...  5.21 us
    all_to_all x1, waiting for transfers between devices, on_device(): lax.all_to_all(totals, 'hosts', split_axis=0, concat_axis=0, tiled=True)  4.86 us
  transfers between devices with their start and end apart: 4, of which 4 were waited for; matrix products, arithmetic and copies ran while one was open for 2% of the time, Pallas kernels for 0%

commit v1 on v0

v1 whole, which is shorter than its diff:
```python
import functools

import jax
import jax.numpy as jnp
from jax import lax
from jax.experimental import pallas as pl
from jax.experimental.pallas import tpu as pltpu
from jax.sharding import PartitionSpec as P

HEAD_SIZE = 128
MASKED_SCORE = -1e30
FACTOR = float(HEAD_SIZE) ** -0.5
LOG2E = 1.4426950408889634
VMEM = pl.BlockSpec(memory_space=pltpu.VMEM)
SMEM = pl.BlockSpec(memory_space=pltpu.SMEM)
NT = (((1,), (1,)), ((), ()))


def dot_nt(a, b):
    return lax.dot_general(a, b, NT, preferred_element_type=jnp.float32)


def dot_nn(a, b):
    return jnp.dot(a, b, preferred_element_type=jnp.float32)


def prepare_kernel(span_ref, query_ref, key_ref, value_ref, message_ref, *piece_refs):
    heads = query_ref.shape[1] // HEAD_SIZE
    query = query_ref[...].astype(jnp.float32)
    for head in range(heads):
        message_ref[head : head + 1, :] = query[:, head * HEAD_SIZE : (head + 1) * HEAD_SIZE]
    start = span_ref[0].astype(jnp.float32)
    message_ref[heads : heads + 8, :] = jnp.full((8, HEAD_SIZE), start, jnp.float32)
    for index, piece_ref in enumerate(piece_refs):
        columns = slice(index * HEAD_SIZE, (index + 1) * HEAD_SIZE)
        rows = key_ref.shape[0]
        piece_ref[:rows, :] = key_ref[:, columns]
        piece_ref[rows:, :] = value_ref[:, columns]


def prepare(query_row, span, keys, values):
    heads = query_row.shape[1] // HEAD_SIZE
    kv_count = keys.shape[1] // HEAD_SIZE
    rows = keys.shape[0]
    piece = jax.ShapeDtypeStruct((2 * rows, HEAD_SIZE), keys.dtype)
    return pl.pallas_call(
        prepare_kernel,
        out_shape=[jax.ShapeDtypeStruct((heads + 8, HEAD_SIZE), jnp.float32)] + [piece] * kv_count,
        in_specs=[SMEM, VMEM, VMEM, VMEM],
        out_specs=[VMEM] * (1 + kv_count),
        cost_estimate=pl.CostEstimate(flops=1000, bytes_accessed=600000, transcendentals=0),
        name="prepare",
    )(span, query_row, keys, values)


def partials_kernel(host_ref, k0_ref, v0_ref, k1_ref, v1_ref, *refs):
    sources = len(refs) // 2
    message_refs, out_refs = refs[:sources], refs[sources:]
    block = k0_ref.shape[0]
    kv_count = k0_ref.shape[1] // HEAD_SIZE
    heads = message_refs[0].shape[0] - 8
    per_kv = heads // kv_count
    rows = sources * heads
    host = host_ref[0]
    queries = jnp.concatenate([ref[:heads, :] for ref in message_refs], 0).astype(jnp.bfloat16)
    starts = jnp.concatenate(
        [jnp.broadcast_to(ref[heads : heads + 1, :], (heads, HEAD_SIZE)) for ref in message_refs], 0
    )
    row_kv = (lax.broadcasted_iota(jnp.int32, (rows, HEAD_SIZE), 0) % heads) // per_kv
    lanes = lax.broadcasted_iota(jnp.int32, (rows, block), 1)

    def chosen(per_head):
        out = per_head[0]
        for index in range(1, kv_count):
            out = jnp.where(row_kv == index, per_head[index], out)
        return out

    scores, shown = [], []
    for key_ref, at in ((k0_ref, host), (k1_ref, host ^ 1)):
        scores.append(
            chosen(
                [
                    dot_nt(queries, key_ref[:, h * HEAD_SIZE : (h + 1) * HEAD_SIZE])
                    for h in range(kv_count)
                ]
            )
            * FACTOR
        )
        shown.append((lanes + at * block).astype(jnp.float32) >= starts)
    masked = [jnp.where(s, x, MASKED_SCORE) for s, x in zip(shown, scores)]
    peak = jnp.max(jnp.maximum(masked[0], masked[1]), -1, keepdims=True)
    weights = [
        jnp.where(s, jnp.exp2((x - peak) * LOG2E), 0.0) for s, x in zip(shown, masked)
    ]
    total = jnp.sum(weights[0] + weights[1], -1, keepdims=True)
    rounded = [w.astype(jnp.bfloat16) for w in weights]
    acc = chosen(
        [
            dot_nn(rounded[0], v0_ref[:, h * HEAD_SIZE : (h + 1) * HEAD_SIZE])
            + dot_nn(rounded[1], v1_ref[:, h * HEAD_SIZE : (h + 1) * HEAD_SIZE])
            for h in range(kv_count)
        ]
    )
    peak_row = jnp.transpose(jnp.broadcast_to(peak, (rows, HEAD_SIZE)))[0:1, :]
    total_row = jnp.transpose(jnp.broadcast_to(total, (rows, HEAD_SIZE)))[0:1, :]
    for index, out_ref in enumerate(out_refs):
        out_ref[:heads, :] = acc[index * heads : (index + 1) * heads, :]
        out_ref[heads : heads + 1, :] = peak_row[:, :HEAD_SIZE]
        out_ref[heads + 1 : heads + 2, :] = total_row[:, :HEAD_SIZE]
        out_ref[heads + 2 : heads + 8, :] = jnp.zeros((6, HEAD_SIZE), jnp.float32)


def partials(host, k0, v0, k1, v1, messages):
    shape = jax.ShapeDtypeStruct(messages[0].shape, jnp.float32)
    return pl.pallas_call(
        partials_kernel,
        out_shape=[shape] * len(messages),
        in_specs=[SMEM] + [VMEM] * (4 + len(messages)),
        out_specs=[VMEM] * len(messages),
        cost_estimate=pl.CostEstimate(flops=1000000, bytes_accessed=900000, transcendentals=40000),
        name="query_partials",
    )(host, k0, v0, k1, v1, *messages)


def merge_kernel(*refs):
    part_refs, answer_ref = refs[:-1], refs[-1]
    heads = part_refs[0].shape[0] - 8
    row = lax.broadcasted_iota(jnp.int32, (heads, HEAD_SIZE), 0)
    lane = lax.broadcasted_iota(jnp.int32, (heads, HEAD_SIZE), 1)

    def column(ref, at, index):
        spread = jnp.broadcast_to(ref[at : at + 1, :], (heads, HEAD_SIZE))
        return jnp.sum(jnp.where(lane == row + index * heads, spread, 0.0), -1, keepdims=True)

    peaks = [column(ref, heads, index) for index, ref in enumerate(part_refs)]
    totals = [column(ref, heads + 1, index) for index, ref in enumerate(part_refs)]
    peak = functools.reduce(jnp.maximum, peaks)
    scales = [jnp.exp(p - peak) for p in peaks]
    total = functools.reduce(jnp.add, [s * t for s, t in zip(scales, totals)])
    merged = functools.reduce(
        jnp.add, [s * ref[:heads, :] for s, ref in zip(scales, part_refs)]
    )
    answer = (merged / total).astype(answer_ref.dtype)
    for head in range(heads):
        answer_ref[:, head * HEAD_SIZE : (head + 1) * HEAD_SIZE] = answer[head : head + 1, :]


def merge(parts):
    heads = parts[0].shape[0] - 8
    return pl.pallas_call(
        merge_kernel,
        out_shape=jax.ShapeDtypeStruct((1, heads * HEAD_SIZE), jnp.bfloat16),
        in_specs=[VMEM] * len(parts),
        out_specs=VMEM,
        cost_estimate=pl.CostEstimate(flops=100000, bytes_accessed=90000, transcendentals=1000),
        name="merge_answer",
    )(*parts)


def context_kernel(
    host_ref, column_ref, doc_ref, query_ref, key_ref, value_ref, *refs
):
    piece_refs, out_ref, bias_ref = refs[:-2], refs[-2], refs[-1]
    step = pl.program_id(0)
    block = query_ref.shape[0]
    heads = query_ref.shape[1] // HEAD_SIZE
    scale = FACTOR * LOG2E

    @pl.when(step == 0)
    def _():
        row = lax.broadcasted_iota(jnp.int32, (block, block), 0)
        lane = lax.broadcasted_iota(jnp.int32, (block, block), 1)
        along = jnp.broadcast_to(doc_ref[...].astype(jnp.float32), (block, block))
        visible = (lane <= row) & (jnp.transpose(along) == along)
        bias_ref[...] = jnp.where(visible, 0.0, MASKED_SCORE)

    anchor = piece_refs[0][...]
    for index in range(1, len(piece_refs)):
        anchor = jnp.where(step == index, piece_refs[index][...], anchor)
    anchor_keys, anchor_values = anchor[:block, :], anchor[block:, :]
    bias = bias_ref[...]
    front = jnp.where(host_ref[0] > 0, 0.0, MASKED_SCORE)
    keys = key_ref[...]
    values = jnp.concatenate([value_ref[...], anchor_values], 0)
    values = jnp.concatenate([values, jnp.ones((2 * block, HEAD_SIZE), values.dtype)], 1)
    for head in range(heads):
        columns = slice(head * HEAD_SIZE, (head + 1) * HEAD_SIZE)
        query = query_ref[:, columns]
        own = dot_nt(query, keys) + bias
        far = dot_nt(query, anchor_keys) + front
        peak = jnp.max(jnp.maximum(own, far), -1, keepdims=True)
        weights = jnp.concatenate(
            [
                jnp.exp2((own - peak) * scale).astype(jnp.bfloat16),
                jnp.exp2((far - peak) * scale).astype(jnp.bfloat16),
            ],
            1,
        )
        sums = dot_nn(weights, values)
        out_ref[:, columns] = (sums[:, :HEAD_SIZE] / sums[:, HEAD_SIZE:]).astype(out_ref.dtype)


def context_attention(host, column, doc_row, queries, keys, values, pieces):
    block, width = queries.shape
    kv_count = keys.shape[1] // HEAD_SIZE
    group = width // kv_count

    def head_of(step, host_ref, column_ref):
        return (0, step ^ column_ref[0])

    whole = pl.BlockSpec(pieces[0].shape, lambda step, *_: (0, 0))
    return pl.pallas_call(
        context_kernel,
        out_shape=jax.ShapeDtypeStruct((block, width), queries.dtype),
        grid_spec=pltpu.PrefetchScalarGridSpec(
            num_scalar_prefetch=2,
            grid=(kv_count,),
            in_specs=[
                pl.BlockSpec((1, block), lambda step, *_: (0, 0)),
                pl.BlockSpec((block, group), head_of),
                pl.BlockSpec((block, HEAD_SIZE), head_of),
                pl.BlockSpec((block, HEAD_SIZE), head_of),
            ]
            + [whole] * len(pieces),
            out_specs=pl.BlockSpec((block, group), head_of),
            scratch_shapes=[pltpu.VMEM((block, block), jnp.float32)],
        ),
        cost_estimate=pl.CostEstimate(
            flops=4 * block * 2 * block * width, bytes_accessed=2600000, transcendentals=1000000
        ),
        name="context_attention",
    )(host, column, doc_row, queries, keys, values, *pieces)


def paired(context_queries, context_keys, context_values, doc_ids, query_token_rows, span_start):
    host_count = lax.axis_size("hosts")
    host = lax.axis_index("hosts")
    depth = host_count // 2
    place, side = host // 2, host % 2
    block = context_queries.shape[0]

    def swap(value, mask):
        return lax.ppermute(value, "hosts", [(i, i ^ mask) for i in range(host_count)])

    message, *own_pieces = prepare(query_token_rows, span_start, context_keys, context_values)
    other_keys, other_values = swap(context_keys, 1), swap(context_values, 1)
    messages = [message] + [swap(message, 2 * k) for k in range(1, depth)]
    sent = [lax.ppermute(own_pieces[k], "hosts", [(0, 2 * k)]) for k in range(1, depth)]
    piece = jnp.where(place == 0, own_pieces[0], functools.reduce(jnp.add, sent))
    piece = jnp.where(side == 0, piece, swap(piece, 1))
    pieces = [piece] + [swap(piece, 2 * k) for k in range(1, depth)]
    host_word = host.reshape(1).astype(jnp.int32)
    parts = partials(
        host_word, context_keys, context_values, other_keys, other_values, messages
    )
    parts = [parts[0]] + [swap(parts[k], 2 * k) for k in range(1, depth)]
    answer = merge(parts)
    block_out = context_attention(
        host_word,
        place.reshape(1).astype(jnp.int32),
        doc_ids.reshape(1, block),
        context_queries,
        context_keys,
        context_values,
        pieces,
    )
    return block_out, answer


def from_root(value, axis, source):
    kept = jnp.where(lax.axis_index(axis) == source, value, 0).astype(value.dtype)
    return lax.psum(kept, axis)


def head_groups(matrix, kv_count):
    count_rows = matrix.shape[0]
    return matrix.reshape(
        count_rows, kv_count, matrix.shape[1] // (kv_count * HEAD_SIZE), HEAD_SIZE
    ).transpose(1, 0, 2, 3)


def kv_groups(matrix, kv_count):
    return matrix.reshape(matrix.shape[0], kv_count, HEAD_SIZE).transpose(1, 0, 2)


def query_partials(queries, key_rows, value_rows, visible):
    kv_count = key_rows.shape[1] // HEAD_SIZE

    def query_per_head(operands):
        query_part, key_part, value_part = operands
        scores = (
            jnp.einsum("qgd,sd->qgs", query_part, key_part, preferred_element_type=jnp.float32)
            * FACTOR
        )
        shown = visible[:, None, :]
        peak_score = jnp.max(jnp.where(shown, scores, MASKED_SCORE), -1)
        weights = jnp.where(shown, jnp.exp(scores - peak_score[..., None]), 0.0)
        totals = jnp.sum(weights, -1)
        partial_acc = jnp.einsum(
            "qgs,sd->qgd",
            weights.astype(jnp.bfloat16),
            value_part,
            preferred_element_type=jnp.float32,
        )
        return (peak_score, totals, partial_acc)

    peaks, totals, accums = lax.map(
        query_per_head,
        (
            head_groups(queries, kv_count),
            kv_groups(key_rows, kv_count),
            kv_groups(value_rows, kv_count),
        ),
    )
    query_count = queries.shape[0]
    peaks = peaks.transpose(1, 0, 2).reshape(query_count, -1)
    totals = totals.transpose(1, 0, 2).reshape(query_count, -1)
    accums = accums.transpose(1, 0, 2, 3).reshape(query_count, -1)
    return (peaks, totals, accums)


def gathered(context_queries, context_keys, context_values, doc_ids, query_token_rows, span_start):
    host = lax.axis_index("hosts")
    host_count = lax.axis_size("hosts")
    block = context_queries.shape[0]
    per_host = query_token_rows.shape[0]
    kv_count = context_keys.shape[1] // HEAD_SIZE
    anchor = from_root(jnp.stack([context_keys, context_values]), "hosts", 0)
    pieces = [
        anchor[:, :, h * HEAD_SIZE : (h + 1) * HEAD_SIZE].reshape(2 * block, HEAD_SIZE)
        for h in range(kv_count)
    ]
    block_out = context_attention(
        host.reshape(1).astype(jnp.int32),
        jnp.zeros((1,), jnp.int32),
        doc_ids.reshape(1, block),
        context_queries,
        context_keys,
        context_values,
        pieces,
    )
    all_queries, all_spans = (
        lax.all_gather(query_token_rows, "hosts", axis=0, tiled=True),
        lax.all_gather(span_start, "hosts", axis=0, tiled=True),
    )
    key_positions = host * block + jnp.arange(block, dtype=jnp.int32)
    query_visible = key_positions[None, :] >= all_spans[:, None]
    peaks, totals, accums = query_partials(
        all_queries, context_keys, context_values, query_visible
    )
    received = [
        lax.all_to_all(x, "hosts", split_axis=0, concat_axis=0, tiled=True).reshape(
            host_count, per_host, -1
        )
        for x in (peaks, totals, accums)
    ]
    source_peaks, source_totals, source_accums = received
    overall = jnp.max(source_peaks, 0)
    scales = jnp.exp(source_peaks - overall[None])
    own_totals = jnp.sum(scales * source_totals, 0)
    own_accums = jnp.sum(jnp.repeat(scales, HEAD_SIZE, axis=2) * source_accums, 0)
    answer = (own_accums / jnp.repeat(own_totals, HEAD_SIZE, axis=1)).astype(jnp.bfloat16)
    return (block_out, answer)


def solution(mesh):
    rows = P(("groups", "hosts"), "tensor")
    words = P(("groups", "hosts"))

    def on_device(context_queries, context_keys, context_values, doc_ids, query_rows, span_start):
        kv_count = context_keys.shape[1] // HEAD_SIZE
        fits = mesh.shape["hosts"] == 2 * kv_count and kv_count == 4 and query_rows.shape[0] == 1
        plan = paired if fits else gathered
        return plan(
            context_queries, context_keys, context_values, doc_ids, query_rows, span_start
        )

    return jax.shard_map(
        on_device,
        mesh=mesh,
        in_specs=(rows, rows, rows, words, rows, words),
        out_specs=(rows, rows),
        check_vma=False,
    )
```

time: 168 us -> 53.4 us (0.32)
  waiting for transfers between devices: 75.3 us -> 5.83 us
  blocking collectives: 43.6 us -> 0 us
  starting transfers between devices: 10.2 us -> 27 us
  Pallas kernels: 0 us -> 15.9 us
  between operations: 14.9 us -> 1.46 us
  matrix products: 8.18 us -> 0 us
  local copies, waits for them, and re-layouts: 9.16 us -> 1.93 us
  other arithmetic: 5.46 us -> 0.91 us
    psum x1 -> x0, waiting for transfers between devices: 58 us -> none  [from_root(): return lax.psum(kept, axis)]
    all_gather x1 -> x0, blocking collectives: 30.5 us -> none  [on_device(): lax.all_gather(query_token_rows, 'hosts', axis=0, tiled=True)]
    ppermute x0 -> x15, starting transfers between devices: none -> 27 us  [the longest x12 18.7 us: swap(): lax.ppermute(value, 'hosts', [(i, i ^ mask) for i in range(host_count)])]
    all_to_all x3 -> x0, waiting for transfers between devices: 17.2 us -> none  [the longest x1 6.74 us: on_device(): lax.all_to_all(accums, 'hosts', split_axis=0, concat_axis=0, tiled=True)]
    pallas_call x0 -> x4, Pallas kernels: none -> 15.9 us  [the longest x1 10.4 us: context_attention(): pl.pallas_call(context_kernel, out_shape=jax.ShapeDtypeStruct((block, wid...]
    unnamed x1 -> x0, blocking collectives: 13.1 us -> none
    all_to_all x3 -> x0, starting transfers between devices: 10.1 us -> none  [the longest x1 3.5 us: on_device(): lax.all_to_all(accums, 'hosts', split_axis=0, concat_axis=0, tiled=True)]
    dot_general x16 -> x0, matrix products: 8.18 us -> none  [the longest x4 5.21 us: block_per_head(): jnp.einsum('rgs,sd->rgd', weights.astype(jnp.bfloat16), value_part, prefe...]
  transfers between devices with their start and end apart: 4 -> 15, of which waited for: 4 -> 4; matrix products, arithmetic and copies ran while one was open for 2% -> 0% of each run, Pallas kernels for 0% -> 7%
where the time goes in v1:
time: 53.4 us; the launch traced here: 53.1 us
  starting transfers between devices  27 us (51%)
  Pallas kernels  15.9 us (30%)
  waiting for transfers between devices  5.83 us (11%)
  local copies, waits for them, and re-layouts  1.93 us (4%)
  between operations  1.46 us (3%)
  other arithmetic  0.91 us (2%)
    ppermute x12, starting transfers between devices, swap(): lax.ppermute(value, 'hosts', [(i, i ^ mask) for i in range(host_count)])  18.7 us
    pallas_call x1, Pallas kernels, context_attention(): pl.pallas_call(context_kernel, out_shape=jax.ShapeDtypeStruct((block, wid...  10.4 us
    ppermute x3, starting transfers between devices, paired(): lax.ppermute(own_pieces[k], 'hosts', [(0, 2 * k)])  8.27 us
    ppermute x12, waiting for transfers between devices, swap(): lax.ppermute(value, 'hosts', [(i, i ^ mask) for i in range(host_count)])  3.65 us
    pallas_call x1, Pallas kernels, partials(): pl.pallas_call(partials_kernel, out_shape=[shape] * len(messages), in_spe...  2.34 us
    ppermute x3, waiting for transfers between devices, paired(): lax.ppermute(own_pieces[k], 'hosts', [(0, 2 * k)])  2.18 us
    unnamed x30, local copies, waits for them, and re-layouts  1.93 us
    pallas_call x1, Pallas kernels, prepare(): pl.pallas_call(prepare_kernel, out_shape=[jax.ShapeDtypeStruct((heads + 8...  1.71 us
  transfers between devices with their start and end apart: 15, of which 4 were waited for; matrix products, arithmetic and copies ran while one was open for 0% of the time, Pallas kernels for 7%

profile of v1, /device:TPU:0, one launch (start us, length us, event | category | flops | bytes accessed | tf_op | source)
XLA Modules:
  0.0 53.1 jit_solution(9364836927527652897)
XLA Ops:
  1.3 1.7 %prepare.1 = (f32[40,128]{1,0:T(8,128)}, bf16[256,128]{1,0:T(8,128)(2,1)}, bf16[256,128]{1,0:T(8,128)(2,1)}, bf16[256,128]{1,0:T(8,128)(2,1)}, bf16[256,128]{1,0:T(8,128)(2,1)}) custom-call(s32[1]{0:T(128)S(6)} %copy.8.span_ref, bf16[1,4096]{1,0:T(2,128)(2,1)} %query_ref.2, bf16[128,512]{1,0:T(8,128)(2,1)} %k0_ref.1, bf16[128,512]{1,0:T(8,128)(2,1)} %v0_ref.1), custom_call_target="tpu_custom_call" | custom-call | flops 1000 | bytes 600000 | tf_op jit(solution)/shard_map/prepare/pallas_call | solution.py:46
  3.0 4.9 %collective-permute-start = (bf16[256,128]{1,0:T(8,128)(2,1)}, bf16[256,128]{1,0:T(8,128)(2,1)S(1)}, u32[]{:S(2)}, u32[]{:S(2)}) collective-permute-start(bf16[256,128]{1,0:T(8,128)(2,1)} %get-tuple-element.12), channel_id=1, source_target_pairs={{0,4},{1,5},{16,20},{17,21}} | collective-permute-start | bytes 196616 | tf_op jit(solution)/shard_map/ppermute | solution.py:248
  7.9 1.7 %collective-permute-start.1 = (bf16[256,128]{1,0:T(8,128)(2,1)}, bf16[256,128]{1,0:T(8,128)(2,1)S(1)}, u32[]{:S(2)}, u32[]{:S(2)}) collective-permute-start(bf16[256,128]{1,0:T(8,128)(2,1)} %get-tuple-element.13), channel_id=1, source_target_pairs={{0,8},{1,9},{16,24},{17,25}} | collective-permute-start | bytes 196616 | tf_op jit(solution)/shard_map/ppermute | solution.py:248
  9.6 1.7 %collective-permute-start.2 = (bf16[256,128]{1,0:T(8,128)(2,1)}, bf16[256,128]{1,0:T(8,128)(2,1)S(1)}, u32[]{:S(2)}, u32[]{:S(2)}) collective-permute-start(bf16[256,128]{1,0:T(8,128)(2,1)} %get-tuple-element.14), channel_id=1, source_target_pairs={{0,12},{1,13},{16,28},{17,29}} | collective-permute-start | bytes 196616 | tf_op jit(solution)/shard_map/ppermute | solution.py:248
  11.3 0.6 %collective-permute-done.1 = bf16[256,128]{1,0:T(8,128)(2,1)S(1)} collective-permute-done((bf16[256,128]{1,0:T(8,128)(2,1)}, bf16[256,128]{1,0:T(8,128)(2,1)S(1)}, u32[]{:S(2)}, u32[]{:S(2)}) %collective-permute-start.1) | collective-permute-done | bytes 65568 | tf_op jit(solution)/shard_map/ppermute | solution.py:248
  11.9 1.6 %collective-permute-done.2 = bf16[256,128]{1,0:T(8,128)(2,1)S(1)} collective-permute-done((bf16[256,128]{1,0:T(8,128)(2,1)}, bf16[256,128]{1,0:T(8,128)(2,1)S(1)}, u32[]{:S(2)}, u32[]{:S(2)}) %collective-permute-start.2) | collective-permute-done | bytes 65568 | tf_op jit(solution)/shard_map/ppermute | solution.py:248
  13.5 0.9 %add_select_fusion = bf16[256,128]{1,0:T(8,128)(2,1)S(1)} fusion(bf16[256,128]{1,0:T(8,128)(2,1)} %get-tuple-element.11, bf16[256,128]{1,0:T(8,128)(2,1)S(1)} %collective-permute-done.2, bf16[256,128]{1,0:T(8,128)(2,1)S(1)} %collective-permute-done, bf16[256,128]{1,0:T(8,128)(2,1)S(1)} %collective-permute-done.1, pred[]{:T(512)S(6)} %eq.9), kind=kLoop, calls=%fused_computation | loop fusion | flops 98304 | bytes 327681 | tf_op jit(solution)/shard_map/jit(_where)/select_n | solution.py:249
  14.5 2.0 %collective-permute-start.7 = (bf16[128,512]{1,0:T(8,128)(2,1)S(1)}, bf16[128,512]{1,0:T(8,128)(2,1)S(1)}, u32[]{:S(2)}, u32[]{:S(2)}) collective-permute-start(bf16[128,512]{1,0:T(8,128)(2,1)S(1)} %copy-done), channel_id=1, source_target_pairs={{0,2},{2,0},{4,6},{6,4},{8,10},{10,8},{12,14},{14,12},{1,3},{3,1},... | collective-permute-start | bytes 393224 | tf_op jit(solution)/shard_map/ppermute | solution.py:243
  16.5 0.1 collective-permute-start.8
  16.6 3.9 %collective-permute-start.11 = (f32[40,128]{1,0:T(8,128)S(1)}, f32[40,128]{1,0:T(8,128)S(1)}, u32[]{:S(2)}, u32[]{:S(2)}) collective-permute-start(f32[40,128]{1,0:T(8,128)S(1)} %copy-done.8), channel_id=1, source_target_pairs={{0,12},{2,14},{4,8},{6,10},{8,4},{10,6},{12,0},{14,2},{1,13},{3,15... | collective-permute-start | bytes 61448 | tf_op jit(solution)/shard_map/ppermute | solution.py:243
  20.5 0.6 %collective-permute-start.9 = (f32[40,128]{1,0:T(8,128)S(1)}, f32[40,128]{1,0:T(8,128)S(1)}, u32[]{:S(2)}, u32[]{:S(2)}) collective-permute-start(f32[40,128]{1,0:T(8,128)S(1)} %copy-done.8), channel_id=1, source_target_pairs={{0,4},{2,6},{4,0},{6,2},{8,12},{10,14},{12,8},{14,10},{1,5},{3,7},... | collective-permute-start | bytes 61448 | tf_op jit(solution)/shard_map/ppermute | solution.py:243
  21.1 1.3 %collective-permute-done.11.refs_3_ = f32[40,128]{1,0:T(8,128)S(1)} collective-permute-done((f32[40,128]{1,0:T(8,128)S(1)}, f32[40,128]{1,0:T(8,128)S(1)}, u32[]{:S(2)}, u32[]{:S(2)}) %collective-permute-start.11) | collective-permute-done | bytes 20512 | tf_op jit(solution)/shard_map/ppermute | solution.py:243
  22.3 3.7 %collective-permute-start.6 = (bf16[256,128]{1,0:T(8,128)(2,1)S(1)}, bf16[256,128]{1,0:T(8,128)(2,1)S(1)}, u32[]{:S(2)}, u32[]{:S(2)}) collective-permute-start(bf16[256,128]{1,0:T(8,128)(2,1)S(1)} %broadcast_select_fusion.refs_0_), channel_id=1, source_target_pairs={{0,12},{2,14},{4,8},{6,10},{8,4},{10,6},{12,0},{14,2},{1,13},{3,15... | collective-permute-start | bytes 196616 | tf_op jit(solution)/shard_map/ppermute | solution.py:243
  26.1 0.7 %collective-permute-start.4 = (bf16[256,128]{1,0:T(8,128)(2,1)S(1)}, bf16[256,128]{1,0:T(8,128)(2,1)S(1)}, u32[]{:S(2)}, u32[]{:S(2)}) collective-permute-start(bf16[256,128]{1,0:T(8,128)(2,1)S(1)} %broadcast_select_fusion.refs_0_), channel_id=1, source_target_pairs={{0,4},{2,6},{4,0},{6,2},{8,12},{10,14},{12,8},{14,10},{1,5},{3,7},... | collective-permute-start | bytes 196616 | tf_op jit(solution)/shard_map/ppermute | solution.py:243
  26.8 0.6 %copy-done.3 = bf16[128,512]{1,0:T(8,128)(2,1)} copy-done((bf16[128,512]{1,0:T(8,128)(2,1)}, bf16[128,512]{1,0:T(8,128)(2,1)S(1)}, u32[]{:S(2)}) %copy-start.3) | copy-done | bytes 131096
  27.4 2.3 %query_partials.1 = (f32[40,128]{1,0:T(8,128)}, f32[40,128]{1,0:T(8,128)}, f32[40,128]{1,0:T(8,128)}, f32[40,128]{1,0:T(8,128)}) custom-call(s32[1]{0:T(128)} %bitcast.host_ref, bf16[128,512]{1,0:T(8,128)(2,1)} %k0_ref.1, bf16[128,512]{1,0:T(8,128)(2,1)} %v0_ref.1, bf16[128,512]{1,0:T(8,128)(2,1)} %copy-done.3, bf16[128,512]{1,0:T(8,128)(2,1)} %copy-done.4, ...), custom_call_target="tpu_custom_call" | custom-call | flops 1000000 | bytes 900000 | tf_op jit(solution)/shard_map/query_partials/pallas_call | solution.py:115
  29.8 1.5 %collective-permute-start.12 = (f32[40,128]{1,0:T(8,128)}, f32[40,128]{1,0:T(8,128)S(1)}, u32[]{:S(2)}, u32[]{:S(2)}) collective-permute-start(f32[40,128]{1,0:T(8,128)} %get-tuple-element.17), channel_id=1, source_target_pairs={{0,4},{2,6},{4,0},{6,2},{8,12},{10,14},{12,8},{14,10},{1,5},{3,7},... | collective-permute-start | bytes 61448 | tf_op jit(solution)/shard_map/ppermute | solution.py:243
  31.3 2.8 %collective-permute-start.13 = (f32[40,128]{1,0:T(8,128)}, f32[40,128]{1,0:T(8,128)S(1)}, u32[]{:S(2)}, u32[]{:S(2)}) collective-permute-start(f32[40,128]{1,0:T(8,128)} %get-tuple-element.18), channel_id=1, source_target_pairs={{0,8},{2,10},{4,12},{6,14},{8,0},{10,2},{12,4},{14,6},{1,9},{3,11}... | collective-permute-start | bytes 61448 | tf_op jit(solution)/shard_map/ppermute | solution.py:243
  34.1 3.4 %collective-permute-start.14 = (f32[40,128]{1,0:T(8,128)}, f32[40,128]{1,0:T(8,128)S(1)}, u32[]{:S(2)}, u32[]{:S(2)}) collective-permute-start(f32[40,128]{1,0:T(8,128)} %get-tuple-element.19), channel_id=1, source_target_pairs={{0,12},{2,14},{4,8},{6,10},{8,4},{10,6},{12,0},{14,2},{1,13},{3,15... | collective-permute-start | bytes 61448 | tf_op jit(solution)/shard_map/ppermute | solution.py:243
  37.5 2.4 %collective-permute-done.14.refs_3_ = f32[40,128]{1,0:T(8,128)S(1)} collective-permute-done((f32[40,128]{1,0:T(8,128)}, f32[40,128]{1,0:T(8,128)S(1)}, u32[]{:S(2)}, u32[]{:S(2)}) %collective-permute-start.14) | collective-permute-done | bytes 20512 | tf_op jit(solution)/shard_map/ppermute | solution.py:243
  39.9 0.6 %copy-done.14 = f32[40,128]{1,0:T(8,128)} copy-done((f32[40,128]{1,0:T(8,128)}, f32[40,128]{1,0:T(8,128)S(1)}, u32[]{:S(2)}) %copy-start.14) | copy-done | bytes 20504
  40.5 1.5 %merge_answer.1 = bf16[1,4096]{1,0:T(2,128)(2,1)} custom-call(f32[40,128]{1,0:T(8,128)} %get-tuple-element.16.refs_0_, f32[40,128]{1,0:T(8,128)} %copy-done.12, f32[40,128]{1,0:T(8,128)} %copy-done.13, f32[40,128]{1,0:T(8,128)} %copy-done.14), custom_call_target="tpu_custom_call" | custom-call | flops 100000 | bytes 90000 | tf_op jit(solution)/shard_map/merge_answer/pallas_call | solution.py:150
  42.0 0.6 %copy-done.5 = bf16[256,128]{1,0:T(8,128)(2,1)} copy-done((bf16[256,128]{1,0:T(8,128)(2,1)}, bf16[256,128]{1,0:T(8,128)(2,1)S(1)}, u32[]{:S(2)}) %copy-start.5) | copy-done | bytes 65560
  42.7 10.4 %context_attention.1 = bf16[128,4096]{1,0:T(8,128)(2,1)} custom-call(s32[1]{0:T(128)} %bitcast.host_ref, s32[1]{0:T(128)} %bitcast.1.column_ref, s32[1,128]{1,0:T(1,128)} %bitcast.3, bf16[128,4096]{1,0:T(8,128)(2,1)} %query_ref.3, bf16[128,512]{1,0:T(8,128)(2,1)} %k0_ref.1, bf16[128,512]{1,0:T(8,128)(2,1)} %v0_ref.1, bf16[256,128]{1,0:T(8,128)(2,1)} %copy-done.2, ...), custom_call_target="tpu_custom_call" | custom-call | flops 536870912 | bytes 2600000 | tf_op jit(solution)/shard_map/context_attention/pallas_call | solution.py:212
  (42 shorter events, 0.3 us)
Async XLA Ops:
  3.0 8.3 %collective-permute-start = (bf16[256,128]{1,0:T(8,128)(2,1)}, bf16[256,128]{1,0:T(8,128)(2,1)S(1)}, u32[]{:S(2)}, u32[]{:S(2)}) collective-permute-start(bf16[256,128]{1,0:T(8,128)(2,1)} %get-tuple-element.12), channel_id=1, source_target_pairs={{0,4},{1,5},{16,20},{17,21}} | collective-permute-start | bytes 196616 | tf_op jit(solution)/shard_map/ppermute | solution.py:248
  7.9 4.0 %collective-permute-start.1 = (bf16[256,128]{1,0:T(8,128)(2,1)}, bf16[256,128]{1,0:T(8,128)(2,1)S(1)}, u32[]{:S(2)}, u32[]{:S(2)}) collective-permute-start(bf16[256,128]{1,0:T(8,128)(2,1)} %get-tuple-element.13), channel_id=1, source_target_pairs={{0,8},{1,9},{16,24},{17,25}} | collective-permute-start | bytes 196616 | tf_op jit(solution)/shard_map/ppermute | solution.py:248
  9.6 3.9 %collective-permute-start.2 = (bf16[256,128]{1,0:T(8,128)(2,1)}, bf16[256,128]{1,0:T(8,128)(2,1)S(1)}, u32[]{:S(2)}, u32[]{:S(2)}) collective-permute-start(bf16[256,128]{1,0:T(8,128)(2,1)} %get-tuple-element.14), channel_id=1, source_target_pairs={{0,12},{1,13},{16,28},{17,29}} | collective-permute-start | bytes 196616 | tf_op jit(solution)/shard_map/ppermute | solution.py:248
  13.5 1.0 %copy-start = (bf16[128,512]{1,0:T(8,128)(2,1)S(1)}, bf16[128,512]{1,0:T(8,128)(2,1)}, u32[]{:S(2)}) copy-start(bf16[128,512]{1,0:T(8,128)(2,1)} %k0_ref.1) | copy-start | bytes 393220
  13.5 3.0 %copy-start.1 = (bf16[128,512]{1,0:T(8,128)(2,1)S(1)}, bf16[128,512]{1,0:T(8,128)(2,1)}, u32[]{:S(2)}) copy-start(bf16[128,512]{1,0:T(8,128)(2,1)} %v0_ref.1) | copy-start | bytes 393220
  13.5 3.1 %copy-start.8 = (f32[40,128]{1,0:T(8,128)S(1)}, f32[40,128]{1,0:T(8,128)}, u32[]{:S(2)}) copy-start(f32[40,128]{1,0:T(8,128)} %get-tuple-element.15.refs_0_) | copy-start | bytes 61444
  14.4 6.1 %collective-permute-start.3 = (bf16[256,128]{1,0:T(8,128)(2,1)S(1)}, bf16[256,128]{1,0:T(8,128)(2,1)S(1)}, u32[]{:S(2)}, u32[]{:S(2)}) collective-permute-start(bf16[256,128]{1,0:T(8,128)(2,1)S(1)} %add_select_fusion), channel_id=1, source_target_pairs={{0,2},{2,0},{4,6},{6,4},{8,10},{10,8},{12,14},{14,12},{1,3},{3,1},... | collective-permute-start | bytes 196616 | tf_op jit(solution)/shard_map/ppermute | solution.py:243
  14.5 12.3 %collective-permute-start.7 = (bf16[128,512]{1,0:T(8,128)(2,1)S(1)}, bf16[128,512]{1,0:T(8,128)(2,1)S(1)}, u32[]{:S(2)}, u32[]{:S(2)}) collective-permute-start(bf16[128,512]{1,0:T(8,128)(2,1)S(1)} %copy-done), channel_id=1, source_target_pairs={{0,2},{2,0},{4,6},{6,4},{8,10},{10,8},{12,14},{14,12},{1,3},{3,1},... | collective-permute-start | bytes 393224 | tf_op jit(solution)/shard_map/ppermute | solution.py:243
  16.5 10.3 %collective-permute-start.8 = (bf16[128,512]{1,0:T(8,128)(2,1)S(1)}, bf16[128,512]{1,0:T(8,128)(2,1)S(1)}, u32[]{:S(2)}, u32[]{:S(2)}) collective-permute-start(bf16[128,512]{1,0:T(8,128)(2,1)S(1)} %copy-done.1), channel_id=1, source_target_pairs={{0,2},{2,0},{4,6},{6,4},{8,10},{10,8},{12,14},{14,12},{1,3},{3,1},... | collective-permute-start | bytes 393224 | tf_op jit(solution)/shard_map/ppermute | solution.py:243
  16.6 5.7 %collective-permute-start.11 = (f32[40,128]{1,0:T(8,128)S(1)}, f32[40,128]{1,0:T(8,128)S(1)}, u32[]{:S(2)}, u32[]{:S(2)}) collective-permute-start(f32[40,128]{1,0:T(8,128)S(1)} %copy-done.8), channel_id=1, source_target_pairs={{0,12},{2,14},{4,8},{6,10},{8,4},{10,6},{12,0},{14,2},{1,13},{3,15... | collective-permute-start | bytes 61448 | tf_op jit(solution)/shard_map/ppermute | solution.py:243
  20.5 5.6 %collective-permute-start.10 = (f32[40,128]{1,0:T(8,128)S(1)}, f32[40,128]{1,0:T(8,128)S(1)}, u32[]{:S(2)}, u32[]{:S(2)}) collective-permute-start(f32[40,128]{1,0:T(8,128)S(1)} %copy-done.8), channel_id=1, source_target_pairs={{0,8},{2,10},{4,12},{6,14},{8,0},{10,2},{12,4},{14,6},{1,9},{3,11}... | collective-permute-start | bytes 61448 | tf_op jit(solution)/shard_map/ppermute | solution.py:243
  20.5 5.6 %collective-permute-start.9 = (f32[40,128]{1,0:T(8,128)S(1)}, f32[40,128]{1,0:T(8,128)S(1)}, u32[]{:S(2)}, u32[]{:S(2)}) collective-permute-start(f32[40,128]{1,0:T(8,128)S(1)} %copy-done.8), channel_id=1, source_target_pairs={{0,4},{2,6},{4,0},{6,2},{8,12},{10,14},{12,8},{14,10},{1,5},{3,7},... | collective-permute-start | bytes 61448 | tf_op jit(solution)/shard_map/ppermute | solution.py:243
  21.1 8.7 %copy-start.2 = (bf16[256,128]{1,0:T(8,128)(2,1)}, bf16[256,128]{1,0:T(8,128)(2,1)S(1)}, u32[]{:S(2)}) copy-start(bf16[256,128]{1,0:T(8,128)(2,1)S(1)} %broadcast_select_fusion.refs_0_) | copy-start | bytes 196612
  22.3 4.4 %copy-start.9 = (f32[40,128]{1,0:T(8,128)}, f32[40,128]{1,0:T(8,128)S(1)}, u32[]{:S(2)}) copy-start(f32[40,128]{1,0:T(8,128)S(1)} %collective-permute-done.11.refs_3_) | copy-start | bytes 61444
  22.3 19.7 %collective-permute-start.6 = (bf16[256,128]{1,0:T(8,128)(2,1)S(1)}, bf16[256,128]{1,0:T(8,128)(2,1)S(1)}, u32[]{:S(2)}, u32[]{:S(2)}) collective-permute-start(bf16[256,128]{1,0:T(8,128)(2,1)S(1)} %broadcast_select_fusion.refs_0_), channel_id=1, source_target_pairs={{0,12},{2,14},{4,8},{6,10},{8,4},{10,6},{12,0},{14,2},{1,13},{3,15... | collective-permute-start | bytes 196616 | tf_op jit(solution)/shard_map/ppermute | solution.py:243
  26.1 0.7 %copy-start.10 = (f32[40,128]{1,0:T(8,128)}, f32[40,128]{1,0:T(8,128)S(1)}, u32[]{:S(2)}) copy-start(f32[40,128]{1,0:T(8,128)S(1)} %collective-permute-done.10.refs_2_) | copy-start | bytes 61444
  26.1 15.9 %collective-permute-start.5 = (bf16[256,128]{1,0:T(8,128)(2,1)S(1)}, bf16[256,128]{1,0:T(8,128)(2,1)S(1)}, u32[]{:S(2)}, u32[]{:S(2)}) collective-permute-start(bf16[256,128]{1,0:T(8,128)(2,1)S(1)} %broadcast_select_fusion.refs_0_), channel_id=1, source_target_pairs={{0,8},{2,10},{4,12},{6,14},{8,0},{10,2},{12,4},{14,6},{1,9},{3,11}... | collective-permute-start | bytes 196616 | tf_op jit(solution)/shard_map/ppermute | solution.py:243
  26.1 0.7 %copy-start.11 = (f32[40,128]{1,0:T(8,128)}, f32[40,128]{1,0:T(8,128)S(1)}, u32[]{:S(2)}) copy-start(f32[40,128]{1,0:T(8,128)S(1)} %collective-permute-done.9.refs_1_) | copy-start | bytes 61444
  26.1 15.9 %collective-permute-start.4 = (bf16[256,128]{1,0:T(8,128)(2,1)S(1)}, bf16[256,128]{1,0:T(8,128)(2,1)S(1)}, u32[]{:S(2)}, u32[]{:S(2)}) collective-permute-start(bf16[256,128]{1,0:T(8,128)(2,1)S(1)} %broadcast_select_fusion.refs_0_), channel_id=1, source_target_pairs={{0,4},{2,6},{4,0},{6,2},{8,12},{10,14},{12,8},{14,10},{1,5},{3,7},... | collective-permute-start | bytes 196616 | tf_op jit(solution)/shard_map/ppermute | solution.py:243
  29.8 4.3 %collective-permute-start.12 = (f32[40,128]{1,0:T(8,128)}, f32[40,128]{1,0:T(8,128)S(1)}, u32[]{:S(2)}, u32[]{:S(2)}) collective-permute-start(f32[40,128]{1,0:T(8,128)} %get-tuple-element.17), channel_id=1, source_target_pairs={{0,4},{2,6},{4,0},{6,2},{8,12},{10,14},{12,8},{14,10},{1,5},{3,7},... | collective-permute-start | bytes 61448 | tf_op jit(solution)/shard_map/ppermute | solution.py:243
  31.3 6.3 %collective-permute-start.13 = (f32[40,128]{1,0:T(8,128)}, f32[40,128]{1,0:T(8,128)S(1)}, u32[]{:S(2)}, u32[]{:S(2)}) collective-permute-start(f32[40,128]{1,0:T(8,128)} %get-tuple-element.18), channel_id=1, source_target_pairs={{0,8},{2,10},{4,12},{6,14},{8,0},{10,2},{12,4},{14,6},{1,9},{3,11}... | collective-permute-start | bytes 61448 | tf_op jit(solution)/shard_map/ppermute | solution.py:243
  34.1 5.8 %copy-start.12 = (f32[40,128]{1,0:T(8,128)}, f32[40,128]{1,0:T(8,128)S(1)}, u32[]{:S(2)}) copy-start(f32[40,128]{1,0:T(8,128)S(1)} %collective-permute-done.12.refs_1_) | copy-start | bytes 61444
  34.1 5.8 %collective-permute-start.14 = (f32[40,128]{1,0:T(8,128)}, f32[40,128]{1,0:T(8,128)S(1)}, u32[]{:S(2)}, u32[]{:S(2)}) collective-permute-start(f32[40,128]{1,0:T(8,128)} %get-tuple-element.19), channel_id=1, source_target_pairs={{0,12},{2,14},{4,8},{6,10},{8,4},{10,6},{12,0},{14,2},{1,13},{3,15... | collective-permute-start | bytes 61448 | tf_op jit(solution)/shard_map/ppermute | solution.py:243
  37.5 2.4 %copy-start.13 = (f32[40,128]{1,0:T(8,128)}, f32[40,128]{1,0:T(8,128)S(1)}, u32[]{:S(2)}) copy-start(f32[40,128]{1,0:T(8,128)S(1)} %collective-permute-done.13.refs_2_) | copy-start | bytes 61444
  (6 other events, 3.9 us)

commit v2 on v1

--- a/solution.py
+++ b/solution.py
@@ -13,7 +13,14 @@
 LOG2E = 1.4426950408889634
 VMEM = pl.BlockSpec(memory_space=pltpu.VMEM)
 SMEM = pl.BlockSpec(memory_space=pltpu.SMEM)
+HBM = pl.BlockSpec(memory_space=pltpu.HBM)
+SPAN_ROWS = 16
+UNIT = 4
 NT = (((1,), (1,)), ((), ()))
+
+
+def in_hbm(x):
+    return pltpu.with_memory_space_constraint(x, pltpu.HBM)
 
 
 def dot_nt(a, b):
@@ -24,47 +31,98 @@
     return jnp.dot(a, b, preferred_element_type=jnp.float32)
 
 
-def prepare_kernel(span_ref, query_ref, key_ref, value_ref, message_ref, *piece_refs):
-    heads = query_ref.shape[1] // HEAD_SIZE
-    query = query_ref[...].astype(jnp.float32)
+def span_rows(start):
+    row = lax.broadcasted_iota(jnp.int32, (SPAN_ROWS, HEAD_SIZE), 0)
+    start = jnp.broadcast_to(start, (SPAN_ROWS, HEAD_SIZE))
+    digit = jnp.where(row < SPAN_ROWS // 2, start // HEAD_SIZE, start % HEAD_SIZE)
+    return digit.astype(jnp.float32).astype(jnp.bfloat16)
+
+
+def span_of(rows):
+    digits = rows.astype(jnp.float32)
+    return digits[0:1, :] * HEAD_SIZE + digits[SPAN_ROWS // 2 : SPAN_ROWS // 2 + 1, :]
+
+
+def prepare_kernel(span_ref, query_ref, key_ref, value_ref, *refs):
+    packet_refs, (row, keys, values, rows_ref, sems) = refs[:-5], refs[-5:]
+    block, heads = key_ref.shape[0], query_ref.shape[1] // HEAD_SIZE
+    copies = [
+        pltpu.make_async_copy(source, target, sems.at[i])
+        for i, (source, target) in enumerate(
+            ((query_ref, row), (key_ref, keys), (value_ref, values))
+        )
+    ]
+    for copy in copies:
+        copy.start()
+    copies.pop(0).wait()
+    query = row[...].astype(jnp.float32)
     for head in range(heads):
-        message_ref[head : head + 1, :] = query[:, head * HEAD_SIZE : (head + 1) * HEAD_SIZE]
-    start = span_ref[0].astype(jnp.float32)
-    message_ref[heads : heads + 8, :] = jnp.full((8, HEAD_SIZE), start, jnp.float32)
-    for index, piece_ref in enumerate(piece_refs):
+        rows_ref[head : head + 1, :] = query[:, head * HEAD_SIZE : (head + 1) * HEAD_SIZE]
+    query_rows = rows_ref[...].astype(jnp.bfloat16)
+    span = span_rows(span_ref[...])
+    for copy in copies:
+        copy.wait()
+    for index, packet_ref in enumerate(packet_refs):
         columns = slice(index * HEAD_SIZE, (index + 1) * HEAD_SIZE)
-        rows = key_ref.shape[0]
-        piece_ref[:rows, :] = key_ref[:, columns]
-        piece_ref[rows:, :] = value_ref[:, columns]
+        packet_ref[:block, :] = keys[:, columns]
+        packet_ref[block : 2 * block, :] = values[:, columns]
+        packet_ref[2 * block : 2 * block + heads, :] = query_rows
+        packet_ref[2 * block + heads :, :] = span
 
 
 def prepare(query_row, span, keys, values):
     heads = query_row.shape[1] // HEAD_SIZE
-    kv_count = keys.shape[1] // HEAD_SIZE
-    rows = keys.shape[0]
-    piece = jax.ShapeDtypeStruct((2 * rows, HEAD_SIZE), keys.dtype)
+    block, width = keys.shape
+    packet = pltpu.VMEM((2 * block + heads + SPAN_ROWS, HEAD_SIZE), keys.dtype)
+    pinned = [in_hbm(x) for x in (query_row, keys, values)]
     return pl.pallas_call(
         prepare_kernel,
-        out_shape=[jax.ShapeDtypeStruct((heads + 8, HEAD_SIZE), jnp.float32)] + [piece] * kv_count,
-        in_specs=[SMEM, VMEM, VMEM, VMEM],
-        out_specs=[VMEM] * (1 + kv_count),
+        out_shape=[packet] * (width // HEAD_SIZE),
+        in_specs=[VMEM, HBM, HBM, HBM],
+        out_specs=[VMEM] * (width // HEAD_SIZE),
+        scratch_shapes=[
+            pltpu.VMEM(query_row.shape, query_row.dtype),
+            pltpu.VMEM((block, width), keys.dtype),
+            pltpu.VMEM((block, width), keys.dtype),
+            pltpu.VMEM((heads, HEAD_SIZE), jnp.float32),
+            pltpu.SemaphoreType.DMA((3,)),
+        ],
+        compiler_params=pltpu.CompilerParams(vmem_limit_bytes=8 * 2**20),
         cost_estimate=pl.CostEstimate(flops=1000, bytes_accessed=600000, transcendentals=0),
         name="prepare",
-    )(span, query_row, keys, values)
-
-
-def partials_kernel(host_ref, k0_ref, v0_ref, k1_ref, v1_ref, *refs):
-    sources = len(refs) // 2
-    message_refs, out_refs = refs[:sources], refs[sources:]
+    )(span.reshape(1, 1), *pinned)
+
+
+def own_bias(doc_row):
+    block = doc_row.shape[1]
+    row = lax.broadcasted_iota(jnp.int32, (block, block), 0)
+    lane = lax.broadcasted_iota(jnp.int32, (block, block), 1)
+    along = jnp.broadcast_to(doc_row.astype(jnp.float32), (block, block))
+    return jnp.where((lane <= row) & (jnp.transpose(along) == along), 0.0, MASKED_SCORE)
+
+
+def partials_kernel(
+    host_ref, doc_ref, context_ref, k0_ref, v0_ref, k1_ref, v1_ref, *refs
+):
+    sources = (len(refs) - 3) // 2
+    packet_refs, out_refs = refs[:sources], refs[sources : 2 * sources]
+    staged_ref, bias_ref, sem = refs[-3:]
+    staging = pltpu.make_async_copy(context_ref, staged_ref, sem)
+    staging.start()
+    bias_ref[...] = own_bias(doc_ref[...])
     block = k0_ref.shape[0]
     kv_count = k0_ref.shape[1] // HEAD_SIZE
-    heads = message_refs[0].shape[0] - 8
+    heads = packet_refs[0].shape[0] - 2 * block - SPAN_ROWS
     per_kv = heads // kv_count
     rows = sources * heads
     host = host_ref[0]
-    queries = jnp.concatenate([ref[:heads, :] for ref in message_refs], 0).astype(jnp.bfloat16)
+    queries = jnp.concatenate([ref[2 * block : 2 * block + heads, :] for ref in packet_refs], 0)
     starts = jnp.concatenate(
-        [jnp.broadcast_to(ref[heads : heads + 1, :], (heads, HEAD_SIZE)) for ref in message_refs], 0
+        [
+            jnp.broadcast_to(span_of(ref[2 * block + heads :, :]), (heads, HEAD_SIZE))
+            for ref in packet_refs
+        ],
+        0,
     )
     row_kv = (lax.broadcasted_iota(jnp.int32, (rows, HEAD_SIZE), 0) % heads) // per_kv
     lanes = lax.broadcasted_iota(jnp.int32, (rows, block), 1)
@@ -108,18 +166,25 @@
         out_ref[heads : heads + 1, :] = peak_row[:, :HEAD_SIZE]
         out_ref[heads + 1 : heads + 2, :] = total_row[:, :HEAD_SIZE]
         out_ref[heads + 2 : heads + 8, :] = jnp.zeros((6, HEAD_SIZE), jnp.float32)
-
-
-def partials(host, k0, v0, k1, v1, messages):
-    shape = jax.ShapeDtypeStruct(messages[0].shape, jnp.float32)
+    staging.wait()
+
+
+def partials(host, docs, context_queries, k0, v0, k1, v1, packets):
+    block = k0.shape[0]
+    heads = packets[0].shape[0] - 2 * block - SPAN_ROWS
+    part = pltpu.VMEM((heads + 8, HEAD_SIZE), jnp.float32)
+    staged = pltpu.VMEM(context_queries.shape, context_queries.dtype)
+    bias = pltpu.VMEM((block, block), jnp.float32)
     return pl.pallas_call(
         partials_kernel,
-        out_shape=[shape] * len(messages),
-        in_specs=[SMEM] + [VMEM] * (4 + len(messages)),
-        out_specs=[VMEM] * len(messages),
+        out_shape=[part] * len(packets) + [staged, bias],
+        in_specs=[SMEM, VMEM, HBM] + [VMEM] * (4 + len(packets)),
+        out_specs=[VMEM] * (len(packets) + 2),
+        scratch_shapes=[pltpu.SemaphoreType.DMA],
+        compiler_params=pltpu.CompilerParams(vmem_limit_bytes=8 * 2**20),
         cost_estimate=pl.CostEstimate(flops=1000000, bytes_accessed=900000, transcendentals=40000),
         name="query_partials",
-    )(host, k0, v0, k1, v1, *messages)
+    )(host, docs.reshape(1, block), in_hbm(context_queries), k0, v0, k1, v1, *packets)
 
 
 def merge_kernel(*refs):
@@ -152,84 +217,102 @@
         out_shape=jax.ShapeDtypeStruct((1, heads * HEAD_SIZE), jnp.bfloat16),
         in_specs=[VMEM] * len(parts),
         out_specs=VMEM,
+        compiler_params=pltpu.CompilerParams(vmem_limit_bytes=8 * 2**20),
         cost_estimate=pl.CostEstimate(flops=100000, bytes_accessed=90000, transcendentals=1000),
         name="merge_answer",
     )(*parts)
 
 
-def context_kernel(
-    host_ref, column_ref, doc_ref, query_ref, key_ref, value_ref, *refs
-):
-    piece_refs, out_ref, bias_ref = refs[:-2], refs[-2], refs[-1]
-    step = pl.program_id(0)
+def context_kernel(host_ref, column_ref, bias_ref, query_ref, key_ref, value_ref, *refs):
+    piece_refs, out_ref, held, sems = refs[:-3], refs[-3], refs[-2], refs[-1]
     block = query_ref.shape[0]
-    heads = query_ref.shape[1] // HEAD_SIZE
+    group = held.shape[2] // HEAD_SIZE
     scale = FACTOR * LOG2E
-
-    @pl.when(step == 0)
-    def _():
-        row = lax.broadcasted_iota(jnp.int32, (block, block), 0)
-        lane = lax.broadcasted_iota(jnp.int32, (block, block), 1)
-        along = jnp.broadcast_to(doc_ref[...].astype(jnp.float32), (block, block))
-        visible = (lane <= row) & (jnp.transpose(along) == along)
-        bias_ref[...] = jnp.where(visible, 0.0, MASKED_SCORE)
-
-    anchor = piece_refs[0][...]
-    for index in range(1, len(piece_refs)):
-        anchor = jnp.where(step == index, piece_refs[index][...], anchor)
-    anchor_keys, anchor_values = anchor[:block, :], anchor[block:, :]
-    bias = bias_ref[...]
     front = jnp.where(host_ref[0] > 0, 0.0, MASKED_SCORE)
-    keys = key_ref[...]
-    values = jnp.concatenate([value_ref[...], anchor_values], 0)
-    values = jnp.concatenate([values, jnp.ones((2 * block, HEAD_SIZE), values.dtype)], 1)
-    for head in range(heads):
-        columns = slice(head * HEAD_SIZE, (head + 1) * HEAD_SIZE)
-        query = query_ref[:, columns]
-        own = dot_nt(query, keys) + bias
-        far = dot_nt(query, anchor_keys) + front
-        peak = jnp.max(jnp.maximum(own, far), -1, keepdims=True)
-        weights = jnp.concatenate(
+    bias = jnp.concatenate([bias_ref[...], jnp.full((block, block), front, jnp.float32)], 1)
+    bias = jnp.concatenate([bias] * UNIT, 0)
+    ones = jnp.ones((2 * block, HEAD_SIZE), jnp.bfloat16)
+
+    def lanes(index, width):
+        return pl.ds(pl.multiple_of((index ^ column_ref[0]) * width, HEAD_SIZE), width)
+
+    def score(index, head):
+        at = lanes(index, group * HEAD_SIZE)
+        query = jnp.concatenate(
             [
-                jnp.exp2((own - peak) * scale).astype(jnp.bfloat16),
-                jnp.exp2((far - peak) * scale).astype(jnp.bfloat16),
+                query_ref[:, pl.ds(at.start + (head + i) * HEAD_SIZE, HEAD_SIZE)]
+                for i in range(UNIT)
             ],
-            1,
-        )
-        sums = dot_nn(weights, values)
-        out_ref[:, columns] = (sums[:, :HEAD_SIZE] / sums[:, HEAD_SIZE:]).astype(out_ref.dtype)
-
-
-def context_attention(host, column, doc_row, queries, keys, values, pieces):
+            0,
+        )
+        keys = jnp.concatenate(
+            [key_ref[:, lanes(index, HEAD_SIZE)], piece_refs[index][:block, :]], 0
+        )
+        return dot_nt(query, keys)
+
+    def weigh(scores):
+        scores = scores + bias
+        peak = jnp.max(scores, -1, keepdims=True)
+        return jnp.exp2((scores - peak) * scale).astype(jnp.bfloat16)
+
+    def gather(index, weights):
+        values = jnp.concatenate(
+            [value_ref[:, lanes(index, HEAD_SIZE)], piece_refs[index][block : 2 * block, :]], 0
+        )
+        return dot_nn(weights, jnp.concatenate([values, ones], 1))
+
+    def finish(index, head, sums):
+        total = sums[:, HEAD_SIZE:]
+        inverse = pl.reciprocal(total, approx=True)
+        inverse = inverse * (2.0 - total * inverse)
+        out = (sums[:, :HEAD_SIZE] * inverse).astype(jnp.bfloat16)
+        for i in range(UNIT):
+            columns = slice((head + i) * HEAD_SIZE, (head + i + 1) * HEAD_SIZE)
+            held[index, :, columns] = out[i * block : (i + 1) * block, :]
+
+    units = [(k, g) for k in range(len(piece_refs)) for g in range(0, group, UNIT)]
+    scores, weights, sums, copies = {}, {}, {}, []
+    for step in range(len(units) + 3):
+        if step >= 3:
+            index, head = units[step - 3]
+            finish(index, head, sums.pop(step - 3))
+            if head + UNIT == group:
+                copies.append(
+                    pltpu.make_async_copy(
+                        held.at[index],
+                        out_ref.at[:, lanes(index, group * HEAD_SIZE)],
+                        sems.at[index],
+                    )
+                )
+                copies[-1].start()
+        if 2 <= step < len(units) + 2:
+            sums[step - 2] = gather(units[step - 2][0], weights.pop(step - 2))
+        if 1 <= step < len(units) + 1:
+            weights[step - 1] = weigh(scores.pop(step - 1))
+        if step < len(units):
+            scores[step] = score(*units[step])
+    for copy in copies:
+        copy.wait()
+
+
+def context_attention(host, column, bias, queries, keys, values, pieces):
     block, width = queries.shape
-    kv_count = keys.shape[1] // HEAD_SIZE
-    group = width // kv_count
-
-    def head_of(step, host_ref, column_ref):
-        return (0, step ^ column_ref[0])
-
-    whole = pl.BlockSpec(pieces[0].shape, lambda step, *_: (0, 0))
+    kv_count = len(pieces)
     return pl.pallas_call(
         context_kernel,
         out_shape=jax.ShapeDtypeStruct((block, width), queries.dtype),
-        grid_spec=pltpu.PrefetchScalarGridSpec(
-            num_scalar_prefetch=2,
-            grid=(kv_count,),
-            in_specs=[
-                pl.BlockSpec((1, block), lambda step, *_: (0, 0)),
-                pl.BlockSpec((block, group), head_of),
-                pl.BlockSpec((block, HEAD_SIZE), head_of),
-                pl.BlockSpec((block, HEAD_SIZE), head_of),
-            ]
-            + [whole] * len(pieces),
-            out_specs=pl.BlockSpec((block, group), head_of),
-            scratch_shapes=[pltpu.VMEM((block, block), jnp.float32)],
-        ),
+        in_specs=[SMEM, SMEM] + [VMEM] * (4 + kv_count),
+        out_specs=HBM,
+        scratch_shapes=[
+            pltpu.VMEM((kv_count, block, width // kv_count), queries.dtype),
+            pltpu.SemaphoreType.DMA((kv_count,)),
+        ],
+        compiler_params=pltpu.CompilerParams(vmem_limit_bytes=24 * 2**20),
         cost_estimate=pl.CostEstimate(
             flops=4 * block * 2 * block * width, bytes_accessed=2600000, transcendentals=1000000
         ),
         name="context_attention",
-    )(host, column, doc_row, queries, keys, values, *pieces)
+    )(host, column, bias, queries, keys, values, *pieces)
 
 
 def paired(context_queries, context_keys, context_values, doc_ids, query_token_rows, span_start):
@@ -242,24 +325,37 @@
     def swap(value, mask):
         return lax.ppermute(value, "hosts", [(i, i ^ mask) for i in range(host_count)])
 
-    message, *own_pieces = prepare(query_token_rows, span_start, context_keys, context_values)
+    packets = prepare(query_token_rows, span_start, context_keys, context_values)
     other_keys, other_values = swap(context_keys, 1), swap(context_values, 1)
-    messages = [message] + [swap(message, 2 * k) for k in range(1, depth)]
-    sent = [lax.ppermute(own_pieces[k], "hosts", [(0, 2 * k)]) for k in range(1, depth)]
-    piece = jnp.where(place == 0, own_pieces[0], functools.reduce(jnp.add, sent))
-    piece = jnp.where(side == 0, piece, swap(piece, 1))
+    packets = [packets[0]] + [swap(packets[k], 2 * k) for k in range(1, depth)]
+    other_keys, other_values, *packets = lax.optimization_barrier(
+        (other_keys, other_values, *packets)
+    )
+    piece = packets[0][: 2 * block]
+    for k in range(1, depth):
+        piece = jnp.where(place == k, packets[k][: 2 * block], piece)
+    crossed = swap(piece, 1)
+    host_word = host.reshape(1).astype(jnp.int32)
+    *parts, staged, bias = partials(
+        host_word,
+        doc_ids,
+        context_queries,
+        context_keys,
+        context_values,
+        other_keys,
+        other_values,
+        packets,
+    )
+    crossed, *parts = lax.optimization_barrier((crossed, *parts))
+    parts = [parts[0]] + [swap(parts[k], 2 * k) for k in range(1, depth)]
+    piece = jnp.where(side == 0, piece, crossed)
     pieces = [piece] + [swap(piece, 2 * k) for k in range(1, depth)]
-    host_word = host.reshape(1).astype(jnp.int32)
-    parts = partials(
-        host_word, context_keys, context_values, other_keys, other_values, messages
-    )
-    parts = [parts[0]] + [swap(parts[k], 2 * k) for k in range(1, depth)]
     answer = merge(parts)
     block_out = context_attention(
         host_word,
         place.reshape(1).astype(jnp.int32),
-        doc_ids.reshape(1, block),
-        context_queries,
+        bias,
+        staged,
         context_keys,
         context_values,
         pieces,
@@ -333,7 +429,7 @@
     block_out = context_attention(
         host.reshape(1).astype(jnp.int32),
         jnp.zeros((1,), jnp.int32),
-        doc_ids.reshape(1, block),
+        own_bias(doc_ids.reshape(1, block)),
         context_queries,
         context_keys,
         context_values,

time: 53.4 us -> 37.9 us (0.71)
  Pallas kernels: 15.9 us -> 5.31 us
  starting transfers between devices: 27 us -> 18.3 us
  waiting for transfers between devices: 5.83 us -> 12 us
  local copies, waits for them, and re-layouts: 1.93 us -> 0.66 us
  other arithmetic: 0.91 us -> 0.04 us
    ppermute x12, waiting for transfers between devices: 3.65 us -> 12 us  [swap(): lax.ppermute(value, 'hosts', [(i, i ^ mask) for i in range(host_count)])]
    ppermute x3 -> x0, starting transfers between devices: 8.27 us -> none  [paired(): lax.ppermute(own_pieces[k], 'hosts', [(0, 2 * k)])]
    pallas_call x1, Pallas kernels: 10.4 us -> 2.28 us  [context_attention(): pl.pallas_call(context_kernel, out_shape=jax.ShapeDtypeStruct((block, wid...]
    ppermute x3 -> x0, waiting for transfers between devices: 2.18 us -> none  [paired(): lax.ppermute(own_pieces[k], 'hosts', [(0, 2 * k)])]
    pallas_call x2, Pallas kernels: 4.05 us -> 2.29 us  [the longest x1 1.23 us: partials(): pl.pallas_call(partials_kernel, out_shape=[part] * len(packets) + [staged...]
    unnamed x30 -> x6, local copies, waits for them, and re-layouts: 1.93 us -> 0.66 us
    select_n x2, other arithmetic: 0.91 us -> 0.04 us  [the longest x1 0.03 us: paired(): piece = jnp.where(place == k, packets[k][:2 * block], piece)]
    pallas_call x1, Pallas kernels: 1.52 us -> 0.74 us  [merge(): pl.pallas_call(merge_kernel, out_shape=jax.ShapeDtypeStruct((1, heads * H...]
  transfers between devices with their start and end apart: 15 -> 12, of which waited for: 4 -> 5; matrix products, arithmetic and copies ran while one was open for 0% -> 0% of each run, Pallas kernels for 7% -> 8%
where the time goes in v2:
time: 37.9 us; the launch traced here: 37.7 us
  starting transfers between devices  18.3 us (48%)
  waiting for transfers between devices  12 us (32%)
  Pallas kernels  5.31 us (14%)
  between operations  1.33 us (4%)
  local copies, waits for them, and re-layouts  0.66 us (2%)
    ppermute x12, starting transfers between devices, swap(): lax.ppermute(value, 'hosts', [(i, i ^ mask) for i in range(host_count)])  18.3 us
    ppermute x12, waiting for transfers between devices, swap(): lax.ppermute(value, 'hosts', [(i, i ^ mask) for i in range(host_count)])  12 us
    pallas_call x1, Pallas kernels, context_attention(): pl.pallas_call(context_kernel, out_shape=jax.ShapeDtypeStruct((block, wid...  2.28 us
    pallas_call x1, Pallas kernels, partials(): pl.pallas_call(partials_kernel, out_shape=[part] * len(packets) + [staged...  1.23 us
    pallas_call x1, Pallas kernels, prepare(): pl.pallas_call(prepare_kernel, out_shape=[packet] * (width // HEAD_SIZE),...  1.06 us
  transfers between devices with their start and end apart: 12, of which 5 were waited for; matrix products, arithmetic and copies ran while one was open for 0% of the time, Pallas kernels for 8%

profile of v2, /device:TPU:0, one launch (start us, length us, event | category | flops | bytes accessed | tf_op | source)
XLA Modules:
  0.0 37.7 jit_solution(7411834319017411154)
XLA Ops:
  0.6 3.0 %collective-permute-start = (bf16[128,512]{1,0:T(8,128)(2,1)}, bf16[128,512]{1,0:T(8,128)(2,1)S(1)}, u32[]{:S(2)}, u32[]{:S(2)}) collective-permute-start(bf16[128,512]{1,0:T(8,128)(2,1)} %key_ref.3), channel_id=1, source_target_pairs={{0,2},{2,0},{4,6},{6,4},{8,10},{10,8},{12,14},{14,12},{1,3},{3,1},... | collective-permute-start | bytes 393224 | tf_op jit(solution)/shard_map/ppermute | solution.py:326
  3.6 0.1 collective-permute-start.1
  4.4 1.1 %prepare.1 = (bf16[304,128]{1,0:T(8,128)(2,1)S(1)}, bf16[304,128]{1,0:T(8,128)(2,1)S(1)}, bf16[304,128]{1,0:T(8,128)(2,1)S(1)}, bf16[304,128]{1,0:T(8,128)(2,1)S(1)}) custom-call(s32[1,1]{1,0:T(1,128)} %bitcast.4.span_ref, bf16[1,4096]{1,0:T(2,128)(2,1)} %query_ref.1, bf16[128,512]{1,0:T(8,128)(2,1)} %key_ref.3, bf16[128,512]{1,0:T(8,128)(2,1)} %value_ref.3), custom_call_target="tpu_custom_call" | custom-call | flops 1000 | bytes 600000 | tf_op jit(solution)/shard_map/prepare/pallas_call | solution.py:78
  5.4 2.1 %collective-permute-start.2 = (bf16[304,128]{1,0:T(8,128)(2,1)S(1)}, bf16[304,128]{1,0:T(8,128)(2,1)S(1)}, u32[]{:S(2)}, u32[]{:S(2)}) collective-permute-start(bf16[304,128]{1,0:T(8,128)(2,1)S(1)} %get-tuple-element.24), channel_id=1, source_target_pairs={{0,4},{2,6},{4,0},{6,2},{8,12},{10,14},{12,8},{14,10},{1,5},{3,7},... | collective-permute-start | bytes 233480 | tf_op jit(solution)/shard_map/ppermute | solution.py:326
  7.5 2.6 %collective-permute-start.3 = (bf16[304,128]{1,0:T(8,128)(2,1)S(1)}, bf16[304,128]{1,0:T(8,128)(2,1)S(1)}, u32[]{:S(2)}, u32[]{:S(2)}) collective-permute-start(bf16[304,128]{1,0:T(8,128)(2,1)S(1)} %get-tuple-element.25), channel_id=1, source_target_pairs={{0,8},{2,10},{4,12},{6,14},{8,0},{10,2},{12,4},{14,6},{1,9},{3,11}... | collective-permute-start | bytes 233480 | tf_op jit(solution)/shard_map/ppermute | solution.py:326
  10.1 0.0 collective-permute-start.4
  10.1 0.0 collective-permute-done.2.refs_1_
  10.1 4.9 %collective-permute-done.3.refs_2_ = bf16[304,128]{1,0:T(8,128)(2,1)S(1)} collective-permute-done((bf16[304,128]{1,0:T(8,128)(2,1)S(1)}, bf16[304,128]{1,0:T(8,128)(2,1)S(1)}, u32[]{:S(2)}, u32[]{:S(2)}) %collective-permute-start.3) | collective-permute-done | bytes 77856 | tf_op jit(solution)/shard_map/ppermute | solution.py:326
  15.0 1.4 %collective-permute-done.4.refs_3_ = bf16[304,128]{1,0:T(8,128)(2,1)S(1)} collective-permute-done((bf16[304,128]{1,0:T(8,128)(2,1)S(1)}, bf16[304,128]{1,0:T(8,128)(2,1)S(1)}, u32[]{:S(2)}, u32[]{:S(2)}) %collective-permute-start.4) | collective-permute-done | bytes 77856 | tf_op jit(solution)/shard_map/ppermute | solution.py:326
  16.4 0.0 copy-start.1
  16.5 1.6 %collective-permute-start.5 = (bf16[256,128]{1,0:T(8,128)(2,1)S(1)}, bf16[256,128]{1,0:T(8,128)(2,1)S(1)}, u32[]{:S(2)}, u32[]{:S(2)}) collective-permute-start(bf16[256,128]{1,0:T(8,128)(2,1)S(1)} %select_select_fusion), channel_id=1, source_target_pairs={{0,2},{2,0},{4,6},{6,4},{8,10},{10,8},{12,14},{14,12},{1,3},{3,1},... | collective-permute-start | bytes 196616 | tf_op jit(solution)/shard_map/ppermute | solution.py:326
  18.0 0.6 %copy-done.2 = s32[128]{0:T(128)S(1)} copy-done((s32[128]{0:T(128)S(1)}, s32[128]{0:T(128)}, u32[]{:S(2)}) %copy-start.2) | copy-done | bytes 536
  18.7 1.2 %query_partials.1 = (f32[40,128]{1,0:T(8,128)S(1)}, f32[40,128]{1,0:T(8,128)S(1)}, f32[40,128]{1,0:T(8,128)S(1)}, f32[40,128]{1,0:T(8,128)S(1)}, bf16[128,4096]{1,0:T(8,128)(2,1)S(1)}, /*index=5*/f32[128,128]{1,0:T(8,128)S(1)}) custom-call(s32[1]{0:T(128)} %bitcast.host_ref, s32[1,128]{1,0:T(1,128)S(1)} %bitcast.5, bf16[128,4096]{1,0:T(8,128)(2,1)} %context_ref.1, ...), custom_call_target="tpu_custom_call" | custom-call | flops 1000000 | bytes 900000 | tf_op jit(solution)/shard_map/query_partials/pallas_call | solution.py:178
  19.9 0.9 %collective-permute-done.5 = bf16[256,128]{1,0:T(8,128)(2,1)S(1)} collective-permute-done((bf16[256,128]{1,0:T(8,128)(2,1)S(1)}, bf16[256,128]{1,0:T(8,128)(2,1)S(1)}, u32[]{:S(2)}, u32[]{:S(2)}) %collective-permute-start.5) | collective-permute-done | bytes 65568 | tf_op jit(solution)/shard_map/ppermute | solution.py:326
  20.8 2.0 %collective-permute-start.8 = (bf16[256,128]{1,0:T(8,128)(2,1)S(1)}, bf16[256,128]{1,0:T(8,128)(2,1)S(1)}, u32[]{:S(2)}, u32[]{:S(2)}) collective-permute-start(bf16[256,128]{1,0:T(8,128)(2,1)S(1)} %broadcast_select_fusion.refs_0_), channel_id=1, source_target_pairs={{0,12},{2,14},{4,8},{6,10},{8,4},{10,6},{12,0},{14,2},{1,13},{3,15... | collective-permute-start | bytes 196616 | tf_op jit(solution)/shard_map/ppermute | solution.py:326
  22.8 0.4 collective-permute-start.7
  23.2 2.1 %collective-permute-start.6 = (bf16[256,128]{1,0:T(8,128)(2,1)S(1)}, bf16[256,128]{1,0:T(8,128)(2,1)S(1)}, u32[]{:S(2)}, u32[]{:S(2)}) collective-permute-start(bf16[256,128]{1,0:T(8,128)(2,1)S(1)} %broadcast_select_fusion.refs_0_), channel_id=1, source_target_pairs={{0,4},{2,6},{4,0},{6,2},{8,12},{10,14},{12,8},{14,10},{1,5},{3,7},... | collective-permute-start | bytes 196616 | tf_op jit(solution)/shard_map/ppermute | solution.py:326
  25.3 0.0 collective-permute-start.9
  25.3 2.5 %collective-permute-start.10 = (f32[40,128]{1,0:T(8,128)S(1)}, f32[40,128]{1,0:T(8,128)S(1)}, u32[]{:S(2)}, u32[]{:S(2)}) collective-permute-start(f32[40,128]{1,0:T(8,128)S(1)} %get-tuple-element.42), channel_id=1, source_target_pairs={{0,8},{2,10},{4,12},{6,14},{8,0},{10,2},{12,4},{14,6},{1,9},{3,11}... | collective-permute-start | bytes 61448 | tf_op jit(solution)/shard_map/ppermute | solution.py:326
  27.8 1.3 %collective-permute-done.9.refs_1_ = f32[40,128]{1,0:T(8,128)S(1)} collective-permute-done((f32[40,128]{1,0:T(8,128)S(1)}, f32[40,128]{1,0:T(8,128)S(1)}, u32[]{:S(2)}, u32[]{:S(2)}) %collective-permute-start.9) | collective-permute-done | bytes 20512 | tf_op jit(solution)/shard_map/ppermute | solution.py:326
  29.1 2.0 %collective-permute-start.11 = (f32[40,128]{1,0:T(8,128)S(1)}, f32[40,128]{1,0:T(8,128)S(1)}, u32[]{:S(2)}, u32[]{:S(2)}) collective-permute-start(f32[40,128]{1,0:T(8,128)S(1)} %get-tuple-element.43), channel_id=1, source_target_pairs={{0,12},{2,14},{4,8},{6,10},{8,4},{10,6},{12,0},{14,2},{1,13},{3,15... | collective-permute-start | bytes 61448 | tf_op jit(solution)/shard_map/ppermute | solution.py:326
  31.1 3.5 %collective-permute-done.11.refs_3_ = f32[40,128]{1,0:T(8,128)S(1)} collective-permute-done((f32[40,128]{1,0:T(8,128)S(1)}, f32[40,128]{1,0:T(8,128)S(1)}, u32[]{:S(2)}, u32[]{:S(2)}) %collective-permute-start.11) | collective-permute-done | bytes 20512 | tf_op jit(solution)/shard_map/ppermute | solution.py:326
  34.6 0.7 %merge_answer.1 = bf16[1,4096]{1,0:T(2,128)(2,1)} custom-call(f32[40,128]{1,0:T(8,128)S(1)} %get-tuple-element.40.refs_0_, f32[40,128]{1,0:T(8,128)S(1)} %collective-permute-done.9.refs_1_, f32[40,128]{1,0:T(8,128)S(1)} %collective-permute-done.10.refs_2_, f32[40,128]{1,0:T(8,128)S(1)} %collective-permute-done.11.refs_3_), custom_call_target="tpu_custom_call" | custom-call | flops 100000 | bytes 90000 | tf_op jit(solution)/shard_map/merge_answer/pallas_call | solution.py:215
  35.4 2.3 %context_attention.1 = bf16[128,4096]{1,0:T(8,128)(2,1)} custom-call(s32[1]{0:T(128)} %bitcast.host_ref, s32[1]{0:T(128)} %bitcast.1.column_ref, f32[128,128]{1,0:T(8,128)S(1)} %get-tuple-element.33.bias_ref, bf16[128,4096]{1,0:T(8,128)(2,1)S(1)} %get-tuple-element.34.query_ref, bf16[128,512]{1,0:T(8,128)(2,1)S(1)} %copy-done, ...), custom_call_target="tpu_custom_call" | custom-call | flops 536870912 | bytes 2600000 | tf_op jit(solution)/shard_map/context_attention/pallas_call | solution.py:301
  (12 shorter events, 0.1 us)
Async XLA Ops:
  0.6 15.8 %collective-permute-start = (bf16[128,512]{1,0:T(8,128)(2,1)}, bf16[128,512]{1,0:T(8,128)(2,1)S(1)}, u32[]{:S(2)}, u32[]{:S(2)}) collective-permute-start(bf16[128,512]{1,0:T(8,128)(2,1)} %key_ref.3), channel_id=1, source_target_pairs={{0,2},{2,0},{4,6},{6,4},{8,10},{10,8},{12,14},{14,12},{1,3},{3,1},... | collective-permute-start | bytes 393224 | tf_op jit(solution)/shard_map/ppermute | solution.py:326
  3.6 12.8 %collective-permute-start.1 = (bf16[128,512]{1,0:T(8,128)(2,1)}, bf16[128,512]{1,0:T(8,128)(2,1)S(1)}, u32[]{:S(2)}, u32[]{:S(2)}) collective-permute-start(bf16[128,512]{1,0:T(8,128)(2,1)} %value_ref.3), channel_id=1, source_target_pairs={{0,2},{2,0},{4,6},{6,4},{8,10},{10,8},{12,14},{14,12},{1,3},{3,1},... | collective-permute-start | bytes 393224 | tf_op jit(solution)/shard_map/ppermute | solution.py:326
  5.4 4.7 %collective-permute-start.2 = (bf16[304,128]{1,0:T(8,128)(2,1)S(1)}, bf16[304,128]{1,0:T(8,128)(2,1)S(1)}, u32[]{:S(2)}, u32[]{:S(2)}) collective-permute-start(bf16[304,128]{1,0:T(8,128)(2,1)S(1)} %get-tuple-element.24), channel_id=1, source_target_pairs={{0,4},{2,6},{4,0},{6,2},{8,12},{10,14},{12,8},{14,10},{1,5},{3,7},... | collective-permute-start | bytes 233480 | tf_op jit(solution)/shard_map/ppermute | solution.py:326
  7.5 7.5 %collective-permute-start.3 = (bf16[304,128]{1,0:T(8,128)(2,1)S(1)}, bf16[304,128]{1,0:T(8,128)(2,1)S(1)}, u32[]{:S(2)}, u32[]{:S(2)}) collective-permute-start(bf16[304,128]{1,0:T(8,128)(2,1)S(1)} %get-tuple-element.25), channel_id=1, source_target_pairs={{0,8},{2,10},{4,12},{6,14},{8,0},{10,2},{12,4},{14,6},{1,9},{3,11}... | collective-permute-start | bytes 233480 | tf_op jit(solution)/shard_map/ppermute | solution.py:326
  10.1 6.3 %collective-permute-start.4 = (bf16[304,128]{1,0:T(8,128)(2,1)S(1)}, bf16[304,128]{1,0:T(8,128)(2,1)S(1)}, u32[]{:S(2)}, u32[]{:S(2)}) collective-permute-start(bf16[304,128]{1,0:T(8,128)(2,1)S(1)} %get-tuple-element.26), channel_id=1, source_target_pairs={{0,12},{2,14},{4,8},{6,10},{8,4},{10,6},{12,0},{14,2},{1,13},{3,15... | collective-permute-start | bytes 233480 | tf_op jit(solution)/shard_map/ppermute | solution.py:326
  16.4 1.6 %copy-start = (bf16[128,512]{1,0:T(8,128)(2,1)S(1)}, bf16[128,512]{1,0:T(8,128)(2,1)}, u32[]{:S(2)}) copy-start(bf16[128,512]{1,0:T(8,128)(2,1)} %key_ref.3) | copy-start | bytes 393220
  16.4 1.6 %copy-start.1 = (bf16[128,512]{1,0:T(8,128)(2,1)S(1)}, bf16[128,512]{1,0:T(8,128)(2,1)}, u32[]{:S(2)}) copy-start(bf16[128,512]{1,0:T(8,128)(2,1)} %value_ref.3) | copy-start | bytes 393220
  16.5 4.3 %collective-permute-start.5 = (bf16[256,128]{1,0:T(8,128)(2,1)S(1)}, bf16[256,128]{1,0:T(8,128)(2,1)S(1)}, u32[]{:S(2)}, u32[]{:S(2)}) collective-permute-start(bf16[256,128]{1,0:T(8,128)(2,1)S(1)} %select_select_fusion), channel_id=1, source_target_pairs={{0,2},{2,0},{4,6},{6,4},{8,10},{10,8},{12,14},{14,12},{1,3},{3,1},... | collective-permute-start | bytes 196616 | tf_op jit(solution)/shard_map/ppermute | solution.py:326
  18.0 0.7 %copy-start.2 = (s32[128]{0:T(128)S(1)}, s32[128]{0:T(128)}, u32[]{:S(2)}) copy-start(s32[128]{0:T(128)} %param.9) | copy-start | bytes 1540
  20.8 14.6 %collective-permute-start.8 = (bf16[256,128]{1,0:T(8,128)(2,1)S(1)}, bf16[256,128]{1,0:T(8,128)(2,1)S(1)}, u32[]{:S(2)}, u32[]{:S(2)}) collective-permute-start(bf16[256,128]{1,0:T(8,128)(2,1)S(1)} %broadcast_select_fusion.refs_0_), channel_id=1, source_target_pairs={{0,12},{2,14},{4,8},{6,10},{8,4},{10,6},{12,0},{14,2},{1,13},{3,15... | collective-permute-start | bytes 196616 | tf_op jit(solution)/shard_map/ppermute | solution.py:326
  22.8 12.6 %collective-permute-start.7 = (bf16[256,128]{1,0:T(8,128)(2,1)S(1)}, bf16[256,128]{1,0:T(8,128)(2,1)S(1)}, u32[]{:S(2)}, u32[]{:S(2)}) collective-permute-start(bf16[256,128]{1,0:T(8,128)(2,1)S(1)} %broadcast_select_fusion.refs_0_), channel_id=1, source_target_pairs={{0,8},{2,10},{4,12},{6,14},{8,0},{10,2},{12,4},{14,6},{1,9},{3,11}... | collective-permute-start | bytes 196616 | tf_op jit(solution)/shard_map/ppermute | solution.py:326
  23.2 12.2 %collective-permute-start.6 = (bf16[256,128]{1,0:T(8,128)(2,1)S(1)}, bf16[256,128]{1,0:T(8,128)(2,1)S(1)}, u32[]{:S(2)}, u32[]{:S(2)}) collective-permute-start(bf16[256,128]{1,0:T(8,128)(2,1)S(1)} %broadcast_select_fusion.refs_0_), channel_id=1, source_target_pairs={{0,4},{2,6},{4,0},{6,2},{8,12},{10,14},{12,8},{14,10},{1,5},{3,7},... | collective-permute-start | bytes 196616 | tf_op jit(solution)/shard_map/ppermute | solution.py:326
  25.3 3.8 %collective-permute-start.9 = (f32[40,128]{1,0:T(8,128)S(1)}, f32[40,128]{1,0:T(8,128)S(1)}, u32[]{:S(2)}, u32[]{:S(2)}) collective-permute-start(f32[40,128]{1,0:T(8,128)S(1)} %get-tuple-element.41), channel_id=1, source_target_pairs={{0,4},{2,6},{4,0},{6,2},{8,12},{10,14},{12,8},{14,10},{1,5},{3,7},... | collective-permute-start | bytes 61448 | tf_op jit(solution)/shard_map/ppermute | solution.py:326
  25.3 5.8 %collective-permute-start.10 = (f32[40,128]{1,0:T(8,128)S(1)}, f32[40,128]{1,0:T(8,128)S(1)}, u32[]{:S(2)}, u32[]{:S(2)}) collective-permute-start(f32[40,128]{1,0:T(8,128)S(1)} %get-tuple-element.42), channel_id=1, source_target_pairs={{0,8},{2,10},{4,12},{6,14},{8,0},{10,2},{12,4},{14,6},{1,9},{3,11}... | collective-permute-start | bytes 61448 | tf_op jit(solution)/shard_map/ppermute | solution.py:326
  29.1 5.6 %collective-permute-start.11 = (f32[40,128]{1,0:T(8,128)S(1)}, f32[40,128]{1,0:T(8,128)S(1)}, u32[]{:S(2)}, u32[]{:S(2)}) collective-permute-start(f32[40,128]{1,0:T(8,128)S(1)} %get-tuple-element.43), channel_id=1, source_target_pairs={{0,12},{2,14},{4,8},{6,10},{8,4},{10,6},{12,0},{14,2},{1,13},{3,15... | collective-permute-start | bytes 61448 | tf_op jit(solution)/shard_map/ppermute | solution.py:326

commit v3 on v1

v3 whole, which is shorter than its diff:
```python
import functools

import jax
import jax.numpy as jnp
from jax import lax
from jax.experimental import pallas as pl
from jax.experimental.pallas import tpu as pltpu
from jax.sharding import PartitionSpec as P

HEAD_SIZE = 128
MASKED_SCORE = -1e30
FACTOR = float(HEAD_SIZE) ** -0.5
LOG2E = 1.4426950408889634
VMEM = pl.BlockSpec(memory_space=pltpu.VMEM)
SMEM = pl.BlockSpec(memory_space=pltpu.SMEM)
HBM = pl.BlockSpec(memory_space=pltpu.HBM)
SPAN_ROWS = 16
WORD_ROWS = 16
UNIT = 4
NT = (((1,), (1,)), ((), ()))


def in_hbm(x):
    return pltpu.with_memory_space_constraint(x, pltpu.HBM)


def dot_nt(a, b):
    return lax.dot_general(a, b, NT, preferred_element_type=jnp.float32)


def dot_nn(a, b):
    return jnp.dot(a, b, preferred_element_type=jnp.float32)


def span_rows(start):
    row = lax.broadcasted_iota(jnp.int32, (SPAN_ROWS, HEAD_SIZE), 0)
    start = jnp.broadcast_to(start, (SPAN_ROWS, HEAD_SIZE))
    digit = jnp.where(row < SPAN_ROWS // 2, start // HEAD_SIZE, start % HEAD_SIZE)
    return digit.astype(jnp.float32).astype(jnp.bfloat16)


def span_of(rows):
    digits = rows.astype(jnp.float32)
    return digits[0:1, :] * HEAD_SIZE + digits[SPAN_ROWS // 2 : SPAN_ROWS // 2 + 1, :]


def own_bias(doc_row):
    block = doc_row.shape[1]
    row = lax.broadcasted_iota(jnp.int32, (block, block), 0)
    lane = lax.broadcasted_iota(jnp.int32, (block, block), 1)
    along = jnp.broadcast_to(doc_row.astype(jnp.float32), (block, block))
    return jnp.where((lane <= row) & (jnp.transpose(along) == along), 0.0, MASKED_SCORE)


def prepare_kernel(span_ref, *refs):
    sources, (message_ref, bias_ref, *staged), scratch = refs[:5], refs[5:10], refs[10:]
    row, docs, rows_ref, sems = scratch
    heads = row.shape[1] // HEAD_SIZE
    copies = [
        pltpu.make_async_copy(source, target, sems.at[i])
        for i, (source, target) in enumerate(zip(sources, (row, docs, *staged)))
    ]
    for copy in copies:
        copy.start()
    copies[0].wait()
    query = row[...].astype(jnp.float32)
    for head in range(heads):
        rows_ref[head : head + 1, :] = query[:, head * HEAD_SIZE : (head + 1) * HEAD_SIZE]
    message_ref[:heads, :] = rows_ref[...].astype(jnp.bfloat16)
    message_ref[heads:, :] = span_rows(span_ref[...].reshape(1, 1))
    copies[1].wait()
    bias_ref[...] = own_bias(docs[...])
    for copy in copies[2:]:
        copy.wait()


def prepare(span, query_row, docs, keys, values, context_queries):
    heads = query_row.shape[1] // HEAD_SIZE
    block = keys.shape[0]
    staged = (keys, values, context_queries)
    out_shape = [
        pltpu.VMEM((heads + SPAN_ROWS, HEAD_SIZE), query_row.dtype),
        pltpu.VMEM((block, block), jnp.float32),
    ] + [pltpu.VMEM(x.shape, x.dtype) for x in staged]
    return pl.pallas_call(
        prepare_kernel,
        out_shape=out_shape,
        in_specs=[VMEM] + [HBM] * 5,
        out_specs=[VMEM] * len(out_shape),
        scratch_shapes=[
            pltpu.VMEM(query_row.shape, query_row.dtype),
            pltpu.VMEM((1, block), jnp.int32),
            pltpu.VMEM((heads, HEAD_SIZE), jnp.float32),
            pltpu.SemaphoreType.DMA((5,)),
        ],
        compiler_params=pltpu.CompilerParams(vmem_limit_bytes=8 * 2**20),
        cost_estimate=pl.CostEstimate(flops=1000, bytes_accessed=2600000, transcendentals=0),
        name="prepare",
    )(span, *[in_hbm(x) for x in (query_row, docs.reshape(1, block), *staged)])


def partials_kernel(host_ref, k0_ref, v0_ref, k1_ref, v1_ref, *refs):
    message_refs, out_refs = refs[:-2], refs[-2:]
    block = k0_ref.shape[0]
    kv_count = k0_ref.shape[1] // HEAD_SIZE
    heads = message_refs[0].shape[0] - SPAN_ROWS
    per_kv = heads // kv_count
    messages = [ref[...] for ref in message_refs]
    rows = len(messages) * heads
    host = host_ref[0]
    queries = jnp.concatenate([message[:heads] for message in messages], 0)
    starts = jnp.concatenate(
        [
            jnp.broadcast_to(span_of(message[heads:]), (heads, HEAD_SIZE))
            for message in messages
        ],
        0,
    )
    row_kv = (lax.broadcasted_iota(jnp.int32, (rows, HEAD_SIZE), 0) % heads) // per_kv
    lanes = lax.broadcasted_iota(jnp.int32, (rows, block), 1)

    def chosen(per_head):
        out = per_head[0]
        for index in range(1, kv_count):
            out = jnp.where(row_kv == index, per_head[index], out)
        return out

    scores, shown = [], []
    for key_ref, at in ((k0_ref, host), (k1_ref, host ^ 1)):
        scores.append(
            chosen(
                [
                    dot_nt(queries, key_ref[:, h * HEAD_SIZE : (h + 1) * HEAD_SIZE])
                    for h in range(kv_count)
                ]
            )
            * FACTOR
        )
        shown.append((lanes + at * block).astype(jnp.float32) >= starts)
    masked = [jnp.where(s, x, MASKED_SCORE) for s, x in zip(shown, scores)]
    peaks = [jnp.max(x, -1, keepdims=True) for x in masked]
    weights = [
        jnp.where(s, jnp.exp(x - p), 0.0) for s, x, p in zip(shown, masked, peaks)
    ]
    peak = jnp.maximum(peaks[0], peaks[1])
    scales = [jnp.exp(p - peak) for p in peaks]
    total, acc = 0.0, 0.0
    for weight, scale, value_ref in zip(weights, scales, (v0_ref, v1_ref)):
        total += scale * jnp.sum(weight, -1, keepdims=True)
        weight = weight.astype(jnp.bfloat16)
        acc += scale * chosen(
            [
                dot_nn(weight, value_ref[:, h * HEAD_SIZE : (h + 1) * HEAD_SIZE])
                for h in range(kv_count)
            ]
        )
    peak_row = jnp.transpose(jnp.broadcast_to(peak, (rows, rows)))[0:1, :]
    total_row = jnp.transpose(jnp.broadcast_to(total, (rows, rows)))[0:1, :]
    acc = acc.astype(jnp.bfloat16)
    row = lax.broadcasted_iota(jnp.int32, (WORD_ROWS, HEAD_SIZE), 0)
    words = jnp.zeros((WORD_ROWS, HEAD_SIZE), jnp.float32)
    for at, rest in ((0, peak_row), (3, total_row)):
        for digit in range(3):
            part = rest.astype(jnp.bfloat16).astype(jnp.float32)
            words = jnp.where(row == at + digit, part, words)
            rest = rest - part
    words = words.astype(jnp.bfloat16)
    size = message_refs[0].shape[0]
    for index in range(len(messages)):
        out_ref, at = out_refs[index // 2], index % 2 * size
        out_ref[at : at + heads, :] = acc[index * heads : (index + 1) * heads]
        out_ref[at + heads : at + size, :] = words


def partials(host, keys, values, other_keys, other_values, messages):
    rows, width = messages[0].shape
    part = pltpu.VMEM((2 * rows, width), messages[0].dtype)
    return pl.pallas_call(
        partials_kernel,
        out_shape=[part] * 2,
        in_specs=[SMEM] + [VMEM] * (4 + len(messages)),
        out_specs=[VMEM] * 2,
        compiler_params=pltpu.CompilerParams(vmem_limit_bytes=8 * 2**20),
        cost_estimate=pl.CostEstimate(flops=1000000, bytes_accessed=900000, transcendentals=40000),
        name="query_partials",
    )(host, keys, values, other_keys, other_values, *messages)


def merged_answer(parts):
    heads = parts[0][0].shape[0] - WORD_ROWS
    row = lax.broadcasted_iota(jnp.int32, (heads, HEAD_SIZE), 0)
    lane = lax.broadcasted_iota(jnp.int32, (heads, HEAD_SIZE), 1)
    peaks, totals, sums = [], [], []
    for part, index in parts:
        sums.append(part[:heads].astype(jnp.float32))
        words = part[heads:].astype(jnp.float32)
        for at, out in ((0, peaks), (3, totals)):
            word = words[at : at + 1, :] + words[at + 1 : at + 2, :] + words[at + 2 : at + 3, :]
            word = jnp.broadcast_to(word, (heads, HEAD_SIZE))
            picked = jnp.where(lane == row + index * heads, word, 0.0)
            out.append(jnp.sum(picked, -1, keepdims=True))
    peak = functools.reduce(jnp.maximum, peaks)
    scales = [jnp.exp(p - peak) for p in peaks]
    total = functools.reduce(jnp.add, [s * t for s, t in zip(scales, totals)])
    merged = functools.reduce(jnp.add, [s * a for s, a in zip(scales, sums)])
    return (merged / total).astype(parts[0][0].dtype)


def chosen_anchor(host_ref, held_ref, arrived_ref, at):
    columns = slice(at, at + HEAD_SIZE)
    odd = jnp.full((held_ref.shape[0], HEAD_SIZE), (host_ref[0] // 2) % 2, jnp.int32)
    return jnp.where(odd == 0, held_ref[:, columns], arrived_ref[:, columns])


def weights_kernel(host_ref, bias_ref, query_ref, key_ref, held_ref, arrived_ref, out_ref):
    block = query_ref.shape[0]
    kv_count = key_ref.shape[1] // HEAD_SIZE
    group = query_ref.shape[1] // key_ref.shape[1]
    scale = FACTOR * LOG2E
    front = jnp.where(host_ref[0] > 0, 0.0, MASKED_SCORE)
    bias = jnp.concatenate([bias_ref[...], jnp.full((block, block), front, jnp.float32)], 1)
    bias = jnp.concatenate([bias] * UNIT, 0)

    def score(first):
        at = first // group * HEAD_SIZE
        far = chosen_anchor(host_ref, held_ref, arrived_ref, at)
        keys = jnp.concatenate([key_ref[:, at : at + HEAD_SIZE], far], 0)
        query = jnp.concatenate(
            [
                query_ref[:, (first + i) * HEAD_SIZE : (first + i + 1) * HEAD_SIZE]
                for i in range(UNIT)
            ],
            0,
        )
        return dot_nt(query, keys)

    def weigh(first, scores):
        scores = scores + bias
        peak = jnp.max(scores, -1, keepdims=True)
        weights = jnp.exp2((scores - peak) * scale)
        out_ref[first * block : (first + UNIT) * block, :] = weights.astype(jnp.bfloat16)

    waiting = None
    for first in range(0, kv_count * group, UNIT):
        scores = score(first)
        if waiting is not None:
            weigh(*waiting)
        waiting = (first, scores)
    weigh(*waiting)


def context_weights(host, bias, queries, keys, held, arrived):
    block, width = queries.shape
    heads = width // HEAD_SIZE
    return pl.pallas_call(
        weights_kernel,
        out_shape=pltpu.VMEM((heads * block, 2 * block), queries.dtype),
        in_specs=[SMEM] + [VMEM] * 5,
        out_specs=VMEM,
        compiler_params=pltpu.CompilerParams(vmem_limit_bytes=16 * 2**20),
        cost_estimate=pl.CostEstimate(
            flops=4 * block * block * width,
            bytes_accessed=4000000,
            transcendentals=2 * heads * block * block,
        ),
        name="context_weights",
    )(host, bias, queries, keys, held, arrived)


def load_kernel(held_ref, kept_ref, back_ref, out_ref):
    block, kv_count = held_ref.shape[0], held_ref.shape[1] // HEAD_SIZE
    size = kept_ref.shape[0] // 2
    for head in range(kv_count):
        columns = slice(head * HEAD_SIZE, (head + 1) * HEAD_SIZE)
        out_ref[head * block : (head + 1) * block, :] = held_ref[:, columns]
    rest = kv_count * block
    out_ref[rest : rest + size, :] = kept_ref[size:, :]
    out_ref[rest + size :, :] = back_ref[size:, :]


def load(held, kept, back):
    rows = held.size // HEAD_SIZE + kept.shape[0]
    return pl.pallas_call(
        load_kernel,
        out_shape=pltpu.VMEM((rows, HEAD_SIZE), held.dtype),
        in_specs=[VMEM] * 3,
        out_specs=VMEM,
        compiler_params=pltpu.CompilerParams(vmem_limit_bytes=8 * 2**20),
        cost_estimate=pl.CostEstimate(flops=1000, bytes_accessed=300000, transcendentals=0),
        name="load",
    )(held, kept, back)


def sums_kernel(answers, host_ref, weight_ref, value_ref, held_ref, arrived_ref, *refs):
    part_refs, scratch = refs[: len(refs) - 4 - answers], refs[-3:]
    out_ref, *answer_refs = refs[len(part_refs) : -3]
    slabs, row, sems = scratch
    kv_count, block, slab = slabs.shape
    group = slab // HEAD_SIZE
    ones = jnp.ones((2 * block, HEAD_SIZE), jnp.bfloat16)
    copies, waiting = [], None
    for answer_ref in answer_refs:
        kept_ref, back_ref = part_refs
        size, rest = kept_ref.shape[0] // 2, kv_count * block
        answer = merged_answer(
            [
                (kept_ref[:size, :], 0),
                (arrived_ref[rest : rest + size, :], 1),
                (back_ref[:size, :], 2),
                (arrived_ref[rest + size :, :], 3),
            ]
        )
        for head in range(answer.shape[0]):
            row[:, head * HEAD_SIZE : (head + 1) * HEAD_SIZE] = answer[head : head + 1, :]
        copies.append(pltpu.make_async_copy(row, answer_ref, sems.at[kv_count]))
        copies[-1].start()

    odd = jnp.full((block, HEAD_SIZE), (host_ref[0] // 2) % 2, jnp.int32)

    def add(first):
        index = first // group
        rows = slice(index * block, (index + 1) * block)
        far = jnp.where(odd == 0, held_ref[rows, :], arrived_ref[rows, :])
        near = value_ref[:, index * HEAD_SIZE : (index + 1) * HEAD_SIZE]
        values = jnp.concatenate([near, far], 0)
        weights = weight_ref[first * block : (first + UNIT) * block, :]
        return dot_nn(weights, jnp.concatenate([values, ones], 1))

    def finish(first, sums):
        total = sums[:, HEAD_SIZE:]
        inverse = pl.reciprocal(total, approx=True)
        inverse = inverse * (2.0 - total * inverse)
        out = (sums[:, :HEAD_SIZE] * inverse).astype(jnp.bfloat16)
        index = first // group
        for i in range(UNIT):
            column = (first % group + i) * HEAD_SIZE
            slabs[index, :, column : column + HEAD_SIZE] = out[i * block : (i + 1) * block, :]
        if first % group + UNIT == group:
            copy = pltpu.make_async_copy(
                slabs.at[index], out_ref.at[:, pl.ds(index * slab, slab)], sems.at[index]
            )
            copy.start()
            copies.append(copy)

    for first in range(0, kv_count * group, UNIT):
        sums = add(first)
        if waiting is not None:
            finish(*waiting)
        waiting = (first, sums)
    finish(*waiting)
    for copy in copies:
        copy.wait()


def context_sums(host, weights, values, held, arrived, parts):
    block, kv_count = values.shape[0], values.shape[1] // HEAD_SIZE
    width = weights.shape[0] // block * HEAD_SIZE
    answers = 1 if parts else 0
    return pl.pallas_call(
        functools.partial(sums_kernel, answers),
        out_shape=[jax.ShapeDtypeStruct((block, width), values.dtype)]
        + [jax.ShapeDtypeStruct((1, width), values.dtype)] * answers,
        in_specs=[SMEM] + [VMEM] * (4 + len(parts)),
        out_specs=[HBM] * (1 + answers),
        scratch_shapes=[
            pltpu.VMEM((kv_count, block, width // kv_count), values.dtype),
            pltpu.VMEM((1, width), values.dtype),
            pltpu.SemaphoreType.DMA((kv_count + 1,)),
        ],
        compiler_params=pltpu.CompilerParams(vmem_limit_bytes=16 * 2**20),
        cost_estimate=pl.CostEstimate(
            flops=4 * block * block * width, bytes_accessed=4000000, transcendentals=0
        ),
        name="context_sums",
    )(host, weights, values, held, arrived, *parts)


def paired(context_queries, context_keys, context_values, doc_ids, query_token_rows, span_start):
    host_count = lax.axis_size("hosts")
    host = lax.axis_index("hosts")
    place, side = host // 2, host % 2

    def swap(value, mask):
        return lax.ppermute(value, "hosts", [(i, i ^ mask) for i in range(host_count)])

    def down(value):
        return lax.ppermute(value, "hosts", [(x, 4 + x) for x in (0, 1)])

    other_keys, other_values = swap(context_keys, 1), swap(context_values, 1)
    message, bias, keys, values, queries = prepare(
        span_start, query_token_rows, doc_ids, context_keys, context_values, context_queries
    )

    def descend(own, other):
        first = jnp.where(side == 0, own, other)
        return jnp.where(place == 2, down(first), first)

    messages = [message] + [swap(message, 2 * k) for k in (1, 2, 3)]
    held_keys = descend(keys, other_keys)
    arrived_keys = swap(held_keys, 2)
    host_word = host.reshape(1).astype(jnp.int32)
    kept, sent = partials(host_word, keys, values, other_keys, other_values, messages)
    back = swap(sent, 4)
    loaded = load(descend(values, other_values), kept, back)
    arrived = swap(loaded, 2)
    weights = context_weights(host_word, bias, queries, keys, held_keys, arrived_keys)
    return tuple(context_sums(host_word, weights, values, loaded, arrived, [kept, back]))


def from_root(value, axis, source):
    kept = jnp.where(lax.axis_index(axis) == source, value, 0).astype(value.dtype)
    return lax.psum(kept, axis)


def head_groups(matrix, kv_count):
    count_rows = matrix.shape[0]
    return matrix.reshape(
        count_rows, kv_count, matrix.shape[1] // (kv_count * HEAD_SIZE), HEAD_SIZE
    ).transpose(1, 0, 2, 3)


def kv_groups(matrix, kv_count):
    return matrix.reshape(matrix.shape[0], kv_count, HEAD_SIZE).transpose(1, 0, 2)


def query_partials(queries, key_rows, value_rows, visible):
    kv_count = key_rows.shape[1] // HEAD_SIZE

    def query_per_head(operands):
        query_part, key_part, value_part = operands
        scores = (
            jnp.einsum("qgd,sd->qgs", query_part, key_part, preferred_element_type=jnp.float32)
            * FACTOR
        )
        shown = visible[:, None, :]
        peak_score = jnp.max(jnp.where(shown, scores, MASKED_SCORE), -1)
        weights = jnp.where(shown, jnp.exp(scores - peak_score[..., None]), 0.0)
        totals = jnp.sum(weights, -1)
        partial_acc = jnp.einsum(
            "qgs,sd->qgd",
            weights.astype(jnp.bfloat16),
            value_part,
            preferred_element_type=jnp.float32,
        )
        return (peak_score, totals, partial_acc)

    peaks, totals, accums = lax.map(
        query_per_head,
        (
            head_groups(queries, kv_count),
            kv_groups(key_rows, kv_count),
            kv_groups(value_rows, kv_count),
        ),
    )
    query_count = queries.shape[0]
    peaks = peaks.transpose(1, 0, 2).reshape(query_count, -1)
    totals = totals.transpose(1, 0, 2).reshape(query_count, -1)
    accums = accums.transpose(1, 0, 2, 3).reshape(query_count, -1)
    return (peaks, totals, accums)


def gathered(context_queries, context_keys, context_values, doc_ids, query_token_rows, span_start):
    host = lax.axis_index("hosts")
    host_count = lax.axis_size("hosts")
    block = context_queries.shape[0]
    per_host = query_token_rows.shape[0]
    anchor = from_root(jnp.stack([context_keys, context_values]), "hosts", 0)
    weights = context_weights(
        host.reshape(1).astype(jnp.int32),
        own_bias(doc_ids.reshape(1, block)),
        context_queries,
        context_keys,
        anchor[0],
        anchor[0],
    )
    kv_count = context_keys.shape[1] // HEAD_SIZE
    by_head = anchor[1].reshape(block, kv_count, HEAD_SIZE).transpose(1, 0, 2)
    by_head = by_head.reshape(kv_count * block, HEAD_SIZE)
    (block_out,) = context_sums(
        host.reshape(1).astype(jnp.int32), weights, context_values, by_head, by_head, []
    )
    all_queries, all_spans = (
        lax.all_gather(query_token_rows, "hosts", axis=0, tiled=True),
        lax.all_gather(span_start, "hosts", axis=0, tiled=True),
    )
    key_positions = host * block + jnp.arange(block, dtype=jnp.int32)
    query_visible = key_positions[None, :] >= all_spans[:, None]
    peaks, totals, accums = query_partials(
        all_queries, context_keys, context_values, query_visible
    )
    received = [
        lax.all_to_all(x, "hosts", split_axis=0, concat_axis=0, tiled=True).reshape(
            host_count, per_host, -1
        )
        for x in (peaks, totals, accums)
    ]
    source_peaks, source_totals, source_accums = received
    overall = jnp.max(source_peaks, 0)
    scales = jnp.exp(source_peaks - overall[None])
    own_totals = jnp.sum(scales * source_totals, 0)
    own_accums = jnp.sum(jnp.repeat(scales, HEAD_SIZE, axis=2) * source_accums, 0)
    answer = (own_accums / jnp.repeat(own_totals, HEAD_SIZE, axis=1)).astype(jnp.bfloat16)
    return (block_out, answer)


def solution(mesh):
    rows = P(("groups", "hosts"), "tensor")
    words = P(("groups", "hosts"))

    def on_device(context_queries, context_keys, context_values, doc_ids, query_rows, span_start):
        kv_count = context_keys.shape[1] // HEAD_SIZE
        fits = mesh.shape["hosts"] == 2 * kv_count and kv_count == 4 and query_rows.shape[0] == 1
        plan = paired if fits else gathered
        return plan(
            context_queries, context_keys, context_values, doc_ids, query_rows, span_start
        )

    return jax.shard_map(
        on_device,
        mesh=mesh,
        in_specs=(rows, rows, rows, words, rows, words),
        out_specs=(rows, rows),
        check_vma=False,
    )
```

time: 53.4 us -> 28.7 us (0.54)
  starting transfers between devices: 27 us -> 13.1 us
  Pallas kernels: 15.9 us -> 4.53 us
  waiting for transfers between devices: 5.83 us -> 9.38 us
  local copies, waits for them, and re-layouts: 1.93 us -> 0 us
  other arithmetic: 0.91 us -> 0.06 us
    pallas_call x4 -> x5, Pallas kernels: 15.9 us -> 4.53 us  [the longest x1 1.47 us: context_sums(): pl.pallas_call(functools.partial(sums_kernel, answers), out_shape=[jax.Sh...]
    ppermute x12 -> x8, starting transfers between devices: 18.7 us -> 7.98 us  [swap(): lax.ppermute(value, 'hosts', [(i, i ^ mask) for i in range(host_count)])]
    ppermute x3 -> x2, starting transfers between devices: 8.27 us -> 5.12 us  [down(): return lax.ppermute(value, 'hosts', [(x, 4 + x) for x in (0, 1)])]
    ppermute x3 -> x2, waiting for transfers between devices: 2.18 us -> 4.4 us  [down(): return lax.ppermute(value, 'hosts', [(x, 4 + x) for x in (0, 1)])]
    unnamed x30 -> x0, local copies, waits for them, and re-layouts: 1.93 us -> none
    ppermute x12 -> x8, waiting for transfers between devices: 3.65 us -> 4.98 us  [swap(): lax.ppermute(value, 'hosts', [(i, i ^ mask) for i in range(host_count)])]
    select_n x2 -> x4, other arithmetic: 0.91 us -> 0.06 us  [the longest x2 0.03 us: descend(): first = jnp.where(side == 0, own, other)]
  transfers between devices with their start and end apart: 15 -> 10, of which waited for: 4 -> 6; matrix products, arithmetic and copies ran while one was open for 0% -> 0% of each run, Pallas kernels for 7% -> 11%
where the time goes in v3:
time: 28.7 us; the launch traced here: 28.5 us
  starting transfers between devices  13.1 us (46%)
  waiting for transfers between devices  9.38 us (33%)
  Pallas kernels  4.53 us (16%)
  between operations  1.39 us (5%)
    ppermute x8, starting transfers between devices, swap(): lax.ppermute(value, 'hosts', [(i, i ^ mask) for i in range(host_count)])  7.98 us
    ppermute x2, starting transfers between devices, down(): return lax.ppermute(value, 'hosts', [(x, 4 + x) for x in (0, 1)])  5.12 us
    ppermute x8, waiting for transfers between devices, swap(): lax.ppermute(value, 'hosts', [(i, i ^ mask) for i in range(host_count)])  4.98 us
    ppermute x2, waiting for transfers between devices, down(): return lax.ppermute(value, 'hosts', [(x, 4 + x) for x in (0, 1)])  4.4 us
    pallas_call x1, Pallas kernels, context_sums(): pl.pallas_call(functools.partial(sums_kernel, answers), out_shape=[jax.Sh...  1.47 us
    pallas_call x1, Pallas kernels, prepare(): pl.pallas_call(prepare_kernel, out_shape=out_shape, in_specs=[VMEM] + [HB...  1.44 us
    pallas_call x1, Pallas kernels, context_weights(): pl.pallas_call(weights_kernel, out_shape=pltpu.VMEM((heads * block, 2 * b...  1.02 us
  transfers between devices with their start and end apart: 10, of which 6 were waited for; matrix products, arithmetic and copies ran while one was open for 0% of the time, Pallas kernels for 11%

profile of v3, /device:TPU:0, one launch (start us, length us, event | category | flops | bytes accessed | tf_op | source)
XLA Modules:
  0.0 28.5 jit_solution(12299412333880577676)
XLA Ops:
  0.6 3.0 %collective-permute-start = (bf16[128,512]{1,0:T(8,128)(2,1)}, bf16[128,512]{1,0:T(8,128)(2,1)S(1)}, u32[]{:S(2)}, u32[]{:S(2)}) collective-permute-start(bf16[128,512]{1,0:T(8,128)(2,1)} %refs_2_.1), channel_id=1, source_target_pairs={{0,2},{2,0},{4,6},{6,4},{8,10},{10,8},{12,14},{14,12},{1,3},{3,1},... | collective-permute-start | bytes 393224 | tf_op jit(solution)/shard_map/ppermute | solution.py:384
  3.6 0.1 collective-permute-start.3
  4.4 1.4 %prepare.1 = (bf16[48,128]{1,0:T(8,128)(2,1)S(1)}, f32[128,128]{1,0:T(8,128)S(1)}, bf16[128,512]{1,0:T(8,128)(2,1)S(1)}, bf16[128,512]{1,0:T(8,128)(2,1)S(1)}, bf16[128,4096]{1,0:T(8,128)(2,1)S(1)}) custom-call(s32[1]{0:T(128)S(6)} %copy.8.span_ref, bf16[1,4096]{1,0:T(2,128)(2,1)} %refs_0_.1, s32[1,128]{1,0:T(1,128)} %bitcast.2, bf16[128,512]{1,0:T(8,128)(2,1)} %refs_2_.1, ...), custom_call_target="tpu_custom_call" | custom-call | flops 1000 | bytes 2600000 | tf_op jit(solution)/shard_map/prepare/pallas_call | solution.py:85
  5.8 2.1 %collective-permute-start.5 = (bf16[48,128]{1,0:T(8,128)(2,1)S(1)}, bf16[48,128]{1,0:T(8,128)(2,1)S(1)}, u32[]{:S(2)}, u32[]{:S(2)}) collective-permute-start(bf16[48,128]{1,0:T(8,128)(2,1)S(1)} %get-tuple-element.13.refs_0_), channel_id=1, source_target_pairs={{0,4},{2,6},{4,0},{6,2},{8,12},{10,14},{12,8},{14,10},{1,5},{3,7},... | collective-permute-start | bytes 36872 | tf_op jit(solution)/shard_map/ppermute | solution.py:384
  7.9 2.6 %collective-permute-start.6 = (bf16[48,128]{1,0:T(8,128)(2,1)S(1)}, bf16[48,128]{1,0:T(8,128)(2,1)S(1)}, u32[]{:S(2)}, u32[]{:S(2)}) collective-permute-start(bf16[48,128]{1,0:T(8,128)(2,1)S(1)} %get-tuple-element.13.refs_0_), channel_id=1, source_target_pairs={{0,8},{2,10},{4,12},{6,14},{8,0},{10,2},{12,4},{14,6},{1,9},{3,11}... | collective-permute-start | bytes 36872 | tf_op jit(solution)/shard_map/ppermute | solution.py:384
  10.5 0.0 collective-permute-start.7
  10.5 0.0 collective-permute-done.k1_ref
  10.5 3.8 %collective-permute-start.1 = (bf16[128,512]{1,0:T(8,128)(2,1)S(1)}, bf16[128,512]{1,0:T(8,128)(2,1)S(1)}, u32[]{:S(2)}, u32[]{:S(2)}) collective-permute-start(bf16[128,512]{1,0:T(8,128)(2,1)S(1)} %broadcast_select_fusion.1), channel_id=1, source_target_pairs={{0,8},{2,10},{1,9},{3,11},{16,24},{18,26},{17,25},{19,27}} | collective-permute-start | bytes 393224 | tf_op jit(solution)/shard_map/ppermute | solution.py:387
  14.4 0.0 collective-permute-done.3.v1_ref
  14.4 1.3 %collective-permute-start.4 = (bf16[128,512]{1,0:T(8,128)(2,1)S(1)}, bf16[128,512]{1,0:T(8,128)(2,1)S(1)}, u32[]{:S(2)}, u32[]{:S(2)}) collective-permute-start(bf16[128,512]{1,0:T(8,128)(2,1)S(1)} %broadcast_select_fusion), channel_id=1, source_target_pairs={{0,8},{2,10},{1,9},{3,11},{16,24},{18,26},{17,25},{19,27}} | collective-permute-start | bytes 393224 | tf_op jit(solution)/shard_map/ppermute | solution.py:387
  15.7 0.0 collective-permute-done.5.refs_1_
  15.7 0.0 collective-permute-done.6.refs_2_
  15.7 0.3 collective-permute-done.7.refs_3_
  16.0 0.6 %query_partials.1 = (bf16[96,128]{1,0:T(8,128)(2,1)S(1)}, bf16[96,128]{1,0:T(8,128)(2,1)S(1)}) custom-call(s32[1]{0:T(128)} %bitcast.host_ref, bf16[128,512]{1,0:T(8,128)(2,1)S(1)} %get-tuple-element.11.key_ref.k0_ref, bf16[128,512]{1,0:T(8,128)(2,1)S(1)} %get-tuple-element.12.v0_ref.value_ref, bf16[128,512]{1,0:T(8,128)(2,1)S(1)} %collective-permute-done.k1_ref, ...), custom_call_target="tpu_custom_call" | custom-call | flops 1000000 | bytes 900000 | tf_op jit(solution)/shard_map/query_partials/pallas_call | solution.py:178
  16.6 0.1 collective-permute-start.8
  16.6 1.7 %collective-permute-done.1 = bf16[128,512]{1,0:T(8,128)(2,1)S(1)} collective-permute-done((bf16[128,512]{1,0:T(8,128)(2,1)S(1)}, bf16[128,512]{1,0:T(8,128)(2,1)S(1)}, u32[]{:S(2)}, u32[]{:S(2)}) %collective-permute-start.1) | collective-permute-done | bytes 131104 | tf_op jit(solution)/shard_map/ppermute | solution.py:387
  18.3 0.1 collective-permute-start.2
  18.4 2.7 %collective-permute-done.4 = bf16[128,512]{1,0:T(8,128)(2,1)S(1)} collective-permute-done((bf16[128,512]{1,0:T(8,128)(2,1)S(1)}, bf16[128,512]{1,0:T(8,128)(2,1)S(1)}, u32[]{:S(2)}, u32[]{:S(2)}) %collective-permute-start.4) | collective-permute-done | bytes 131104 | tf_op jit(solution)/shard_map/ppermute | solution.py:387
  21.2 0.5 %collective-permute-done.8.back_ref.refs_1_ = bf16[96,128]{1,0:T(8,128)(2,1)S(1)} collective-permute-done((bf16[96,128]{1,0:T(8,128)(2,1)S(1)}, bf16[96,128]{1,0:T(8,128)(2,1)S(1)}, u32[]{:S(2)}, u32[]{:S(2)}) %collective-permute-start.8) | collective-permute-done | bytes 24608 | tf_op jit(solution)/shard_map/ppermute | solution.py:384
  21.7 0.1 collective-permute-start.9
  21.8 2.5 %collective-permute-done.2.arrived_ref = bf16[128,512]{1,0:T(8,128)(2,1)S(1)} collective-permute-done((bf16[128,512]{1,0:T(8,128)(2,1)S(1)}, bf16[128,512]{1,0:T(8,128)(2,1)S(1)}, u32[]{:S(2)}, u32[]{:S(2)}) %collective-permute-start.2) | collective-permute-done | bytes 131104 | tf_op jit(solution)/shard_map/ppermute | solution.py:384
  24.2 1.0 %context_weights.1.weight_ref = bf16[4096,256]{1,0:T(8,128)(2,1)S(1)} custom-call(s32[1]{0:T(128)} %bitcast.host_ref, f32[128,128]{1,0:T(8,128)S(1)} %get-tuple-element.9.bias_ref, bf16[128,4096]{1,0:T(8,128)(2,1)S(1)} %get-tuple-element.10.query_ref, bf16[128,512]{1,0:T(8,128)(2,1)S(1)} %get-tuple-element.11.key_ref.k0_ref, ...), custom_call_target="tpu_custom_call" | custom-call | flops 268435456 | bytes 4000000 | tf_op jit(solution)/shard_map/context_weights/pallas_call | solution.py:255
  25.3 1.7 %collective-permute-done.9.arrived_ref = bf16[608,128]{1,0:T(8,128)(2,1)S(1)} collective-permute-done((bf16[608,128]{1,0:T(8,128)(2,1)S(1)}, bf16[608,128]{1,0:T(8,128)(2,1)S(1)}, u32[]{:S(2)}, u32[]{:S(2)}) %collective-permute-start.9) | collective-permute-done | bytes 155680 | tf_op jit(solution)/shard_map/ppermute | solution.py:384
  27.0 1.5 %context_sums.1 = (bf16[128,4096]{1,0:T(8,128)(2,1)}, bf16[1,4096]{1,0:T(2,128)(2,1)}) custom-call(s32[1]{0:T(128)} %bitcast.host_ref, bf16[4096,256]{1,0:T(8,128)(2,1)S(1)} %context_weights.1.weight_ref, bf16[128,512]{1,0:T(8,128)(2,1)S(1)} %get-tuple-element.12.v0_ref.value_ref, bf16[608,128]{1,0:T(8,128)(2,1)S(1)} %load.1.held_ref, ...), custom_call_target="tpu_custom_call" | custom-call | flops 268435456 | bytes 4000000 | tf_op jit(solution)/shard_map/context_sums/pallas_call | solution.py:359
  (5 shorter events, 0.1 us)
Async XLA Ops:
  0.6 9.9 %collective-permute-start = (bf16[128,512]{1,0:T(8,128)(2,1)}, bf16[128,512]{1,0:T(8,128)(2,1)S(1)}, u32[]{:S(2)}, u32[]{:S(2)}) collective-permute-start(bf16[128,512]{1,0:T(8,128)(2,1)} %refs_2_.1), channel_id=1, source_target_pairs={{0,2},{2,0},{4,6},{6,4},{8,10},{10,8},{12,14},{14,12},{1,3},{3,1},... | collective-permute-start | bytes 393224 | tf_op jit(solution)/shard_map/ppermute | solution.py:384
  3.6 10.7 %collective-permute-start.3 = (bf16[128,512]{1,0:T(8,128)(2,1)}, bf16[128,512]{1,0:T(8,128)(2,1)S(1)}, u32[]{:S(2)}, u32[]{:S(2)}) collective-permute-start(bf16[128,512]{1,0:T(8,128)(2,1)} %refs_3_.1), channel_id=1, source_target_pairs={{0,2},{2,0},{4,6},{6,4},{8,10},{10,8},{12,14},{14,12},{1,3},{3,1},... | collective-permute-start | bytes 393224 | tf_op jit(solution)/shard_map/ppermute | solution.py:384
  5.8 9.9 %collective-permute-start.5 = (bf16[48,128]{1,0:T(8,128)(2,1)S(1)}, bf16[48,128]{1,0:T(8,128)(2,1)S(1)}, u32[]{:S(2)}, u32[]{:S(2)}) collective-permute-start(bf16[48,128]{1,0:T(8,128)(2,1)S(1)} %get-tuple-element.13.refs_0_), channel_id=1, source_target_pairs={{0,4},{2,6},{4,0},{6,2},{8,12},{10,14},{12,8},{14,10},{1,5},{3,7},... | collective-permute-start | bytes 36872 | tf_op jit(solution)/shard_map/ppermute | solution.py:384
  7.9 7.8 %collective-permute-start.6 = (bf16[48,128]{1,0:T(8,128)(2,1)S(1)}, bf16[48,128]{1,0:T(8,128)(2,1)S(1)}, u32[]{:S(2)}, u32[]{:S(2)}) collective-permute-start(bf16[48,128]{1,0:T(8,128)(2,1)S(1)} %get-tuple-element.13.refs_0_), channel_id=1, source_target_pairs={{0,8},{2,10},{4,12},{6,14},{8,0},{10,2},{12,4},{14,6},{1,9},{3,11}... | collective-permute-start | bytes 36872 | tf_op jit(solution)/shard_map/ppermute | solution.py:384
  10.5 5.5 %collective-permute-start.7 = (bf16[48,128]{1,0:T(8,128)(2,1)S(1)}, bf16[48,128]{1,0:T(8,128)(2,1)S(1)}, u32[]{:S(2)}, u32[]{:S(2)}) collective-permute-start(bf16[48,128]{1,0:T(8,128)(2,1)S(1)} %get-tuple-element.13.refs_0_), channel_id=1, source_target_pairs={{0,12},{2,14},{4,8},{6,10},{8,4},{10,6},{12,0},{14,2},{1,13},{3,15... | collective-permute-start | bytes 36872 | tf_op jit(solution)/shard_map/ppermute | solution.py:384
  10.5 7.8 %collective-permute-start.1 = (bf16[128,512]{1,0:T(8,128)(2,1)S(1)}, bf16[128,512]{1,0:T(8,128)(2,1)S(1)}, u32[]{:S(2)}, u32[]{:S(2)}) collective-permute-start(bf16[128,512]{1,0:T(8,128)(2,1)S(1)} %broadcast_select_fusion.1), channel_id=1, source_target_pairs={{0,8},{2,10},{1,9},{3,11},{16,24},{18,26},{17,25},{19,27}} | collective-permute-start | bytes 393224 | tf_op jit(solution)/shard_map/ppermute | solution.py:387
  14.4 6.7 %collective-permute-start.4 = (bf16[128,512]{1,0:T(8,128)(2,1)S(1)}, bf16[128,512]{1,0:T(8,128)(2,1)S(1)}, u32[]{:S(2)}, u32[]{:S(2)}) collective-permute-start(bf16[128,512]{1,0:T(8,128)(2,1)S(1)} %broadcast_select_fusion), channel_id=1, source_target_pairs={{0,8},{2,10},{1,9},{3,11},{16,24},{18,26},{17,25},{19,27}} | collective-permute-start | bytes 393224 | tf_op jit(solution)/shard_map/ppermute | solution.py:387
  16.6 5.1 %collective-permute-start.8 = (bf16[96,128]{1,0:T(8,128)(2,1)S(1)}, bf16[96,128]{1,0:T(8,128)(2,1)S(1)}, u32[]{:S(2)}, u32[]{:S(2)}) collective-permute-start(bf16[96,128]{1,0:T(8,128)(2,1)S(1)} %get-tuple-element.15), channel_id=1, source_target_pairs={{0,8},{2,10},{4,12},{6,14},{8,0},{10,2},{12,4},{14,6},{1,9},{3,11}... | collective-permute-start | bytes 73736 | tf_op jit(solution)/shard_map/ppermute | solution.py:384
  18.3 5.9 %collective-permute-start.2 = (bf16[128,512]{1,0:T(8,128)(2,1)S(1)}, bf16[128,512]{1,0:T(8,128)(2,1)S(1)}, u32[]{:S(2)}, u32[]{:S(2)}) collective-permute-start(bf16[128,512]{1,0:T(8,128)(2,1)S(1)} %broadcast_select_fusion.3.held_ref), channel_id=1, source_target_pairs={{0,4},{2,6},{4,0},{6,2},{8,12},{10,14},{12,8},{14,10},{1,5},{3,7},... | collective-permute-start | bytes 393224 | tf_op jit(solution)/shard_map/ppermute | solution.py:384
  21.7 5.3 %collective-permute-start.9 = (bf16[608,128]{1,0:T(8,128)(2,1)S(1)}, bf16[608,128]{1,0:T(8,128)(2,1)S(1)}, u32[]{:S(2)}, u32[]{:S(2)}) collective-permute-start(bf16[608,128]{1,0:T(8,128)(2,1)S(1)} %load.1.held_ref), channel_id=1, source_target_pairs={{0,4},{2,6},{4,0},{6,2},{8,12},{10,14},{12,8},{14,10},{1,5},{3,7},... | collective-permute-start | bytes 466952 | tf_op jit(solution)/shard_map/ppermute | solution.py:384

commit v4 on v3

--- a/solution.py
+++ b/solution.py
@@ -53,12 +53,11 @@
 
 
 def prepare_kernel(span_ref, *refs):
-    sources, (message_ref, bias_ref, *staged), scratch = refs[:5], refs[5:10], refs[10:]
-    row, docs, rows_ref, sems = scratch
+    sources, (message_ref, *staged), (row, rows_ref, sems) = refs[:3], refs[3:6], refs[6:]
     heads = row.shape[1] // HEAD_SIZE
     copies = [
         pltpu.make_async_copy(source, target, sems.at[i])
-        for i, (source, target) in enumerate(zip(sources, (row, docs, *staged)))
+        for i, (source, target) in enumerate(zip(sources, (row, *staged)))
     ]
     for copy in copies:
         copy.start()
@@ -68,35 +67,57 @@
         rows_ref[head : head + 1, :] = query[:, head * HEAD_SIZE : (head + 1) * HEAD_SIZE]
     message_ref[:heads, :] = rows_ref[...].astype(jnp.bfloat16)
     message_ref[heads:, :] = span_rows(span_ref[...].reshape(1, 1))
-    copies[1].wait()
-    bias_ref[...] = own_bias(docs[...])
-    for copy in copies[2:]:
+    for copy in copies[1:]:
         copy.wait()
 
 
-def prepare(span, query_row, docs, keys, values, context_queries):
+def prepare(span, query_row, keys, values):
     heads = query_row.shape[1] // HEAD_SIZE
-    block = keys.shape[0]
-    staged = (keys, values, context_queries)
-    out_shape = [
-        pltpu.VMEM((heads + SPAN_ROWS, HEAD_SIZE), query_row.dtype),
-        pltpu.VMEM((block, block), jnp.float32),
-    ] + [pltpu.VMEM(x.shape, x.dtype) for x in staged]
+    out_shape = [pltpu.VMEM((heads + SPAN_ROWS, HEAD_SIZE), query_row.dtype)]
+    out_shape += [pltpu.VMEM(x.shape, x.dtype) for x in (keys, values)]
     return pl.pallas_call(
         prepare_kernel,
         out_shape=out_shape,
-        in_specs=[VMEM] + [HBM] * 5,
+        in_specs=[VMEM] + [HBM] * 3,
         out_specs=[VMEM] * len(out_shape),
         scratch_shapes=[
             pltpu.VMEM(query_row.shape, query_row.dtype),
-            pltpu.VMEM((1, block), jnp.int32),
             pltpu.VMEM((heads, HEAD_SIZE), jnp.float32),
-            pltpu.SemaphoreType.DMA((5,)),
+            pltpu.SemaphoreType.DMA((3,)),
         ],
         compiler_params=pltpu.CompilerParams(vmem_limit_bytes=8 * 2**20),
-        cost_estimate=pl.CostEstimate(flops=1000, bytes_accessed=2600000, transcendentals=0),
+        cost_estimate=pl.CostEstimate(flops=1000, bytes_accessed=600000, transcendentals=0),
         name="prepare",
-    )(span, *[in_hbm(x) for x in (query_row, docs.reshape(1, block), *staged)])
+    )(span, *[in_hbm(x) for x in (query_row, keys, values)])
+
+
+def stage_kernel(docs_ref, query_ref, bias_ref, staged_ref, docs, sems):
+    copies = [
+        pltpu.make_async_copy(docs_ref, docs, sems.at[0]),
+        pltpu.make_async_copy(query_ref, staged_ref, sems.at[1]),
+    ]
+    for copy in copies:
+        copy.start()
+    copies[0].wait()
+    bias_ref[...] = own_bias(docs[...])
+    copies[1].wait()
+
+
+def stage(docs, context_queries):
+    block = docs.shape[0]
+    return pl.pallas_call(
+        stage_kernel,
+        out_shape=[
+            pltpu.VMEM((block, block), jnp.float32),
+            pltpu.VMEM(context_queries.shape, context_queries.dtype),
+        ],
+        in_specs=[HBM] * 2,
+        out_specs=[VMEM] * 2,
+        scratch_shapes=[pltpu.VMEM((1, block), jnp.int32), pltpu.SemaphoreType.DMA((2,))],
+        compiler_params=pltpu.CompilerParams(vmem_limit_bytes=8 * 2**20),
+        cost_estimate=pl.CostEstimate(flops=1000, bytes_accessed=2100000, transcendentals=0),
+        name="stage",
+    )(in_hbm(docs.reshape(1, block)), in_hbm(context_queries))
 
 
 def partials_kernel(host_ref, k0_ref, v0_ref, k1_ref, v1_ref, *refs):
@@ -105,7 +126,7 @@
     kv_count = k0_ref.shape[1] // HEAD_SIZE
     heads = message_refs[0].shape[0] - SPAN_ROWS
     per_kv = heads // kv_count
-    messages = [ref[...] for ref in message_refs]
+    messages = [message_refs[i][...] for i in (0, 3, 2, 1)]
     rows = len(messages) * heads
     host = host_ref[0]
     queries = jnp.concatenate([message[:heads] for message in messages], 0)
@@ -384,18 +405,21 @@
         return lax.ppermute(value, "hosts", [(i, i ^ mask) for i in range(host_count)])
 
     def down(value):
-        return lax.ppermute(value, "hosts", [(x, 4 + x) for x in (0, 1)])
+        return lax.ppermute(
+            value, "hosts", [(i, i ^ (1 if i // 2 % 2 else 4)) for i in range(host_count)]
+        )
 
     other_keys, other_values = swap(context_keys, 1), swap(context_values, 1)
-    message, bias, keys, values, queries = prepare(
-        span_start, query_token_rows, doc_ids, context_keys, context_values, context_queries
-    )
+    message, keys, values = prepare(
+        span_start, query_token_rows, context_keys, context_values
+    )
+    bias, queries = stage(doc_ids, context_queries)
 
     def descend(own, other):
         first = jnp.where(side == 0, own, other)
         return jnp.where(place == 2, down(first), first)
 
-    messages = [message] + [swap(message, 2 * k) for k in (1, 2, 3)]
+    messages = [message] + [swap(message, 2 * k) for k in (3, 2, 1)]
     held_keys = descend(keys, other_keys)
     arrived_keys = swap(held_keys, 2)
     host_word = host.reshape(1).astype(jnp.int32)

time: 28.7 us -> 27.4 us (0.955)
  waiting for transfers between devices: 9.38 us -> 7.11 us
  Pallas kernels: 4.53 us -> 5.4 us
    ppermute x8, starting transfers between devices: 7.98 us -> 10.2 us  [swap(): lax.ppermute(value, 'hosts', [(i, i ^ mask) for i in range(host_count)])]
    ppermute x2, starting transfers between devices: 5.12 us -> 3.06 us  [down(): lax.ppermute(value, 'hosts', [(i, i ^ (1 if i // 2 % 2 else 4)) for i in...]
    ppermute x2, waiting for transfers between devices: 4.4 us -> 2.73 us  [down(): lax.ppermute(value, 'hosts', [(i, i ^ (1 if i // 2 % 2 else 4)) for i in...]
    pallas_call x0 -> x1, Pallas kernels: none -> 1.26 us  [stage(): pl.pallas_call(stage_kernel, out_shape=[pltpu.VMEM((block, block), jnp.fl...]
    ppermute x8, waiting for transfers between devices: 4.98 us -> 4.38 us  [swap(): lax.ppermute(value, 'hosts', [(i, i ^ mask) for i in range(host_count)])]
    pallas_call x1, Pallas kernels: 1.44 us -> 1.01 us  [prepare(): pl.pallas_call(prepare_kernel, out_shape=out_shape, in_specs=[VMEM] + [HB...]
  transfers between devices with their start and end apart: 10 -> 10, of which waited for: 6 -> 6; matrix products, arithmetic and copies ran while one was open for 0% -> 0% of each run, Pallas kernels for 11% -> 14%
where the time goes in v4:
time: 27.4 us; the launch traced here: 27.2 us
  starting transfers between devices  13.2 us (48%)
  waiting for transfers between devices  7.11 us (26%)
  Pallas kernels  5.4 us (20%)
  between operations  1.34 us (5%)
    ppermute x8, starting transfers between devices, swap(): lax.ppermute(value, 'hosts', [(i, i ^ mask) for i in range(host_count)])  10.2 us
    ppermute x8, waiting for transfers between devices, swap(): lax.ppermute(value, 'hosts', [(i, i ^ mask) for i in range(host_count)])  4.38 us
    ppermute x2, starting transfers between devices, down(): lax.ppermute(value, 'hosts', [(i, i ^ (1 if i // 2 % 2 else 4)) for i in...  3.06 us
    ppermute x2, waiting for transfers between devices, down(): lax.ppermute(value, 'hosts', [(i, i ^ (1 if i // 2 % 2 else 4)) for i in...  2.73 us
    pallas_call x1, Pallas kernels, context_sums(): pl.pallas_call(functools.partial(sums_kernel, answers), out_shape=[jax.Sh...  1.48 us
    pallas_call x1, Pallas kernels, stage(): pl.pallas_call(stage_kernel, out_shape=[pltpu.VMEM((block, block), jnp.fl...  1.26 us
    pallas_call x1, Pallas kernels, context_weights(): pl.pallas_call(weights_kernel, out_shape=pltpu.VMEM((heads * block, 2 * b...  1.06 us
    pallas_call x1, Pallas kernels, prepare(): pl.pallas_call(prepare_kernel, out_shape=out_shape, in_specs=[VMEM] + [HB...  1.01 us
  transfers between devices with their start and end apart: 10, of which 6 were waited for; matrix products, arithmetic and copies ran while one was open for 0% of the time, Pallas kernels for 14%

profile of v4, /device:TPU:0, one launch (start us, length us, event | category | flops | bytes accessed | tf_op | source)
XLA Modules:
  0.0 27.2 jit_solution(9065563409416488296)
XLA Ops:
  0.6 3.0 %collective-permute-start = (bf16[128,512]{1,0:T(8,128)(2,1)}, bf16[128,512]{1,0:T(8,128)(2,1)S(1)}, u32[]{:S(2)}, u32[]{:S(2)}) collective-permute-start(bf16[128,512]{1,0:T(8,128)(2,1)} %refs_1_.1), channel_id=1, source_target_pairs={{0,2},{2,0},{4,6},{6,4},{8,10},{10,8},{12,14},{14,12},{1,3},{3,1},... | collective-permute-start | bytes 393224 | tf_op jit(solution)/shard_map/ppermute | solution.py:405
  3.6 0.1 collective-permute-start.3
  4.4 1.0 %prepare.1 = (bf16[48,128]{1,0:T(8,128)(2,1)S(1)}, bf16[128,512]{1,0:T(8,128)(2,1)S(1)}, bf16[128,512]{1,0:T(8,128)(2,1)S(1)}) custom-call(s32[1]{0:T(128)S(6)} %copy.8.span_ref, bf16[1,4096]{1,0:T(2,128)(2,1)} %refs_0_.1, bf16[128,512]{1,0:T(8,128)(2,1)} %refs_1_.1, bf16[128,512]{1,0:T(8,128)(2,1)} %refs_2_.1), custom_call_target="tpu_custom_call" | custom-call | flops 1000 | bytes 600000 | tf_op jit(solution)/shard_map/prepare/pallas_call | solution.py:78
  5.4 4.1 %collective-permute-start.5 = (bf16[48,128]{1,0:T(8,128)(2,1)S(1)}, bf16[48,128]{1,0:T(8,128)(2,1)S(1)}, u32[]{:S(2)}, u32[]{:S(2)}) collective-permute-start(bf16[48,128]{1,0:T(8,128)(2,1)S(1)} %get-tuple-element.13.refs_0_), channel_id=1, source_target_pairs={{0,12},{2,14},{4,8},{6,10},{8,4},{10,6},{12,0},{14,2},{1,13},{3,15... | collective-permute-start | bytes 36872 | tf_op jit(solution)/shard_map/ppermute | solution.py:405
  9.5 0.0 collective-permute-start.6
  9.5 0.6 %collective-permute-start.7 = (bf16[48,128]{1,0:T(8,128)(2,1)S(1)}, bf16[48,128]{1,0:T(8,128)(2,1)S(1)}, u32[]{:S(2)}, u32[]{:S(2)}) collective-permute-start(bf16[48,128]{1,0:T(8,128)(2,1)S(1)} %get-tuple-element.13.refs_0_), channel_id=1, source_target_pairs={{0,4},{2,6},{4,0},{6,2},{8,12},{10,14},{12,8},{14,10},{1,5},{3,7},... | collective-permute-start | bytes 36872 | tf_op jit(solution)/shard_map/ppermute | solution.py:405
  10.2 0.0 collective-permute-done.k1_ref
  10.2 2.4 %collective-permute-start.1 = (bf16[128,512]{1,0:T(8,128)(2,1)S(1)}, bf16[128,512]{1,0:T(8,128)(2,1)S(1)}, u32[]{:S(2)}, u32[]{:S(2)}) collective-permute-start(bf16[128,512]{1,0:T(8,128)(2,1)S(1)} %broadcast_select_fusion.1), channel_id=1, source_target_pairs={{0,8},{2,10},{4,6},{6,4},{8,0},{10,2},{12,14},{14,12},{1,9},{3,11}... | collective-permute-start | bytes 393224 | tf_op jit(solution)/shard_map/ppermute | solution.py:408
  12.5 0.0 collective-permute-done.3.v1_ref
  12.5 0.7 %collective-permute-start.4 = (bf16[128,512]{1,0:T(8,128)(2,1)S(1)}, bf16[128,512]{1,0:T(8,128)(2,1)S(1)}, u32[]{:S(2)}, u32[]{:S(2)}) collective-permute-start(bf16[128,512]{1,0:T(8,128)(2,1)S(1)} %broadcast_select_fusion), channel_id=1, source_target_pairs={{0,8},{2,10},{4,6},{6,4},{8,0},{10,2},{12,14},{14,12},{1,9},{3,11}... | collective-permute-start | bytes 393224 | tf_op jit(solution)/shard_map/ppermute | solution.py:408
  13.3 0.9 %collective-permute-done.6.refs_2_ = bf16[48,128]{1,0:T(8,128)(2,1)S(1)} collective-permute-done((bf16[48,128]{1,0:T(8,128)(2,1)S(1)}, bf16[48,128]{1,0:T(8,128)(2,1)S(1)}, u32[]{:S(2)}, u32[]{:S(2)}) %collective-permute-start.6) | collective-permute-done | bytes 12320 | tf_op jit(solution)/shard_map/ppermute | solution.py:405
  14.1 0.0 collective-permute-done.7.refs_3_
  14.1 0.6 %query_partials.1 = (bf16[96,128]{1,0:T(8,128)(2,1)S(1)}, bf16[96,128]{1,0:T(8,128)(2,1)S(1)}) custom-call(s32[1]{0:T(128)} %bitcast.host_ref, bf16[128,512]{1,0:T(8,128)(2,1)S(1)} %get-tuple-element.11.key_ref.k0_ref, bf16[128,512]{1,0:T(8,128)(2,1)S(1)} %get-tuple-element.12.v0_ref.value_ref, bf16[128,512]{1,0:T(8,128)(2,1)S(1)} %collective-permute-done.k1_ref, ...), custom_call_target="tpu_custom_call" | custom-call | flops 1000000 | bytes 900000 | tf_op jit(solution)/shard_map/query_partials/pallas_call | solution.py:199
  14.7 2.1 %collective-permute-start.8 = (bf16[96,128]{1,0:T(8,128)(2,1)S(1)}, bf16[96,128]{1,0:T(8,128)(2,1)S(1)}, u32[]{:S(2)}, u32[]{:S(2)}) collective-permute-start(bf16[96,128]{1,0:T(8,128)(2,1)S(1)} %get-tuple-element.15), channel_id=1, source_target_pairs={{0,8},{2,10},{4,12},{6,14},{8,0},{10,2},{12,4},{14,6},{1,9},{3,11}... | collective-permute-start | bytes 73736 | tf_op jit(solution)/shard_map/ppermute | solution.py:405
  16.8 1.1 %collective-permute-done.1 = bf16[128,512]{1,0:T(8,128)(2,1)S(1)} collective-permute-done((bf16[128,512]{1,0:T(8,128)(2,1)S(1)}, bf16[128,512]{1,0:T(8,128)(2,1)S(1)}, u32[]{:S(2)}, u32[]{:S(2)}) %collective-permute-start.1) | collective-permute-done | bytes 131104 | tf_op jit(solution)/shard_map/ppermute | solution.py:408
  17.9 0.1 collective-permute-start.2
  18.0 1.6 %collective-permute-done.4 = bf16[128,512]{1,0:T(8,128)(2,1)S(1)} collective-permute-done((bf16[128,512]{1,0:T(8,128)(2,1)S(1)}, bf16[128,512]{1,0:T(8,128)(2,1)S(1)}, u32[]{:S(2)}, u32[]{:S(2)}) %collective-permute-start.4) | collective-permute-done | bytes 131104 | tf_op jit(solution)/shard_map/ppermute | solution.py:408
  19.6 0.2 collective-permute-done.8.back_ref.refs_1_
  19.9 0.2 collective-permute-start.9
  20.1 1.3 %stage.1 = (f32[128,128]{1,0:T(8,128)S(1)}, bf16[128,4096]{1,0:T(8,128)(2,1)S(1)}) custom-call(s32[1,128]{1,0:T(1,128)} %bitcast.2, bf16[128,4096]{1,0:T(8,128)(2,1)} %query_ref.1), custom_call_target="tpu_custom_call" | custom-call | flops 1000 | bytes 2100000 | tf_op jit(solution)/shard_map/stage/pallas_call | solution.py:108
  21.4 2.7 %collective-permute-done.2.arrived_ref = bf16[128,512]{1,0:T(8,128)(2,1)S(1)} collective-permute-done((bf16[128,512]{1,0:T(8,128)(2,1)S(1)}, bf16[128,512]{1,0:T(8,128)(2,1)S(1)}, u32[]{:S(2)}, u32[]{:S(2)}) %collective-permute-start.2) | collective-permute-done | bytes 131104 | tf_op jit(solution)/shard_map/ppermute | solution.py:405
  24.0 1.1 %context_weights.1.weight_ref = bf16[4096,256]{1,0:T(8,128)(2,1)S(1)} custom-call(s32[1]{0:T(128)} %bitcast.host_ref, f32[128,128]{1,0:T(8,128)S(1)} %get-tuple-element.9.bias_ref, bf16[128,4096]{1,0:T(8,128)(2,1)S(1)} %get-tuple-element.10.query_ref, bf16[128,512]{1,0:T(8,128)(2,1)S(1)} %get-tuple-element.11.key_ref.k0_ref, ...), custom_call_target="tpu_custom_call" | custom-call | flops 268435456 | bytes 4000000 | tf_op jit(solution)/shard_map/context_weights/pallas_call | solution.py:276
  25.1 0.6 %collective-permute-done.9.arrived_ref = bf16[608,128]{1,0:T(8,128)(2,1)S(1)} collective-permute-done((bf16[608,128]{1,0:T(8,128)(2,1)S(1)}, bf16[608,128]{1,0:T(8,128)(2,1)S(1)}, u32[]{:S(2)}, u32[]{:S(2)}) %collective-permute-start.9) | collective-permute-done | bytes 155680 | tf_op jit(solution)/shard_map/ppermute | solution.py:405
  25.7 1.5 %context_sums.1 = (bf16[128,4096]{1,0:T(8,128)(2,1)}, bf16[1,4096]{1,0:T(2,128)(2,1)}) custom-call(s32[1]{0:T(128)} %bitcast.host_ref, bf16[4096,256]{1,0:T(8,128)(2,1)S(1)} %context_weights.1.weight_ref, bf16[128,512]{1,0:T(8,128)(2,1)S(1)} %get-tuple-element.12.v0_ref.value_ref, bf16[608,128]{1,0:T(8,128)(2,1)S(1)} %load.1.held_ref, ...), custom_call_target="tpu_custom_call" | custom-call | flops 268435456 | bytes 4000000 | tf_op jit(solution)/shard_map/context_sums/pallas_call | solution.py:380
  (6 shorter events, 0.1 us)
Async XLA Ops:
  0.6 9.5 %collective-permute-start = (bf16[128,512]{1,0:T(8,128)(2,1)}, bf16[128,512]{1,0:T(8,128)(2,1)S(1)}, u32[]{:S(2)}, u32[]{:S(2)}) collective-permute-start(bf16[128,512]{1,0:T(8,128)(2,1)} %refs_1_.1), channel_id=1, source_target_pairs={{0,2},{2,0},{4,6},{6,4},{8,10},{10,8},{12,14},{14,12},{1,3},{3,1},... | collective-permute-start | bytes 393224 | tf_op jit(solution)/shard_map/ppermute | solution.py:405
  3.6 8.9 %collective-permute-start.3 = (bf16[128,512]{1,0:T(8,128)(2,1)}, bf16[128,512]{1,0:T(8,128)(2,1)S(1)}, u32[]{:S(2)}, u32[]{:S(2)}) collective-permute-start(bf16[128,512]{1,0:T(8,128)(2,1)} %refs_2_.1), channel_id=1, source_target_pairs={{0,2},{2,0},{4,6},{6,4},{8,10},{10,8},{12,14},{14,12},{1,3},{3,1},... | collective-permute-start | bytes 393224 | tf_op jit(solution)/shard_map/ppermute | solution.py:405
  5.4 7.9 %collective-permute-start.5 = (bf16[48,128]{1,0:T(8,128)(2,1)S(1)}, bf16[48,128]{1,0:T(8,128)(2,1)S(1)}, u32[]{:S(2)}, u32[]{:S(2)}) collective-permute-start(bf16[48,128]{1,0:T(8,128)(2,1)S(1)} %get-tuple-element.13.refs_0_), channel_id=1, source_target_pairs={{0,12},{2,14},{4,8},{6,10},{8,4},{10,6},{12,0},{14,2},{1,13},{3,15... | collective-permute-start | bytes 36872 | tf_op jit(solution)/shard_map/ppermute | solution.py:405
  9.5 4.6 %collective-permute-start.6 = (bf16[48,128]{1,0:T(8,128)(2,1)S(1)}, bf16[48,128]{1,0:T(8,128)(2,1)S(1)}, u32[]{:S(2)}, u32[]{:S(2)}) collective-permute-start(bf16[48,128]{1,0:T(8,128)(2,1)S(1)} %get-tuple-element.13.refs_0_), channel_id=1, source_target_pairs={{0,8},{2,10},{4,12},{6,14},{8,0},{10,2},{12,4},{14,6},{1,9},{3,11}... | collective-permute-start | bytes 36872 | tf_op jit(solution)/shard_map/ppermute | solution.py:405
  9.5 4.6 %collective-permute-start.7 = (bf16[48,128]{1,0:T(8,128)(2,1)S(1)}, bf16[48,128]{1,0:T(8,128)(2,1)S(1)}, u32[]{:S(2)}, u32[]{:S(2)}) collective-permute-start(bf16[48,128]{1,0:T(8,128)(2,1)S(1)} %get-tuple-element.13.refs_0_), channel_id=1, source_target_pairs={{0,4},{2,6},{4,0},{6,2},{8,12},{10,14},{12,8},{14,10},{1,5},{3,7},... | collective-permute-start | bytes 36872 | tf_op jit(solution)/shard_map/ppermute | solution.py:405
  10.2 7.7 %collective-permute-start.1 = (bf16[128,512]{1,0:T(8,128)(2,1)S(1)}, bf16[128,512]{1,0:T(8,128)(2,1)S(1)}, u32[]{:S(2)}, u32[]{:S(2)}) collective-permute-start(bf16[128,512]{1,0:T(8,128)(2,1)S(1)} %broadcast_select_fusion.1), channel_id=1, source_target_pairs={{0,8},{2,10},{4,6},{6,4},{8,0},{10,2},{12,14},{14,12},{1,9},{3,11}... | collective-permute-start | bytes 393224 | tf_op jit(solution)/shard_map/ppermute | solution.py:408
  12.5 7.1 %collective-permute-start.4 = (bf16[128,512]{1,0:T(8,128)(2,1)S(1)}, bf16[128,512]{1,0:T(8,128)(2,1)S(1)}, u32[]{:S(2)}, u32[]{:S(2)}) collective-permute-start(bf16[128,512]{1,0:T(8,128)(2,1)S(1)} %broadcast_select_fusion), channel_id=1, source_target_pairs={{0,8},{2,10},{4,6},{6,4},{8,0},{10,2},{12,14},{14,12},{1,9},{3,11}... | collective-permute-start | bytes 393224 | tf_op jit(solution)/shard_map/ppermute | solution.py:408
  14.7 5.2 %collective-permute-start.8 = (bf16[96,128]{1,0:T(8,128)(2,1)S(1)}, bf16[96,128]{1,0:T(8,128)(2,1)S(1)}, u32[]{:S(2)}, u32[]{:S(2)}) collective-permute-start(bf16[96,128]{1,0:T(8,128)(2,1)S(1)} %get-tuple-element.15), channel_id=1, source_target_pairs={{0,8},{2,10},{4,12},{6,14},{8,0},{10,2},{12,4},{14,6},{1,9},{3,11}... | collective-permute-start | bytes 73736 | tf_op jit(solution)/shard_map/ppermute | solution.py:405
  17.9 6.1 %collective-permute-start.2 = (bf16[128,512]{1,0:T(8,128)(2,1)S(1)}, bf16[128,512]{1,0:T(8,128)(2,1)S(1)}, u32[]{:S(2)}, u32[]{:S(2)}) collective-permute-start(bf16[128,512]{1,0:T(8,128)(2,1)S(1)} %broadcast_select_fusion.3.held_ref), channel_id=1, source_target_pairs={{0,4},{2,6},{4,0},{6,2},{8,12},{10,14},{12,8},{14,10},{1,5},{3,7},... | collective-permute-start | bytes 393224 | tf_op jit(solution)/shard_map/ppermute | solution.py:405
  19.9 5.8 %collective-permute-start.9 = (bf16[608,128]{1,0:T(8,128)(2,1)S(1)}, bf16[608,128]{1,0:T(8,128)(2,1)S(1)}, u32[]{:S(2)}, u32[]{:S(2)}) collective-permute-start(bf16[608,128]{1,0:T(8,128)(2,1)S(1)} %load.1.held_ref), channel_id=1, source_target_pairs={{0,4},{2,6},{4,0},{6,2},{8,12},{10,14},{12,8},{14,10},{1,5},{3,7},... | collective-permute-start | bytes 466952 | tf_op jit(solution)/shard_map/ppermute | solution.py:405

commit v5 on v4

--- a/solution.py
+++ b/solution.py
@@ -126,7 +126,7 @@
     kv_count = k0_ref.shape[1] // HEAD_SIZE
     heads = message_refs[0].shape[0] - SPAN_ROWS
     per_kv = heads // kv_count
-    messages = [message_refs[i][...] for i in (0, 3, 2, 1)]
+    messages = [message_refs[i][...] for i in (0, 3, 1, 2)]
     rows = len(messages) * heads
     host = host_ref[0]
     queries = jnp.concatenate([message[:heads] for message in messages], 0)
@@ -419,9 +419,11 @@
         first = jnp.where(side == 0, own, other)
         return jnp.where(place == 2, down(first), first)
 
-    messages = [message] + [swap(message, 2 * k) for k in (3, 2, 1)]
+    messages = [message] + [swap(message, 2 * k) for k in (2, 3, 1)]
     held_keys = descend(keys, other_keys)
-    arrived_keys = swap(held_keys, 2)
+    arrived_keys = lax.ppermute(
+        held_keys, "hosts", [(i, i ^ 2) for i in range(host_count) if i // 2 % 2 == 0]
+    )
     host_word = host.reshape(1).astype(jnp.int32)
     kept, sent = partials(host_word, keys, values, other_keys, other_values, messages)
     back = swap(sent, 4)

time: 27.4 us -> 27 us (0.985)
  waiting for transfers between devices: 7.11 us -> 5.55 us
  starting transfers between devices: 13.2 us -> 14.3 us
    ppermute x0 -> x1, starting transfers between devices: none -> 1.52 us  [paired(): lax.ppermute(held_keys, 'hosts', [(i, i ^ 2) for i in range(host_count) i...]
    ppermute x2, waiting for transfers between devices: 2.73 us -> 1.44 us  [down(): lax.ppermute(value, 'hosts', [(i, i ^ (1 if i // 2 % 2 else 4)) for i in...]
    ppermute x8 -> x7, waiting for transfers between devices: 4.38 us -> 3.2 us  [swap(): lax.ppermute(value, 'hosts', [(i, i ^ mask) for i in range(host_count)])]
    ppermute x0 -> x1, waiting for transfers between devices: none -> 0.91 us  [paired(): lax.ppermute(held_keys, 'hosts', [(i, i ^ 2) for i in range(host_count) i...]
    ppermute x8 -> x7, starting transfers between devices: 10.2 us -> 9.75 us  [swap(): lax.ppermute(value, 'hosts', [(i, i ^ mask) for i in range(host_count)])]
  transfers between devices with their start and end apart: 10 -> 10, of which waited for: 6 -> 7; matrix products, arithmetic and copies ran while one was open for 0% -> 0% of each run, Pallas kernels for 14% -> 15%
where the time goes in v5:
time: 27 us; the launch traced here: 26.7 us
  starting transfers between devices  14.3 us (53%)
  waiting for transfers between devices  5.55 us (21%)
  Pallas kernels  5.41 us (20%)
  between operations  1.35 us (5%)
    ppermute x7, starting transfers between devices, swap(): lax.ppermute(value, 'hosts', [(i, i ^ mask) for i in range(host_count)])  9.75 us
    ppermute x7, waiting for transfers between devices, swap(): lax.ppermute(value, 'hosts', [(i, i ^ mask) for i in range(host_count)])  3.2 us
    ppermute x2, starting transfers between devices, down(): lax.ppermute(value, 'hosts', [(i, i ^ (1 if i // 2 % 2 else 4)) for i in...  3.06 us
    ppermute x1, starting transfers between devices, paired(): lax.ppermute(held_keys, 'hosts', [(i, i ^ 2) for i in range(host_count) i...  1.52 us
    pallas_call x1, Pallas kernels, context_sums(): pl.pallas_call(functools.partial(sums_kernel, answers), out_shape=[jax.Sh...  1.48 us
    ppermute x2, waiting for transfers between devices, down(): lax.ppermute(value, 'hosts', [(i, i ^ (1 if i // 2 % 2 else 4)) for i in...  1.44 us
    pallas_call x1, Pallas kernels, stage(): pl.pallas_call(stage_kernel, out_shape=[pltpu.VMEM((block, block), jnp.fl...  1.26 us
    pallas_call x1, Pallas kernels, context_weights(): pl.pallas_call(weights_kernel, out_shape=pltpu.VMEM((heads * block, 2 * b...  1.07 us
  transfers between devices with their start and end apart: 10, of which 7 were waited for; matrix products, arithmetic and copies ran while one was open for 0% of the time, Pallas kernels for 15%

profile of v5, /device:TPU:0, one launch (start us, length us, event | category | flops | bytes accessed | tf_op | source)
XLA Modules:
  0.0 26.7 jit_solution(14410936860955403188)
XLA Ops:
  0.6 3.0 %collective-permute-start = (bf16[128,512]{1,0:T(8,128)(2,1)}, bf16[128,512]{1,0:T(8,128)(2,1)S(1)}, u32[]{:S(2)}, u32[]{:S(2)}) collective-permute-start(bf16[128,512]{1,0:T(8,128)(2,1)} %refs_1_.1), channel_id=1, source_target_pairs={{0,2},{2,0},{4,6},{6,4},{8,10},{10,8},{12,14},{14,12},{1,3},{3,1},... | collective-permute-start | bytes 393224 | tf_op jit(solution)/shard_map/ppermute | solution.py:405
  3.6 0.1 collective-permute-start.3
  4.4 1.0 %prepare.1 = (bf16[48,128]{1,0:T(8,128)(2,1)S(1)}, bf16[128,512]{1,0:T(8,128)(2,1)S(1)}, bf16[128,512]{1,0:T(8,128)(2,1)S(1)}) custom-call(s32[1]{0:T(128)S(6)} %copy.8.span_ref, bf16[1,4096]{1,0:T(2,128)(2,1)} %refs_0_.1, bf16[128,512]{1,0:T(8,128)(2,1)} %refs_1_.1, bf16[128,512]{1,0:T(8,128)(2,1)} %refs_2_.1), custom_call_target="tpu_custom_call" | custom-call | flops 1000 | bytes 600000 | tf_op jit(solution)/shard_map/prepare/pallas_call | solution.py:78
  5.4 3.1 %collective-permute-start.5 = (bf16[48,128]{1,0:T(8,128)(2,1)S(1)}, bf16[48,128]{1,0:T(8,128)(2,1)S(1)}, u32[]{:S(2)}, u32[]{:S(2)}) collective-permute-start(bf16[48,128]{1,0:T(8,128)(2,1)S(1)} %get-tuple-element.13.refs_0_), channel_id=1, source_target_pairs={{0,8},{2,10},{4,12},{6,14},{8,0},{10,2},{12,4},{14,6},{1,9},{3,11}... | collective-permute-start | bytes 36872 | tf_op jit(solution)/shard_map/ppermute | solution.py:405
  8.5 1.3 %collective-permute-start.6 = (bf16[48,128]{1,0:T(8,128)(2,1)S(1)}, bf16[48,128]{1,0:T(8,128)(2,1)S(1)}, u32[]{:S(2)}, u32[]{:S(2)}) collective-permute-start(bf16[48,128]{1,0:T(8,128)(2,1)S(1)} %get-tuple-element.13.refs_0_), channel_id=1, source_target_pairs={{0,12},{2,14},{4,8},{6,10},{8,4},{10,6},{12,0},{14,2},{1,13},{3,15... | collective-permute-start | bytes 36872 | tf_op jit(solution)/shard_map/ppermute | solution.py:405
  9.8 0.2 collective-permute-start.7
  10.1 0.0 collective-permute-done.k1_ref
  10.1 2.9 %collective-permute-start.1 = (bf16[128,512]{1,0:T(8,128)(2,1)S(1)}, bf16[128,512]{1,0:T(8,128)(2,1)S(1)}, u32[]{:S(2)}, u32[]{:S(2)}) collective-permute-start(bf16[128,512]{1,0:T(8,128)(2,1)S(1)} %broadcast_select_fusion.1), channel_id=1, source_target_pairs={{0,8},{2,10},{4,6},{6,4},{8,0},{10,2},{12,14},{14,12},{1,9},{3,11}... | collective-permute-start | bytes 393224 | tf_op jit(solution)/shard_map/ppermute | solution.py:408
  13.0 0.0 collective-permute-done.3.v1_ref
  13.0 0.2 collective-permute-start.4
  13.2 0.9 %collective-permute-done.6.refs_2_ = bf16[48,128]{1,0:T(8,128)(2,1)S(1)} collective-permute-done((bf16[48,128]{1,0:T(8,128)(2,1)S(1)}, bf16[48,128]{1,0:T(8,128)(2,1)S(1)}, u32[]{:S(2)}, u32[]{:S(2)}) %collective-permute-start.6) | collective-permute-done | bytes 12320 | tf_op jit(solution)/shard_map/ppermute | solution.py:405
  14.1 0.1 collective-permute-done.7.refs_3_
  14.2 0.6 %query_partials.1 = (bf16[96,128]{1,0:T(8,128)(2,1)S(1)}, bf16[96,128]{1,0:T(8,128)(2,1)S(1)}) custom-call(s32[1]{0:T(128)} %bitcast.host_ref, bf16[128,512]{1,0:T(8,128)(2,1)S(1)} %get-tuple-element.11.key_ref.k0_ref, bf16[128,512]{1,0:T(8,128)(2,1)S(1)} %get-tuple-element.12.v0_ref.value_ref, bf16[128,512]{1,0:T(8,128)(2,1)S(1)} %collective-permute-done.k1_ref, ...), custom_call_target="tpu_custom_call" | custom-call | flops 1000000 | bytes 900000 | tf_op jit(solution)/shard_map/query_partials/pallas_call | solution.py:199
  14.7 1.9 %collective-permute-start.8 = (bf16[96,128]{1,0:T(8,128)(2,1)S(1)}, bf16[96,128]{1,0:T(8,128)(2,1)S(1)}, u32[]{:S(2)}, u32[]{:S(2)}) collective-permute-start(bf16[96,128]{1,0:T(8,128)(2,1)S(1)} %get-tuple-element.15), channel_id=1, source_target_pairs={{0,8},{2,10},{4,12},{6,14},{8,0},{10,2},{12,4},{14,6},{1,9},{3,11}... | collective-permute-start | bytes 73736 | tf_op jit(solution)/shard_map/ppermute | solution.py:405
  16.6 1.0 %collective-permute-done.1 = bf16[128,512]{1,0:T(8,128)(2,1)S(1)} collective-permute-done((bf16[128,512]{1,0:T(8,128)(2,1)S(1)}, bf16[128,512]{1,0:T(8,128)(2,1)S(1)}, u32[]{:S(2)}, u32[]{:S(2)}) %collective-permute-start.1) | collective-permute-done | bytes 131104 | tf_op jit(solution)/shard_map/ppermute | solution.py:408
  17.6 1.5 %collective-permute-start.2 = (bf16[128,512]{1,0:T(8,128)(2,1)S(1)}, bf16[128,512]{1,0:T(8,128)(2,1)S(1)}, u32[]{:S(2)}, u32[]{:S(2)}) collective-permute-start(bf16[128,512]{1,0:T(8,128)(2,1)S(1)} %broadcast_select_fusion.3.held_ref), channel_id=1, source_target_pairs={{0,4},{2,6},{8,12},{10,14},{1,5},{3,7},{9,13},{11,15},{16,20},{18,... | collective-permute-start | bytes 393224 | tf_op jit(solution)/shard_map/ppermute | solution.py:424
  19.2 0.5 %collective-permute-done.4 = bf16[128,512]{1,0:T(8,128)(2,1)S(1)} collective-permute-done((bf16[128,512]{1,0:T(8,128)(2,1)S(1)}, bf16[128,512]{1,0:T(8,128)(2,1)S(1)}, u32[]{:S(2)}, u32[]{:S(2)}) %collective-permute-start.4) | collective-permute-done | bytes 131104 | tf_op jit(solution)/shard_map/ppermute | solution.py:408
  19.7 0.2 collective-permute-done.8.back_ref.refs_1_
  19.9 0.1 collective-permute-start.9
  20.0 1.3 %stage.1 = (f32[128,128]{1,0:T(8,128)S(1)}, bf16[128,4096]{1,0:T(8,128)(2,1)S(1)}) custom-call(s32[1,128]{1,0:T(1,128)} %bitcast.2, bf16[128,4096]{1,0:T(8,128)(2,1)} %query_ref.1), custom_call_target="tpu_custom_call" | custom-call | flops 1000 | bytes 2100000 | tf_op jit(solution)/shard_map/stage/pallas_call | solution.py:108
  21.3 0.9 %collective-permute-done.2.arrived_ref = bf16[128,512]{1,0:T(8,128)(2,1)S(1)} collective-permute-done((bf16[128,512]{1,0:T(8,128)(2,1)S(1)}, bf16[128,512]{1,0:T(8,128)(2,1)S(1)}, u32[]{:S(2)}, u32[]{:S(2)}) %collective-permute-start.2) | collective-permute-done | bytes 131104 | tf_op jit(solution)/shard_map/ppermute | solution.py:424
  22.2 1.1 %context_weights.1.weight_ref = bf16[4096,256]{1,0:T(8,128)(2,1)S(1)} custom-call(s32[1]{0:T(128)} %bitcast.host_ref, f32[128,128]{1,0:T(8,128)S(1)} %get-tuple-element.9.bias_ref, bf16[128,4096]{1,0:T(8,128)(2,1)S(1)} %get-tuple-element.10.query_ref, bf16[128,512]{1,0:T(8,128)(2,1)S(1)} %get-tuple-element.11.key_ref.k0_ref, ...), custom_call_target="tpu_custom_call" | custom-call | flops 268435456 | bytes 4000000 | tf_op jit(solution)/shard_map/context_weights/pallas_call | solution.py:276
  23.3 2.0 %collective-permute-done.9.arrived_ref = bf16[608,128]{1,0:T(8,128)(2,1)S(1)} collective-permute-done((bf16[608,128]{1,0:T(8,128)(2,1)S(1)}, bf16[608,128]{1,0:T(8,128)(2,1)S(1)}, u32[]{:S(2)}, u32[]{:S(2)}) %collective-permute-start.9) | collective-permute-done | bytes 155680 | tf_op jit(solution)/shard_map/ppermute | solution.py:405
  25.2 1.5 %context_sums.1 = (bf16[128,4096]{1,0:T(8,128)(2,1)}, bf16[1,4096]{1,0:T(2,128)(2,1)}) custom-call(s32[1]{0:T(128)} %bitcast.host_ref, bf16[4096,256]{1,0:T(8,128)(2,1)S(1)} %context_weights.1.weight_ref, bf16[128,512]{1,0:T(8,128)(2,1)S(1)} %get-tuple-element.12.v0_ref.value_ref, bf16[608,128]{1,0:T(8,128)(2,1)S(1)} %load.1.held_ref, ...), custom_call_target="tpu_custom_call" | custom-call | flops 268435456 | bytes 4000000 | tf_op jit(solution)/shard_map/context_sums/pallas_call | solution.py:380
  (6 shorter events, 0.1 us)
Async XLA Ops:
  0.6 9.4 %collective-permute-start = (bf16[128,512]{1,0:T(8,128)(2,1)}, bf16[128,512]{1,0:T(8,128)(2,1)S(1)}, u32[]{:S(2)}, u32[]{:S(2)}) collective-permute-start(bf16[128,512]{1,0:T(8,128)(2,1)} %refs_1_.1), channel_id=1, source_target_pairs={{0,2},{2,0},{4,6},{6,4},{8,10},{10,8},{12,14},{14,12},{1,3},{3,1},... | collective-permute-start | bytes 393224 | tf_op jit(solution)/shard_map/ppermute | solution.py:405
  3.6 9.3 %collective-permute-start.3 = (bf16[128,512]{1,0:T(8,128)(2,1)}, bf16[128,512]{1,0:T(8,128)(2,1)S(1)}, u32[]{:S(2)}, u32[]{:S(2)}) collective-permute-start(bf16[128,512]{1,0:T(8,128)(2,1)} %refs_2_.1), channel_id=1, source_target_pairs={{0,2},{2,0},{4,6},{6,4},{8,10},{10,8},{12,14},{14,12},{1,3},{3,1},... | collective-permute-start | bytes 393224 | tf_op jit(solution)/shard_map/ppermute | solution.py:405
  5.4 7.8 %collective-permute-start.5 = (bf16[48,128]{1,0:T(8,128)(2,1)S(1)}, bf16[48,128]{1,0:T(8,128)(2,1)S(1)}, u32[]{:S(2)}, u32[]{:S(2)}) collective-permute-start(bf16[48,128]{1,0:T(8,128)(2,1)S(1)} %get-tuple-element.13.refs_0_), channel_id=1, source_target_pairs={{0,8},{2,10},{4,12},{6,14},{8,0},{10,2},{12,4},{14,6},{1,9},{3,11}... | collective-permute-start | bytes 36872 | tf_op jit(solution)/shard_map/ppermute | solution.py:405
  8.5 5.6 %collective-permute-start.6 = (bf16[48,128]{1,0:T(8,128)(2,1)S(1)}, bf16[48,128]{1,0:T(8,128)(2,1)S(1)}, u32[]{:S(2)}, u32[]{:S(2)}) collective-permute-start(bf16[48,128]{1,0:T(8,128)(2,1)S(1)} %get-tuple-element.13.refs_0_), channel_id=1, source_target_pairs={{0,12},{2,14},{4,8},{6,10},{8,4},{10,6},{12,0},{14,2},{1,13},{3,15... | collective-permute-start | bytes 36872 | tf_op jit(solution)/shard_map/ppermute | solution.py:405
  9.8 4.3 %collective-permute-start.7 = (bf16[48,128]{1,0:T(8,128)(2,1)S(1)}, bf16[48,128]{1,0:T(8,128)(2,1)S(1)}, u32[]{:S(2)}, u32[]{:S(2)}) collective-permute-start(bf16[48,128]{1,0:T(8,128)(2,1)S(1)} %get-tuple-element.13.refs_0_), channel_id=1, source_target_pairs={{0,4},{2,6},{4,0},{6,2},{8,12},{10,14},{12,8},{14,10},{1,5},{3,7},... | collective-permute-start | bytes 36872 | tf_op jit(solution)/shard_map/ppermute | solution.py:405
  10.1 7.5 %collective-permute-start.1 = (bf16[128,512]{1,0:T(8,128)(2,1)S(1)}, bf16[128,512]{1,0:T(8,128)(2,1)S(1)}, u32[]{:S(2)}, u32[]{:S(2)}) collective-permute-start(bf16[128,512]{1,0:T(8,128)(2,1)S(1)} %broadcast_select_fusion.1), channel_id=1, source_target_pairs={{0,8},{2,10},{4,6},{6,4},{8,0},{10,2},{12,14},{14,12},{1,9},{3,11}... | collective-permute-start | bytes 393224 | tf_op jit(solution)/shard_map/ppermute | solution.py:408
  13.0 6.6 %collective-permute-start.4 = (bf16[128,512]{1,0:T(8,128)(2,1)S(1)}, bf16[128,512]{1,0:T(8,128)(2,1)S(1)}, u32[]{:S(2)}, u32[]{:S(2)}) collective-permute-start(bf16[128,512]{1,0:T(8,128)(2,1)S(1)} %broadcast_select_fusion), channel_id=1, source_target_pairs={{0,8},{2,10},{4,6},{6,4},{8,0},{10,2},{12,14},{14,12},{1,9},{3,11}... | collective-permute-start | bytes 393224 | tf_op jit(solution)/shard_map/ppermute | solution.py:408
  14.7 5.2 %collective-permute-start.8 = (bf16[96,128]{1,0:T(8,128)(2,1)S(1)}, bf16[96,128]{1,0:T(8,128)(2,1)S(1)}, u32[]{:S(2)}, u32[]{:S(2)}) collective-permute-start(bf16[96,128]{1,0:T(8,128)(2,1)S(1)} %get-tuple-element.15), channel_id=1, source_target_pairs={{0,8},{2,10},{4,12},{6,14},{8,0},{10,2},{12,4},{14,6},{1,9},{3,11}... | collective-permute-start | bytes 73736 | tf_op jit(solution)/shard_map/ppermute | solution.py:405
  17.6 4.5 %collective-permute-start.2 = (bf16[128,512]{1,0:T(8,128)(2,1)S(1)}, bf16[128,512]{1,0:T(8,128)(2,1)S(1)}, u32[]{:S(2)}, u32[]{:S(2)}) collective-permute-start(bf16[128,512]{1,0:T(8,128)(2,1)S(1)} %broadcast_select_fusion.3.held_ref), channel_id=1, source_target_pairs={{0,4},{2,6},{8,12},{10,14},{1,5},{3,7},{9,13},{11,15},{16,20},{18,... | collective-permute-start | bytes 393224 | tf_op jit(solution)/shard_map/ppermute | solution.py:424
  19.9 5.3 %collective-permute-start.9 = (bf16[608,128]{1,0:T(8,128)(2,1)S(1)}, bf16[608,128]{1,0:T(8,128)(2,1)S(1)}, u32[]{:S(2)}, u32[]{:S(2)}) collective-permute-start(bf16[608,128]{1,0:T(8,128)(2,1)S(1)} %load.1.held_ref), channel_id=1, source_target_pairs={{0,4},{2,6},{4,0},{6,2},{8,12},{10,14},{12,8},{14,10},{1,5},{3,7},... | collective-permute-start | bytes 466952 | tf_op jit(solution)/shard_map/ppermute | solution.py:405

commit v6 on v5

--- a/solution.py
+++ b/solution.py
@@ -126,7 +126,7 @@
     kv_count = k0_ref.shape[1] // HEAD_SIZE
     heads = message_refs[0].shape[0] - SPAN_ROWS
     per_kv = heads // kv_count
-    messages = [message_refs[i][...] for i in (0, 3, 1, 2)]
+    messages = [message_refs[i][...] for i in (0, 2, 3, 1)]
     rows = len(messages) * heads
     host = host_ref[0]
     queries = jnp.concatenate([message[:heads] for message in messages], 0)
@@ -419,7 +419,7 @@
         first = jnp.where(side == 0, own, other)
         return jnp.where(place == 2, down(first), first)
 
-    messages = [message] + [swap(message, 2 * k) for k in (2, 3, 1)]
+    messages = [message] + [swap(message, 2 * k) for k in (3, 1, 2)]
     held_keys = descend(keys, other_keys)
     arrived_keys = lax.ppermute(
         held_keys, "hosts", [(i, i ^ 2) for i in range(host_count) if i // 2 % 2 == 0]

time: 27 us -> 26.7 us (0.989)
  waiting for transfers between devices: 5.55 us -> 3.93 us
  starting transfers between devices: 14.3 us -> 15.7 us
    ppermute x7, starting transfers between devices: 9.75 us -> 11.3 us  [swap(): lax.ppermute(value, 'hosts', [(i, i ^ mask) for i in range(host_count)])]
    ppermute x7, waiting for transfers between devices: 3.2 us -> 2.07 us  [swap(): lax.ppermute(value, 'hosts', [(i, i ^ mask) for i in range(host_count)])]
    ppermute x1, waiting for transfers between devices: 0.91 us -> 0.01 us  [paired(): lax.ppermute(held_keys, 'hosts', [(i, i ^ 2) for i in range(host_count) i...]
    ppermute x2, waiting for transfers between devices: 1.44 us -> 1.85 us  [down(): lax.ppermute(value, 'hosts', [(i, i ^ (1 if i // 2 % 2 else 4)) for i in...]
  transfers between devices with their start and end apart: 10 -> 10, of which waited for: 7 -> 6; matrix products, arithmetic and copies ran while one was open for 0% -> 0% of each run, Pallas kernels for 15% -> 15%
where the time goes in v6:
time: 26.7 us; the launch traced here: 26.5 us
  starting transfers between devices  15.7 us (59%)
  Pallas kernels  5.41 us (20%)
  waiting for transfers between devices  3.93 us (15%)
  between operations  1.35 us (5%)
    ppermute x7, starting transfers between devices, swap(): lax.ppermute(value, 'hosts', [(i, i ^ mask) for i in range(host_count)])  11.3 us
    ppermute x2, starting transfers between devices, down(): lax.ppermute(value, 'hosts', [(i, i ^ (1 if i // 2 % 2 else 4)) for i in...  3.06 us
    ppermute x7, waiting for transfers between devices, swap(): lax.ppermute(value, 'hosts', [(i, i ^ mask) for i in range(host_count)])  2.07 us
    ppermute x2, waiting for transfers between devices, down(): lax.ppermute(value, 'hosts', [(i, i ^ (1 if i // 2 % 2 else 4)) for i in...  1.85 us
    pallas_call x1, Pallas kernels, context_sums(): pl.pallas_call(functools.partial(sums_kernel, answers), out_shape=[jax.Sh...  1.47 us
    ppermute x1, starting transfers between devices, paired(): lax.ppermute(held_keys, 'hosts', [(i, i ^ 2) for i in range(host_count) i...  1.33 us
    pallas_call x1, Pallas kernels, stage(): pl.pallas_call(stage_kernel, out_shape=[pltpu.VMEM((block, block), jnp.fl...  1.26 us
    pallas_call x1, Pallas kernels, context_weights(): pl.pallas_call(weights_kernel, out_shape=pltpu.VMEM((heads * block, 2 * b...  1.07 us
  transfers between devices with their start and end apart: 10, of which 6 were waited for; matrix products, arithmetic and copies ran while one was open for 0% of the time, Pallas kernels for 15%

profile of v6, /device:TPU:0, one launch (start us, length us, event | category | flops | bytes accessed | tf_op | source)
XLA Modules:
  0.0 26.5 jit_solution(12275740169650544296)
XLA Ops:
  0.6 3.0 %collective-permute-start = (bf16[128,512]{1,0:T(8,128)(2,1)}, bf16[128,512]{1,0:T(8,128)(2,1)S(1)}, u32[]{:S(2)}, u32[]{:S(2)}) collective-permute-start(bf16[128,512]{1,0:T(8,128)(2,1)} %refs_1_.1), channel_id=1, source_target_pairs={{0,2},{2,0},{4,6},{6,4},{8,10},{10,8},{12,14},{14,12},{1,3},{3,1},... | collective-permute-start | bytes 393224 | tf_op jit(solution)/shard_map/ppermute | solution.py:405
  3.6 0.1 collective-permute-start.3
  4.4 1.0 %prepare.1 = (bf16[48,128]{1,0:T(8,128)(2,1)S(1)}, bf16[128,512]{1,0:T(8,128)(2,1)S(1)}, bf16[128,512]{1,0:T(8,128)(2,1)S(1)}) custom-call(s32[1]{0:T(128)S(6)} %copy.8.span_ref, bf16[1,4096]{1,0:T(2,128)(2,1)} %refs_0_.1, bf16[128,512]{1,0:T(8,128)(2,1)} %refs_1_.1, bf16[128,512]{1,0:T(8,128)(2,1)} %refs_2_.1), custom_call_target="tpu_custom_call" | custom-call | flops 1000 | bytes 600000 | tf_op jit(solution)/shard_map/prepare/pallas_call | solution.py:78
  5.4 4.1 %collective-permute-start.5 = (bf16[48,128]{1,0:T(8,128)(2,1)S(1)}, bf16[48,128]{1,0:T(8,128)(2,1)S(1)}, u32[]{:S(2)}, u32[]{:S(2)}) collective-permute-start(bf16[48,128]{1,0:T(8,128)(2,1)S(1)} %get-tuple-element.13.refs_0_), channel_id=1, source_target_pairs={{0,12},{2,14},{4,8},{6,10},{8,4},{10,6},{12,0},{14,2},{1,13},{3,15... | collective-permute-start | bytes 36872 | tf_op jit(solution)/shard_map/ppermute | solution.py:405
  9.5 0.0 collective-permute-start.6
  9.5 0.6 %collective-permute-start.7 = (bf16[48,128]{1,0:T(8,128)(2,1)S(1)}, bf16[48,128]{1,0:T(8,128)(2,1)S(1)}, u32[]{:S(2)}, u32[]{:S(2)}) collective-permute-start(bf16[48,128]{1,0:T(8,128)(2,1)S(1)} %get-tuple-element.13.refs_0_), channel_id=1, source_target_pairs={{0,8},{2,10},{4,12},{6,14},{8,0},{10,2},{12,4},{14,6},{1,9},{3,11}... | collective-permute-start | bytes 36872 | tf_op jit(solution)/shard_map/ppermute | solution.py:405
  10.2 0.0 collective-permute-done.k1_ref
  10.2 2.4 %collective-permute-start.1 = (bf16[128,512]{1,0:T(8,128)(2,1)S(1)}, bf16[128,512]{1,0:T(8,128)(2,1)S(1)}, u32[]{:S(2)}, u32[]{:S(2)}) collective-permute-start(bf16[128,512]{1,0:T(8,128)(2,1)S(1)} %broadcast_select_fusion.1), channel_id=1, source_target_pairs={{0,8},{2,10},{4,6},{6,4},{8,0},{10,2},{12,14},{14,12},{1,9},{3,11}... | collective-permute-start | bytes 393224 | tf_op jit(solution)/shard_map/ppermute | solution.py:408
  12.5 0.0 collective-permute-done.3.v1_ref
  12.5 0.7 %collective-permute-start.4 = (bf16[128,512]{1,0:T(8,128)(2,1)S(1)}, bf16[128,512]{1,0:T(8,128)(2,1)S(1)}, u32[]{:S(2)}, u32[]{:S(2)}) collective-permute-start(bf16[128,512]{1,0:T(8,128)(2,1)S(1)} %broadcast_select_fusion), channel_id=1, source_target_pairs={{0,8},{2,10},{4,6},{6,4},{8,0},{10,2},{12,14},{14,12},{1,9},{3,11}... | collective-permute-start | bytes 393224 | tf_op jit(solution)/shard_map/ppermute | solution.py:408
  13.3 0.0 collective-permute-done.5.refs_1_
  13.3 0.2 collective-permute-done.6.refs_2_
  13.4 0.7 %collective-permute-done.7.refs_3_ = bf16[48,128]{1,0:T(8,128)(2,1)S(1)} collective-permute-done((bf16[48,128]{1,0:T(8,128)(2,1)S(1)}, bf16[48,128]{1,0:T(8,128)(2,1)S(1)}, u32[]{:S(2)}, u32[]{:S(2)}) %collective-permute-start.7) | collective-permute-done | bytes 12320 | tf_op jit(solution)/shard_map/ppermute | solution.py:405
  14.1 0.6 %query_partials.1 = (bf16[96,128]{1,0:T(8,128)(2,1)S(1)}, bf16[96,128]{1,0:T(8,128)(2,1)S(1)}) custom-call(s32[1]{0:T(128)} %bitcast.host_ref, bf16[128,512]{1,0:T(8,128)(2,1)S(1)} %get-tuple-element.11.key_ref.k0_ref, bf16[128,512]{1,0:T(8,128)(2,1)S(1)} %get-tuple-element.12.v0_ref.value_ref, bf16[128,512]{1,0:T(8,128)(2,1)S(1)} %collective-permute-done.k1_ref, ...), custom_call_target="tpu_custom_call" | custom-call | flops 1000000 | bytes 900000 | tf_op jit(solution)/shard_map/query_partials/pallas_call | solution.py:199
  14.7 1.5 %collective-permute-start.8 = (bf16[96,128]{1,0:T(8,128)(2,1)S(1)}, bf16[96,128]{1,0:T(8,128)(2,1)S(1)}, u32[]{:S(2)}, u32[]{:S(2)}) collective-permute-start(bf16[96,128]{1,0:T(8,128)(2,1)S(1)} %get-tuple-element.15), channel_id=1, source_target_pairs={{0,8},{2,10},{4,12},{6,14},{8,0},{10,2},{12,4},{14,6},{1,9},{3,11}... | collective-permute-start | bytes 73736 | tf_op jit(solution)/shard_map/ppermute | solution.py:405
  16.2 1.7 %collective-permute-done.1 = bf16[128,512]{1,0:T(8,128)(2,1)S(1)} collective-permute-done((bf16[128,512]{1,0:T(8,128)(2,1)S(1)}, bf16[128,512]{1,0:T(8,128)(2,1)S(1)}, u32[]{:S(2)}, u32[]{:S(2)}) %collective-permute-start.1) | collective-permute-done | bytes 131104 | tf_op jit(solution)/shard_map/ppermute | solution.py:408
  17.9 1.3 %collective-permute-start.2 = (bf16[128,512]{1,0:T(8,128)(2,1)S(1)}, bf16[128,512]{1,0:T(8,128)(2,1)S(1)}, u32[]{:S(2)}, u32[]{:S(2)}) collective-permute-start(bf16[128,512]{1,0:T(8,128)(2,1)S(1)} %broadcast_select_fusion.3.held_ref), channel_id=1, source_target_pairs={{0,4},{2,6},{8,12},{10,14},{1,5},{3,7},{9,13},{11,15},{16,20},{18,... | collective-permute-start | bytes 393224 | tf_op jit(solution)/shard_map/ppermute | solution.py:424
  19.3 0.1 collective-permute-done.4
  19.4 0.2 collective-permute-done.8.back_ref.refs_1_
  19.7 2.0 %collective-permute-start.9 = (bf16[608,128]{1,0:T(8,128)(2,1)S(1)}, bf16[608,128]{1,0:T(8,128)(2,1)S(1)}, u32[]{:S(2)}, u32[]{:S(2)}) collective-permute-start(bf16[608,128]{1,0:T(8,128)(2,1)S(1)} %load.1.held_ref), channel_id=1, source_target_pairs={{0,4},{2,6},{4,0},{6,2},{8,12},{10,14},{12,8},{14,10},{1,5},{3,7},... | collective-permute-start | bytes 466952 | tf_op jit(solution)/shard_map/ppermute | solution.py:405
  21.7 1.3 %stage.1 = (f32[128,128]{1,0:T(8,128)S(1)}, bf16[128,4096]{1,0:T(8,128)(2,1)S(1)}) custom-call(s32[1,128]{1,0:T(1,128)} %bitcast.2, bf16[128,4096]{1,0:T(8,128)(2,1)} %query_ref.1), custom_call_target="tpu_custom_call" | custom-call | flops 1000 | bytes 2100000 | tf_op jit(solution)/shard_map/stage/pallas_call | solution.py:108
  23.0 1.1 %context_weights.1.weight_ref = bf16[4096,256]{1,0:T(8,128)(2,1)S(1)} custom-call(s32[1]{0:T(128)} %bitcast.host_ref, f32[128,128]{1,0:T(8,128)S(1)} %get-tuple-element.9.bias_ref, bf16[128,4096]{1,0:T(8,128)(2,1)S(1)} %get-tuple-element.10.query_ref, bf16[128,512]{1,0:T(8,128)(2,1)S(1)} %get-tuple-element.11.key_ref.k0_ref, ...), custom_call_target="tpu_custom_call" | custom-call | flops 268435456 | bytes 4000000 | tf_op jit(solution)/shard_map/context_weights/pallas_call | solution.py:276
  24.0 1.0 %collective-permute-done.9.arrived_ref = bf16[608,128]{1,0:T(8,128)(2,1)S(1)} collective-permute-done((bf16[608,128]{1,0:T(8,128)(2,1)S(1)}, bf16[608,128]{1,0:T(8,128)(2,1)S(1)}, u32[]{:S(2)}, u32[]{:S(2)}) %collective-permute-start.9) | collective-permute-done | bytes 155680 | tf_op jit(solution)/shard_map/ppermute | solution.py:405
  25.0 1.5 %context_sums.1 = (bf16[128,4096]{1,0:T(8,128)(2,1)}, bf16[1,4096]{1,0:T(2,128)(2,1)}) custom-call(s32[1]{0:T(128)} %bitcast.host_ref, bf16[4096,256]{1,0:T(8,128)(2,1)S(1)} %context_weights.1.weight_ref, bf16[128,512]{1,0:T(8,128)(2,1)S(1)} %get-tuple-element.12.v0_ref.value_ref, bf16[608,128]{1,0:T(8,128)(2,1)S(1)} %load.1.held_ref, ...), custom_call_target="tpu_custom_call" | custom-call | flops 268435456 | bytes 4000000 | tf_op jit(solution)/shard_map/context_sums/pallas_call | solution.py:380
  (6 shorter events, 0.1 us)
Async XLA Ops:
  0.6 9.5 %collective-permute-start = (bf16[128,512]{1,0:T(8,128)(2,1)}, bf16[128,512]{1,0:T(8,128)(2,1)S(1)}, u32[]{:S(2)}, u32[]{:S(2)}) collective-permute-start(bf16[128,512]{1,0:T(8,128)(2,1)} %refs_1_.1), channel_id=1, source_target_pairs={{0,2},{2,0},{4,6},{6,4},{8,10},{10,8},{12,14},{14,12},{1,3},{3,1},... | collective-permute-start | bytes 393224 | tf_op jit(solution)/shard_map/ppermute | solution.py:405
  3.6 8.9 %collective-permute-start.3 = (bf16[128,512]{1,0:T(8,128)(2,1)}, bf16[128,512]{1,0:T(8,128)(2,1)S(1)}, u32[]{:S(2)}, u32[]{:S(2)}) collective-permute-start(bf16[128,512]{1,0:T(8,128)(2,1)} %refs_2_.1), channel_id=1, source_target_pairs={{0,2},{2,0},{4,6},{6,4},{8,10},{10,8},{12,14},{14,12},{1,3},{3,1},... | collective-permute-start | bytes 393224 | tf_op jit(solution)/shard_map/ppermute | solution.py:405
  5.4 7.9 %collective-permute-start.5 = (bf16[48,128]{1,0:T(8,128)(2,1)S(1)}, bf16[48,128]{1,0:T(8,128)(2,1)S(1)}, u32[]{:S(2)}, u32[]{:S(2)}) collective-permute-start(bf16[48,128]{1,0:T(8,128)(2,1)S(1)} %get-tuple-element.13.refs_0_), channel_id=1, source_target_pairs={{0,12},{2,14},{4,8},{6,10},{8,4},{10,6},{12,0},{14,2},{1,13},{3,15... | collective-permute-start | bytes 36872 | tf_op jit(solution)/shard_map/ppermute | solution.py:405
  9.5 3.9 %collective-permute-start.6 = (bf16[48,128]{1,0:T(8,128)(2,1)S(1)}, bf16[48,128]{1,0:T(8,128)(2,1)S(1)}, u32[]{:S(2)}, u32[]{:S(2)}) collective-permute-start(bf16[48,128]{1,0:T(8,128)(2,1)S(1)} %get-tuple-element.13.refs_0_), channel_id=1, source_target_pairs={{0,4},{2,6},{4,0},{6,2},{8,12},{10,14},{12,8},{14,10},{1,5},{3,7},... | collective-permute-start | bytes 36872 | tf_op jit(solution)/shard_map/ppermute | solution.py:405
  9.5 4.6 %collective-permute-start.7 = (bf16[48,128]{1,0:T(8,128)(2,1)S(1)}, bf16[48,128]{1,0:T(8,128)(2,1)S(1)}, u32[]{:S(2)}, u32[]{:S(2)}) collective-permute-start(bf16[48,128]{1,0:T(8,128)(2,1)S(1)} %get-tuple-element.13.refs_0_), channel_id=1, source_target_pairs={{0,8},{2,10},{4,12},{6,14},{8,0},{10,2},{12,4},{14,6},{1,9},{3,11}... | collective-permute-start | bytes 36872 | tf_op jit(solution)/shard_map/ppermute | solution.py:405
  10.2 7.7 %collective-permute-start.1 = (bf16[128,512]{1,0:T(8,128)(2,1)S(1)}, bf16[128,512]{1,0:T(8,128)(2,1)S(1)}, u32[]{:S(2)}, u32[]{:S(2)}) collective-permute-start(bf16[128,512]{1,0:T(8,128)(2,1)S(1)} %broadcast_select_fusion.1), channel_id=1, source_target_pairs={{0,8},{2,10},{4,6},{6,4},{8,0},{10,2},{12,14},{14,12},{1,9},{3,11}... | collective-permute-start | bytes 393224 | tf_op jit(solution)/shard_map/ppermute | solution.py:408
  12.5 6.9 %collective-permute-start.4 = (bf16[128,512]{1,0:T(8,128)(2,1)S(1)}, bf16[128,512]{1,0:T(8,128)(2,1)S(1)}, u32[]{:S(2)}, u32[]{:S(2)}) collective-permute-start(bf16[128,512]{1,0:T(8,128)(2,1)S(1)} %broadcast_select_fusion), channel_id=1, source_target_pairs={{0,8},{2,10},{4,6},{6,4},{8,0},{10,2},{12,14},{14,12},{1,9},{3,11}... | collective-permute-start | bytes 393224 | tf_op jit(solution)/shard_map/ppermute | solution.py:408
  14.7 5.0 %collective-permute-start.8 = (bf16[96,128]{1,0:T(8,128)(2,1)S(1)}, bf16[96,128]{1,0:T(8,128)(2,1)S(1)}, u32[]{:S(2)}, u32[]{:S(2)}) collective-permute-start(bf16[96,128]{1,0:T(8,128)(2,1)S(1)} %get-tuple-element.15), channel_id=1, source_target_pairs={{0,8},{2,10},{4,12},{6,14},{8,0},{10,2},{12,4},{14,6},{1,9},{3,11}... | collective-permute-start | bytes 73736 | tf_op jit(solution)/shard_map/ppermute | solution.py:405
  17.9 5.0 %collective-permute-start.2 = (bf16[128,512]{1,0:T(8,128)(2,1)S(1)}, bf16[128,512]{1,0:T(8,128)(2,1)S(1)}, u32[]{:S(2)}, u32[]{:S(2)}) collective-permute-start(bf16[128,512]{1,0:T(8,128)(2,1)S(1)} %broadcast_select_fusion.3.held_ref), channel_id=1, source_target_pairs={{0,4},{2,6},{8,12},{10,14},{1,5},{3,7},{9,13},{11,15},{16,20},{18,... | collective-permute-start | bytes 393224 | tf_op jit(solution)/shard_map/ppermute | solution.py:424
  19.7 5.3 %collective-permute-start.9 = (bf16[608,128]{1,0:T(8,128)(2,1)S(1)}, bf16[608,128]{1,0:T(8,128)(2,1)S(1)}, u32[]{:S(2)}, u32[]{:S(2)}) collective-permute-start(bf16[608,128]{1,0:T(8,128)(2,1)S(1)} %load.1.held_ref), channel_id=1, source_target_pairs={{0,4},{2,6},{4,0},{6,2},{8,12},{10,14},{12,8},{14,10},{1,5},{3,7},... | collective-permute-start | bytes 466952 | tf_op jit(solution)/shard_map/ppermute | solution.py:405
